TPU v7x, 512 devices: a whole 4x4x16 slice. The times are simulated.
512 devices in a mesh: node: 32 (over x, z_lo), local: 16 (over z_hi, y, core).
Axes of the slice: x: 4, y: 4, z: 16 (z_hi: 2, z_lo: 8; z = z_hi * 8 + z_lo), core: 2. Of those that a mesh axis runs over, the one named last changes fastest.
Arguments:
- acts: bfloat16 [114688, 4096], P(('node', 'local')), may hold values from -24 to 24
- grads_out: bfloat16 [114688, 1024], P(('node', 'local')), may hold values from -6 to 6
- quant: bfloat16 [4096, 1024], P('local'), may hold values from -127 to 127, as said below
- scales: float32 [4096, 8], P('local'), may hold values from 5e-05 to 0.0005
Outputs:
- grad_input: bfloat16 [114688, 4096], P(('node', 'local'))
- weight_grad: float32 [4096, 1024], P(('local', 'node'))
Inputs may be any that keep to these rules, and one draw needn't show every extreme that they name: quant holds whole numbers.
All inputs are finite; a program needn't handle non-finite values.
Results may differ from a plain program's by a relative error of at most 0.0049.
Values may be sent and summed in bfloat16 or wider, within the bound.
No kernel may reach another device: no remote copies, remote signals or barrier semaphores. Data moves between devices by JAX's collectives and lax.ppermute only.
A program may use at most 128 MiB of HBM per device.

v0:
```python
import math

import jax
import jax.numpy as jnp
from jax import lax
from jax.sharding import PartitionSpec as P

BLOCK = 128


def shards(acts, grads_out, quant, scales):
    tok_rows = acts.shape[0]
    width = acts.shape[1]
    columns = grads_out.shape[1]
    shard_rows = quant.shape[0]
    local_count = lax.axis_size("local")
    node_count = lax.axis_size("node")
    total_tokens = tok_rows * local_count * node_count
    blocked = (
        quant.astype(jnp.float32).reshape(shard_rows, columns // BLOCK, BLOCK) * scales[:, :, None]
    )
    weight_shard = blocked.reshape(shard_rows, columns).astype(jnp.bfloat16)
    grad_full = lax.dot_general(
        grads_out,
        lax.all_gather(weight_shard, "local", axis=0, tiled=True),
        (((1,), (1,)), ((), ())),
        preferred_element_type=jnp.float32,
    )
    grad_input = grad_full.astype(jnp.bfloat16)
    factor = 1.0 / math.sqrt(total_tokens)
    own_width = width // local_count
    partial_value = lax.dot_general(
        acts, grads_out, (((0,), (0,)), ((), ())), preferred_element_type=jnp.float32
    )
    partial_value = (partial_value * factor).astype(jnp.bfloat16)
    pieces = partial_value.reshape(local_count, own_width, columns)
    received = lax.all_to_all(pieces, "local", split_axis=0, concat_axis=0, tiled=True)
    node_part = jnp.sum(received, axis=0, dtype=jnp.float32).astype(jnp.bfloat16)
    slices = node_part.reshape(node_count, own_width // node_count, columns)
    gathered = lax.all_to_all(slices, "node", split_axis=0, concat_axis=0, tiled=True)
    weight_grad = jnp.sum(gathered, axis=0, dtype=jnp.float32)
    return (grad_input, weight_grad)


def solution(mesh):
    placed = (
        P(("node", "local"), None),
        P(("node", "local"), None),
        P("local", None),
        P("local", None),
    )
    return jax.shard_map(
        shards,
        mesh=mesh,
        in_specs=placed,
        out_specs=(P(("node", "local"), None), P(("local", "node"), None)),
        check_vma=False,
    )
```

profile of v0, /device:TPU:24, one launch (start us, length us, event | category | flops | bytes accessed | tf_op | source)
XLA Modules:
  0.0 608.0 jit_solution(10344820200438594054)
XLA Ops:
  7.2 0.0 copy-start
  7.2 1.5 copy-done
  8.7 6.6 %multiply_convert_fusion = bf16[4096,1024]{1,0:T(8,128)(2,1)} fusion(bf16[224,4096]{1,0:T(8,128)(2,1)S(1)} %copy-done, bf16[224,1024]{1,0:T(8,128)(2,1)} %param.5), kind=kOutput, calls=%fused_computation | convolution fusion | flops 1887436800 | bytes 10682368 | tf_op jit(solution)/shard_map/dot_general | solution.py:32
  15.3 0.0 copy-start.2
  15.3 0.0 copy-start.1
  15.3 18.1 %all-to-all-start = ((bf16[16,256,1024]{2,1,0:T(8,128)(2,1)}), bf16[16,256,1024]{2,1,0:T(8,128)(2,1)}, u32[]{:S(2)}, u32[]{:S(2)}) async-start(bf16[16,256,1024]{2,1,0:T(8,128)(2,1)} %bitcast.13), calls=%async_computation | async-start | bytes 16777216 | tf_op jit(solution)/shard_map/all_to_all | solution.py:37
  33.4 0.0 copy-start.3
  33.4 0.0 all-gather.2.cloned.1.call-start
  33.5 0.0 copy-done.2
  33.5 0.1 copy.7
  33.6 0.3 mul.17
  33.9 0.0 copy-done.1
  34.0 1.1 fusion.1
  35.0 0.0 all-gather.2.cloned.1.call-update
  35.0 182.0 %all-to-all-done = bf16[16,256,1024]{2,1,0:T(8,128)(2,1)} async-done(((bf16[16,256,1024]{2,1,0:T(8,128)(2,1)}), bf16[16,256,1024]{2,1,0:T(8,128)(2,1)}, u32[]{:S(2)}, u32[]{:S(2)}) %all-to-all-start) | async-done | bytes 8388640 | tf_op jit(solution)/shard_map/all_to_all | solution.py:37
  217.1 6.3 %reduce_sum.21 = bf16[256,1024]{1,0:T(8,128)(2,1)} reduce(bf16[16,256,1024]{2,1,0:T(8,128)(2,1)} %all-to-all-done, bf16[]{:T(256)} %constant.4.clone.1), dimensions={0}, to_apply=%region_0.0 | reduce | flops 3932160 | bytes 8912898 | tf_op jit(solution)/shard_map/reduce_sum | solution.py:38
  223.4 345.8 %all-to-all-start.1 = ((bf16[32,8,1024]{2,1,0:T(8,128)(2,1)}), bf16[32,8,1024]{2,1,0:T(8,128)(2,1)S(1)}, u32[]{:S(2)}, u32[]{:S(2)}) async-start(bf16[32,8,1024]{2,1,0:T(8,128)(2,1)} %bitcast.2), calls=%async_computation.1 | async-start | bytes 1048576 | tf_op jit(solution)/shard_map/all_to_all | solution.py:40
  569.2 0.0 all-gather.2.cloned.1.call-done
  569.3 0.0 copy-done.3
  569.3 7.2 %fusion = bf16[224,4096]{1,0:T(8,128)(2,1)} fusion(bf16[4096,1024]{1,0:T(8,128)(2,1)} %all-gather.2.cloned.1.call-done, bf16[224,1024]{1,0:T(8,128)(2,1)S(1)} %copy-done.3), kind=kOutput, calls=%fused_computation.2 | convolution fusion | flops 1879965696 | bytes 10682368 | tf_op jit(solution)/shard_map/dot_general | solution.py:23
  576.5 23.9 %all-to-all-done.1 = bf16[32,8,1024]{2,1,0:T(8,128)(2,1)S(1)} async-done(((bf16[32,8,1024]{2,1,0:T(8,128)(2,1)}), bf16[32,8,1024]{2,1,0:T(8,128)(2,1)S(1)}, u32[]{:S(2)}, u32[]{:S(2)}) %all-to-all-start.1) | async-done | bytes 524320 | tf_op jit(solution)/shard_map/all_to_all | solution.py:40
  600.5 0.7 convert_reduce_fusion
Async XLA Ops:
  7.2 1.5 copy-start
  15.3 18.2 %copy-start.2 = (f32[256,8]{0,1:T(8,128)S(1)}, f32[256,8]{0,1:T(8,128)}, u32[]{:S(2)}) copy-start(f32[256,8]{0,1:T(8,128)} %param.7) | copy-start | bytes 24580
  15.3 18.6 %copy-start.1 = (bf16[256,1024]{1,0:T(8,128)(2,1)S(1)}, bf16[256,1024]{1,0:T(8,128)(2,1)}, u32[]{:S(2)}) copy-start(bf16[256,1024]{1,0:T(8,128)(2,1)} %param.6) | copy-start | bytes 1572868
  15.3 201.8 %all-to-all-start = ((bf16[16,256,1024]{2,1,0:T(8,128)(2,1)}), bf16[16,256,1024]{2,1,0:T(8,128)(2,1)}, u32[]{:S(2)}, u32[]{:S(2)}) async-start(bf16[16,256,1024]{2,1,0:T(8,128)(2,1)} %bitcast.13), calls=%async_computation | async-start | bytes 16777216 | tf_op jit(solution)/shard_map/all_to_all | solution.py:37
  33.4 535.9 %copy-start.3 = (bf16[224,1024]{1,0:T(8,128)(2,1)S(1)}, bf16[224,1024]{1,0:T(8,128)(2,1)}, u32[]{:S(2)}) copy-start(bf16[224,1024]{1,0:T(8,128)(2,1)} %param.5) | copy-start | bytes 1376260
  33.4 535.8 %all-gather.2.cloned.1.call-start = ((), (), s32[]{:S(2)}) async-start(), calls=%async_computation.2 | async-start | bytes 8912896 | tf_op jit(solution)/shard_map/all_gather | solution.py:25
  223.4 377.0 %all-to-all-start.1 = ((bf16[32,8,1024]{2,1,0:T(8,128)(2,1)}), bf16[32,8,1024]{2,1,0:T(8,128)(2,1)S(1)}, u32[]{:S(2)}, u32[]{:S(2)}) async-start(bf16[32,8,1024]{2,1,0:T(8,128)(2,1)} %bitcast.2), calls=%async_computation.1 | async-start | bytes 1048576 | tf_op jit(solution)/shard_map/all_to_all | solution.py:40
Sparse Core Ops, SparseCore 0:
  38.1 480.6 all-gather.1
where the time goes:
time: 608 us
  starting transfers between devices  364 us (60%)
  waiting for transfers between devices  206 us (34%)
  between operations  14.1 us (2%)
  matrix products  13.9 us (2%)
  other arithmetic  8.11 us (1%)
    all_to_all x1, starting transfers between devices, shards(): lax.all_to_all(slices, 'node', split_axis=0, concat_axis=0, tiled=True)  346 us
    all_to_all x1, waiting for transfers between devices, shards(): lax.all_to_all(pieces, 'local', split_axis=0, concat_axis=0, tiled=True)  182 us
    all_to_all x1, waiting for transfers between devices, shards(): lax.all_to_all(slices, 'node', split_axis=0, concat_axis=0, tiled=True)  23.9 us
    all_to_all x1, starting transfers between devices, shards(): lax.all_to_all(pieces, 'local', split_axis=0, concat_axis=0, tiled=True)  18.1 us
  transfers between devices with their start and end apart: 3, of which 2 were waited for; matrix products, arithmetic and copies ran while one was open for 2% of the time, Pallas kernels for 0%

commit v1 on v0

v1 whole, which is shorter than its diff:
```python
import math

import jax
import jax.numpy as jnp
from jax import lax
from jax.sharding import Mesh
from jax.sharding import PartitionSpec as P

BLOCK = 128
NX, NZL, NZH, NY, NC = 4, 8, 2, 4, 2
NZ = NZL * NZH
AXES = ("x", "zl", "zh", "y", "c")


def shift(value, axis, step):
    size = lax.axis_size(axis)
    return lax.ppermute(value, axis, [(i, (i + step) % size) for i in range(size)])


def chip_shift(value, move):
    def index(x, z, y, c):
        return (((x * NZL + z % NZL) * NZH + z // NZL) * NY + y) * NC + c

    pairs = [
        (index(x, z, y, c), index(x, move(z), y, c))
        for x in range(NX)
        for z in range(NZ)
        for y in range(NY)
        for c in range(NC)
    ]
    return lax.ppermute(value, AXES, pairs)


def pick(array, index, axis):
    return lax.dynamic_index_in_dim(array, index, axis, keepdims=False)


def total_of(parts):
    total = parts[0].astype(jnp.float32)
    for part in parts[1:]:
        total = total + part.astype(jnp.float32)
    return total


def shards(acts, grads_out, quant, scales):
    tokens, width = acts.shape
    columns = grads_out.shape[1]
    shard_rows = quant.shape[0]
    total_tokens = tokens * lax.axis_size(AXES)
    x, zl, zh, y, c = (lax.axis_index(name) for name in AXES)
    z = zh * NZL + zl
    bf16 = jnp.bfloat16

    blocked = (
        quant.astype(jnp.float32).reshape(shard_rows, columns // BLOCK, BLOCK) * scales[:, :, None]
    )
    weight = blocked.reshape(shard_rows, columns).astype(bf16)

    quarter = lax.dynamic_slice_in_dim(weight, x * (shard_rows // NX), shard_rows // NX, 0)
    other = chip_shift(quarter, lambda i: (i + NZL) % NZ)
    own_half = lax.all_gather(weight, ("y", "c"), axis=0, tiled=True)
    other_half = lax.all_gather(other, ("x", "y", "c"), axis=0, tiled=True)
    other_half = (
        other_half.reshape(NX, NY * NC, shard_rows // NX, columns)
        .transpose(1, 0, 2, 3)
        .reshape(NY * NC * shard_rows, columns)
    )

    groups = acts.reshape(tokens, NZH * NY, NC, width // (NZH * NY * NC))
    mine = pick(groups, c, 2).reshape(tokens, width // NC)
    theirs = pick(groups, 1 - c, 2).reshape(tokens, width // NC)
    acts_in = shift(theirs, "c", 1)
    grads_in = shift(grads_out, "c", 1)
    acts_two = jnp.concatenate([mine, acts_in], axis=0)
    grads_two = jnp.concatenate([grads_out, grads_in], axis=0)
    factor = 1.0 / math.sqrt(total_tokens)
    part = lax.dot_general(
        acts_two, grads_two, (((0,), (0,)), ((), ())), preferred_element_type=jnp.float32
    )
    part = (part * factor).astype(bf16)
    half = columns // 2
    part = part.reshape(NZH, NY, NX, NZL * 8, columns)

    left, right = part[..., :half], part[..., half:]
    left_in, right_in = [pick(left, y, 1)], [pick(right, x, 2)]
    for k in (1, 3, 2):
        left_in.append(shift(pick(left, (y + k) % NY, 1), "y", k))
        right_in.append(shift(pick(right, (x + k) % NX, 2), "x", k))
    left = total_of(left_in).astype(bf16)
    right = total_of(right_in).astype(bf16)
    left_in, right_in = [pick(left, x, 1)], [pick(right, y, 1)]
    for k in (1, 3, 2):
        left_in.append(shift(pick(left, (x + k) % NX, 1), "x", k))
        right_in.append(shift(pick(right, (y + k) % NY, 1), "y", k))
    left, right = total_of(left_in), total_of(right_in)
    rows = jnp.concatenate([left, right], axis=-1).astype(bf16)
    rows = rows.reshape(4, 4, 8, columns)
    run, place = z // 4, z % 4
    parts = [pick(rows, place, 1)]
    for k in (1, 3, 2):
        parts.append(
            chip_shift(
                pick(rows, (place + k) % 4, 1),
                lambda i, k=k: (i // 4) * 4 + (i + k) % 4,
            )
        )
    rows = total_of(parts)
    parts = [pick(rows, run, 0)]
    for k in (1, 3, 2):
        parts.append(chip_shift(pick(rows, (run + k) % 4, 0), lambda i, k=k: (i + 4 * k) % NZ))
    weight_grad = total_of(parts)

    def input_half(rows_half):
        return lax.dot_general(
            grads_out, rows_half, (((1,), (1,)), ((), ())), preferred_element_type=jnp.float32
        ).astype(bf16)

    own, far = input_half(own_half), input_half(other_half)
    low, high = jnp.where(zh == 0, own, far), jnp.where(zh == 0, far, own)
    grad_input = jnp.concatenate([low, high], axis=1)
    return (grad_input, weight_grad)


def solution(mesh):
    fine = Mesh(mesh.devices.reshape(NX, NZL, NZH, NY, NC), AXES)
    tokens = P(AXES, None)
    rows = P(("zh", "y", "c"), None)
    return jax.shard_map(
        shards,
        mesh=fine,
        in_specs=(tokens, tokens, rows, rows),
        out_specs=(tokens, P(("zh", "y", "c", "x", "zl"), None)),
        check_vma=False,
    )
```

time: 608 us -> 194 us (0.32)
  starting transfers between devices: 364 us -> 96.2 us
  waiting for transfers between devices: 206 us -> 36.9 us
  local copies, waits for them, and re-layouts: 1.97 us -> 27.4 us
    all_to_all x2 -> x0, starting transfers between devices: 364 us -> none  [the longest x1 346 us: shards(): lax.all_to_all(slices, 'node', split_axis=0, concat_axis=0, tiled=True)]
    all_to_all x2 -> x0, waiting for transfers between devices: 206 us -> none  [the longest x1 182 us: shards(): lax.all_to_all(pieces, 'local', split_axis=0, concat_axis=0, tiled=True)]
    ppermute x0 -> x21, starting transfers between devices: none -> 96.1 us  [the longest x7 53.6 us: chip_shift(): return lax.ppermute(value, AXES, pairs)]
    ppermute x0 -> x21, waiting for transfers between devices: none -> 36.8 us  [the longest x14 24.9 us: shift(): lax.ppermute(value, axis, [(i, (i + step) % size) for i in range(size)])]
    dynamic_slice x0 -> x2, local copies, waits for them, and re-layouts: none -> 12.6 us  [the longest x1 11.7 us: pick(): return lax.dynamic_index_in_dim(array, index, axis, keepdims=False)]
    reduce_sum x2 -> x0, other arithmetic: 7.04 us -> none  [the longest x1 6.35 us: shards(): jnp.sum(received, axis=0, dtype=jnp.float32).astype(jnp.bfloat16)]
    dot_general x2 -> x3, matrix products: 13.9 us -> 8.71 us  [the longest x2 5.03 us: input_half(): lax.dot_general(grads_out, rows_half, (((1,), (1,)), ((), ())), preferred...]
  transfers between devices with their start and end apart: 3 -> 23, of which waited for: 2 -> 9; matrix products, arithmetic and copies ran while one was open for 2% -> 17% of each run, Pallas kernels for 0% -> 0%
where the time goes in v1:
time: 194 us; the launch traced here: 192 us
  starting transfers between devices  96.2 us (50%)
  waiting for transfers between devices  36.9 us (19%)
  local copies, waits for them, and re-layouts  27.4 us (14%)
  between operations  14.7 us (8%)
  matrix products  8.71 us (4%)
  other arithmetic  7.78 us (4%)
    ppermute x7, starting transfers between devices, chip_shift(): return lax.ppermute(value, AXES, pairs)  53.6 us
    ppermute x14, starting transfers between devices, shift(): lax.ppermute(value, axis, [(i, (i + step) % size) for i in range(size)])  42.5 us
    ppermute x14, waiting for transfers between devices, shift(): lax.ppermute(value, axis, [(i, (i + step) % size) for i in range(size)])  24.9 us
    ppermute x7, waiting for transfers between devices, chip_shift(): return lax.ppermute(value, AXES, pairs)  12 us
    dynamic_slice x1, local copies, waits for them, and re-layouts, pick(): return lax.dynamic_index_in_dim(array, index, axis, keepdims=False)  11.7 us
    dot_general x2, matrix products, input_half(): lax.dot_general(grads_out, rows_half, (((1,), (1,)), ((), ())), preferred...  5.03 us
    reshape x1, local copies, waits for them, and re-layouts, shards(): groups = acts.reshape(tokens, NZH * NY, NC, width // (NZH * NY * NC))  4.81 us
    unnamed x11, local copies, waits for them, and re-layouts  4.48 us
  transfers between devices with their start and end apart: 23, of which 9 were waited for; matrix products, arithmetic and copies ran while one was open for 17% of the time, Pallas kernels for 0%

profile of v1, /device:TPU:24, one launch (start us, length us, event | category | flops | bytes accessed | tf_op | source)
XLA Modules:
  0.0 191.7 jit_solution(12113918828767558020)
XLA Ops:
  11.5 15.7 %collective-permute-start = (bf16[64,1024]{1,0:T(8,128)(2,1)S(1)}, bf16[64,1024]{1,0:T(8,128)(2,1)S(1)}, u32[]{:S(2)}, u32[]{:S(2)}) collective-permute-start(bf16[64,1024]{1,0:T(8,128)(2,1)S(1)} %constant_dynamic-slice_fusion), channel_id=1, source_target_pairs={{0,8},{1,9},{2,10},{3,11},{4,12},{5,13},{6,14},{7,15},{16,24},{17,... | collective-permute-start | bytes 393224 | tf_op jit(solution)/shard_map/ppermute | solution.py:31
  27.2 3.8 %collective-permute-done = bf16[64,1024]{1,0:T(8,128)(2,1)S(1)} collective-permute-done((bf16[64,1024]{1,0:T(8,128)(2,1)S(1)}, bf16[64,1024]{1,0:T(8,128)(2,1)S(1)}, u32[]{:S(2)}, u32[]{:S(2)}) %collective-permute-start) | collective-permute-done | bytes 131104 | tf_op jit(solution)/shard_map/ppermute | solution.py:31
  31.7 4.8 %reshape.45 = bf16[224,8,2,256]{3,2,1,0:T(2,128)(2,1)S(1)} reshape(bf16[224,4096]{1,0:T(8,128)(2,1)} %param.4) | data formatting | bytes 3670016 | tf_op jit(solution)/shard_map/reshape | solution.py:69
  36.5 11.7 %dynamic-slice_reduce_fusion.1 = (bf16[224,8,256]{2,1,0:T(8,128)(2,1)S(1)}, bf16[224,8,256]{2,1,0:T(8,128)(2,1)}) fusion(bf16[224,8,2,256]{3,2,1,0:T(2,128)(2,1)S(1)} %reshape.45, s32[]{:T(128)S(6)} %select_n.166, s32[]{:T(128)S(6)} %select_n.167), kind=kLoop, calls=%fused_computation.8 | loop fusion | bytes 3670024 | tf_op jit(solution)/shard_map/jit(dynamic_index_in_dim)/dynamic_slice | solution.py:35
  55.5 3.7 %multiply_convert_fusion = bf16[2048,1024]{1,0:T(8,128)(2,1)S(1)} fusion(bf16[224,2048]{1,0:T(8,128)(2,1)} %collective-permute-done.1, bf16[224,2048]{1,0:T(8,128)(2,1)S(1)} %bitcast.102, bf16[224,1024]{1,0:T(8,128)(2,1)} %collective-permute-done.2, bf16[224,1024]{1,0:T(8,128)(2,1)S(1)} %copy-done.2), kind=kOutput, calls=%fused_computation | convolution fusion | flops 1888747520 | bytes 6946816 | tf_op jit(solution)/shard_map/dot_general | solution.py:77
  61.9 4.7 %collective-permute-start.10 = (bf16[2,4,64,512]{3,2,1,0:T(8,128)(2,1)}, bf16[2,4,64,512]{3,2,1,0:T(8,128)(2,1)}, u32[]{:S(2)}, u32[]{:S(2)}) collective-permute-start(bf16[2,4,64,512]{3,2,1,0:T(8,128)(2,1)} %get-tuple-element.8), channel_id=1, source_target_pairs={{0,384},{128,0},{256,128},{384,256},{1,385},{129,1},{257,129},{385... | collective-permute-start | bytes 1572872 | tf_op jit(solution)/shard_map/ppermute | solution.py:17
  66.6 2.7 %collective-permute-start.11 = (bf16[2,4,64,512]{3,2,1,0:T(8,128)(2,1)S(1)}, bf16[2,4,64,512]{3,2,1,0:T(8,128)(2,1)}, u32[]{:S(2)}, u32[]{:S(2)}) collective-permute-start(bf16[2,4,64,512]{3,2,1,0:T(8,128)(2,1)S(1)} %get-tuple-element.7), channel_id=1, source_target_pairs={{0,256},{128,384},{256,0},{384,128},{1,257},{129,385},{257,1},{385... | collective-permute-start | bytes 1572872 | tf_op jit(solution)/shard_map/ppermute | solution.py:17
  69.3 2.8 %collective-permute-start.9 = (bf16[2,4,64,512]{3,2,1,0:T(8,128)(2,1)S(1)}, bf16[2,4,64,512]{3,2,1,0:T(8,128)(2,1)}, u32[]{:S(2)}, u32[]{:S(2)}) collective-permute-start(bf16[2,4,64,512]{3,2,1,0:T(8,128)(2,1)S(1)} %get-tuple-element.6), channel_id=1, source_target_pairs={{0,128},{128,256},{256,384},{384,0},{1,129},{129,257},{257,385},{3... | collective-permute-start | bytes 1572872 | tf_op jit(solution)/shard_map/ppermute | solution.py:17
  75.5 3.7 %collective-permute-start.4 = (bf16[2,4,64,512]{3,2,1,0:T(8,128)(2,1)}, bf16[2,4,64,512]{3,2,1,0:T(8,128)(2,1)}, u32[]{:S(2)}, u32[]{:S(2)}) collective-permute-start(bf16[2,4,64,512]{3,2,1,0:T(8,128)(2,1)} %get-tuple-element.11), channel_id=1, source_target_pairs={{0,6},{2,0},{4,2},{6,4},{1,7},{3,1},{5,3},{7,5},{8,14},{10,8},{12,... | collective-permute-start | bytes 1572872 | tf_op jit(solution)/shard_map/ppermute | solution.py:17
  79.2 12.3 %collective-permute-done.10 = bf16[2,4,64,512]{3,2,1,0:T(8,128)(2,1)} collective-permute-done((bf16[2,4,64,512]{3,2,1,0:T(8,128)(2,1)}, bf16[2,4,64,512]{3,2,1,0:T(8,128)(2,1)}, u32[]{:S(2)}, u32[]{:S(2)}) %collective-permute-start.10) | collective-permute-done | bytes 524320 | tf_op jit(solution)/shard_map/ppermute | solution.py:17
  91.5 3.2 %collective-permute-start.5 = (bf16[2,4,64,512]{3,2,1,0:T(8,128)(2,1)}, bf16[2,4,64,512]{3,2,1,0:T(8,128)(2,1)}, u32[]{:S(2)}, u32[]{:S(2)}) collective-permute-start(bf16[2,4,64,512]{3,2,1,0:T(8,128)(2,1)} %get-tuple-element.10), channel_id=1, source_target_pairs={{0,4},{2,6},{4,0},{6,2},{1,5},{3,7},{5,1},{7,3},{8,12},{10,14},{12... | collective-permute-start | bytes 1572872 | tf_op jit(solution)/shard_map/ppermute | solution.py:17
  101.4 3.7 %collective-permute-start.13 = (bf16[2,64,512]{2,1,0:T(8,128)(2,1)S(1)}, bf16[2,64,512]{2,1,0:T(8,128)(2,1)S(1)}, u32[]{:S(2)}, u32[]{:S(2)}) collective-permute-start(bf16[2,64,512]{2,1,0:T(8,128)(2,1)S(1)} %get-tuple-element.16), channel_id=1, source_target_pairs={{0,6},{2,0},{4,2},{6,4},{1,7},{3,1},{5,3},{7,5},{8,14},{10,8},{12,... | collective-permute-start | bytes 393224 | tf_op jit(solution)/shard_map/ppermute | solution.py:17
  105.1 3.1 %collective-permute-start.14 = (bf16[2,64,512]{2,1,0:T(8,128)(2,1)S(1)}, bf16[2,64,512]{2,1,0:T(8,128)(2,1)S(1)}, u32[]{:S(2)}, u32[]{:S(2)}) collective-permute-start(bf16[2,64,512]{2,1,0:T(8,128)(2,1)S(1)} %get-tuple-element.15), channel_id=1, source_target_pairs={{0,4},{2,6},{4,0},{6,2},{1,5},{3,7},{5,1},{7,3},{8,12},{10,14},{12... | collective-permute-start | bytes 393224 | tf_op jit(solution)/shard_map/ppermute | solution.py:17
  112.0 5.1 %collective-permute-start.7 = (bf16[2,64,512]{2,1,0:T(8,128)(2,1)S(1)}, bf16[2,64,512]{2,1,0:T(8,128)(2,1)S(1)}, u32[]{:S(2)}, u32[]{:S(2)}) collective-permute-start(bf16[2,64,512]{2,1,0:T(8,128)(2,1)S(1)} %get-tuple-element.19), channel_id=1, source_target_pairs={{0,384},{128,0},{256,128},{384,256},{1,385},{129,1},{257,129},{385... | collective-permute-start | bytes 393224 | tf_op jit(solution)/shard_map/ppermute | solution.py:17
  117.1 2.6 %collective-permute-start.8 = (bf16[2,64,512]{2,1,0:T(8,128)(2,1)S(1)}, bf16[2,64,512]{2,1,0:T(8,128)(2,1)S(1)}, u32[]{:S(2)}, u32[]{:S(2)}) collective-permute-start(bf16[2,64,512]{2,1,0:T(8,128)(2,1)S(1)} %get-tuple-element.18), channel_id=1, source_target_pairs={{0,256},{128,384},{256,0},{384,128},{1,257},{129,385},{257,1},{385... | collective-permute-start | bytes 393224 | tf_op jit(solution)/shard_map/ppermute | solution.py:17
  119.9 3.8 %collective-permute-done.7 = bf16[2,64,512]{2,1,0:T(8,128)(2,1)S(1)} collective-permute-done((bf16[2,64,512]{2,1,0:T(8,128)(2,1)S(1)}, bf16[2,64,512]{2,1,0:T(8,128)(2,1)S(1)}, u32[]{:S(2)}, u32[]{:S(2)}) %collective-permute-start.7) | collective-permute-done | bytes 131104 | tf_op jit(solution)/shard_map/ppermute | solution.py:17
  123.7 5.1 %collective-permute-done.8 = bf16[2,64,512]{2,1,0:T(8,128)(2,1)S(1)} collective-permute-done((bf16[2,64,512]{2,1,0:T(8,128)(2,1)S(1)}, bf16[2,64,512]{2,1,0:T(8,128)(2,1)S(1)}, u32[]{:S(2)}, u32[]{:S(2)}) %collective-permute-start.8) | collective-permute-done | bytes 131104 | tf_op jit(solution)/shard_map/ppermute | solution.py:17
  128.9 10.6 %collective-permute-start.15 = (bf16[4,8,1024]{2,1,0:T(8,128)(2,1)S(1)}, bf16[4,8,1024]{2,1,0:T(8,128)(2,1)S(1)}, u32[]{:S(2)}, u32[]{:S(2)}) collective-permute-start(bf16[4,8,1024]{2,1,0:T(8,128)(2,1)S(1)} %get-tuple-element.20), channel_id=1, source_target_pairs={{0,16},{1,17},{2,18},{3,19},{4,20},{5,21},{6,22},{7,23},{16,32},{1... | collective-permute-start | bytes 196616 | tf_op jit(solution)/shard_map/ppermute | solution.py:31
  141.5 3.4 %collective-permute-start.17 = (bf16[4,8,1024]{2,1,0:T(8,128)(2,1)S(1)}, bf16[4,8,1024]{2,1,0:T(8,128)(2,1)S(1)}, u32[]{:S(2)}, u32[]{:S(2)}) collective-permute-start(bf16[4,8,1024]{2,1,0:T(8,128)(2,1)S(1)} %get-tuple-element.22), channel_id=1, source_target_pairs={{0,32},{1,33},{2,34},{3,35},{4,36},{5,37},{6,38},{7,39},{16,48},{1... | collective-permute-start | bytes 196616 | tf_op jit(solution)/shard_map/ppermute | solution.py:31
  148.6 7.8 %collective-permute-start.18 = (f32[8,1024]{1,0:T(8,128)S(1)}, f32[8,1024]{1,0:T(8,128)S(1)}, u32[]{:S(2)}, u32[]{:S(2)}) collective-permute-start(f32[8,1024]{1,0:T(8,128)S(1)} %get-tuple-element.23), channel_id=1, source_target_pairs={{0,64},{1,65},{2,66},{3,67},{4,68},{5,69},{6,70},{7,71},{16,80},{1... | collective-permute-start | bytes 98312 | tf_op jit(solution)/shard_map/ppermute | solution.py:31
  156.4 4.0 %collective-permute-start.19 = (f32[8,1024]{1,0:T(8,128)S(1)}, f32[8,1024]{1,0:T(8,128)S(1)}, u32[]{:S(2)}, u32[]{:S(2)}) collective-permute-start(f32[8,1024]{1,0:T(8,128)S(1)} %get-tuple-element.25), channel_id=1, source_target_pairs={{0,72},{1,73},{2,74},{3,75},{4,76},{5,77},{6,78},{7,79},{16,88},{1... | collective-permute-start | bytes 98312 | tf_op jit(solution)/shard_map/ppermute | solution.py:31
  160.4 10.2 %collective-permute-start.20 = (f32[8,1024]{1,0:T(8,128)S(1)}, f32[8,1024]{1,0:T(8,128)S(1)}, u32[]{:S(2)}, u32[]{:S(2)}) collective-permute-start(f32[8,1024]{1,0:T(8,128)S(1)} %get-tuple-element.24), channel_id=1, source_target_pairs={{0,8},{1,9},{2,10},{3,11},{4,12},{5,13},{6,14},{7,15},{16,24},{17,... | collective-permute-start | bytes 98312 | tf_op jit(solution)/shard_map/ppermute | solution.py:31
  170.6 4.6 %collective-permute-done.20 = f32[8,1024]{1,0:T(8,128)S(1)} collective-permute-done((f32[8,1024]{1,0:T(8,128)S(1)}, f32[8,1024]{1,0:T(8,128)S(1)}, u32[]{:S(2)}, u32[]{:S(2)}) %collective-permute-start.20) | collective-permute-done | bytes 32800 | tf_op jit(solution)/shard_map/ppermute | solution.py:31
  175.8 3.6 %convolution_convert_fusion.1 = bf16[2048,224]{0,1:T(8,128)(2,1)S(1)} fusion(bf16[2048,1024]{1,0:T(8,128)(2,1)} %all-gather.3.cloned.1.call-done, bf16[224,1024]{1,0:T(8,128)(2,1)S(1)} %copy-done.3), kind=kOutput, calls=%fused_computation.2 | convolution fusion | flops 939982848 | bytes 5570560 | tf_op jit(solution)/shard_map/dot_general | solution.py:114
  (58 shorter events, 40.4 us)
Async XLA Ops:
  7.2 168.7 %all-gather.3.cloned.1.call-start = ((), (), s32[]{:S(2)}) async-start(), calls=%async_computation | async-start | bytes 4718592 | tf_op jit(solution)/shard_map/all_gather | solution.py:61
  10.5 168.9 %all-gather.5.cloned.1.call-start = ((), (), s32[]{:S(2)}) async-start(), calls=%async_computation.1 | async-start | bytes 4325376 | tf_op jit(solution)/shard_map/all_gather | solution.py:62
  11.5 19.5 %collective-permute-start = (bf16[64,1024]{1,0:T(8,128)(2,1)S(1)}, bf16[64,1024]{1,0:T(8,128)(2,1)S(1)}, u32[]{:S(2)}, u32[]{:S(2)}) collective-permute-start(bf16[64,1024]{1,0:T(8,128)(2,1)S(1)} %constant_dynamic-slice_fusion), channel_id=1, source_target_pairs={{0,8},{1,9},{2,10},{3,11},{4,12},{5,13},{6,14},{7,15},{16,24},{17,... | collective-permute-start | bytes 393224 | tf_op jit(solution)/shard_map/ppermute | solution.py:31
  49.6 5.9 %collective-permute-start.1 = (bf16[224,2048]{1,0:T(8,128)(2,1)S(1)}, bf16[224,2048]{1,0:T(8,128)(2,1)}, u32[]{:S(2)}, u32[]{:S(2)}) collective-permute-start(bf16[224,2048]{1,0:T(8,128)(2,1)S(1)} %bitcast.101), channel_id=1, source_target_pairs={{0,1},{1,0},{2,3},{3,2},{4,5},{5,4},{6,7},{7,6},{8,9},{9,8},{10,11... | collective-permute-start | bytes 2752520 | tf_op jit(solution)/shard_map/ppermute | solution.py:17
  51.6 4.0 %collective-permute-start.2 = (bf16[224,1024]{1,0:T(8,128)(2,1)S(1)}, bf16[224,1024]{1,0:T(8,128)(2,1)}, u32[]{:S(2)}, u32[]{:S(2)}) collective-permute-start(bf16[224,1024]{1,0:T(8,128)(2,1)S(1)} %copy-done.2), channel_id=1, source_target_pairs={{0,1},{1,0},{2,3},{3,2},{4,5},{5,4},{6,7},{7,6},{8,9},{9,8},{10,11... | collective-permute-start | bytes 1376264 | tf_op jit(solution)/shard_map/ppermute | solution.py:17
  61.9 29.6 %collective-permute-start.10 = (bf16[2,4,64,512]{3,2,1,0:T(8,128)(2,1)}, bf16[2,4,64,512]{3,2,1,0:T(8,128)(2,1)}, u32[]{:S(2)}, u32[]{:S(2)}) collective-permute-start(bf16[2,4,64,512]{3,2,1,0:T(8,128)(2,1)} %get-tuple-element.8), channel_id=1, source_target_pairs={{0,384},{128,0},{256,128},{384,256},{1,385},{129,1},{257,129},{385... | collective-permute-start | bytes 1572872 | tf_op jit(solution)/shard_map/ppermute | solution.py:17
  66.6 28.2 %collective-permute-start.11 = (bf16[2,4,64,512]{3,2,1,0:T(8,128)(2,1)S(1)}, bf16[2,4,64,512]{3,2,1,0:T(8,128)(2,1)}, u32[]{:S(2)}, u32[]{:S(2)}) collective-permute-start(bf16[2,4,64,512]{3,2,1,0:T(8,128)(2,1)S(1)} %get-tuple-element.7), channel_id=1, source_target_pairs={{0,256},{128,384},{256,0},{384,128},{1,257},{129,385},{257,1},{385... | collective-permute-start | bytes 1572872 | tf_op jit(solution)/shard_map/ppermute | solution.py:17
  69.3 28.0 %collective-permute-start.9 = (bf16[2,4,64,512]{3,2,1,0:T(8,128)(2,1)S(1)}, bf16[2,4,64,512]{3,2,1,0:T(8,128)(2,1)}, u32[]{:S(2)}, u32[]{:S(2)}) collective-permute-start(bf16[2,4,64,512]{3,2,1,0:T(8,128)(2,1)S(1)} %get-tuple-element.6), channel_id=1, source_target_pairs={{0,128},{128,256},{256,384},{384,0},{1,129},{129,257},{257,385},{3... | collective-permute-start | bytes 1572872 | tf_op jit(solution)/shard_map/ppermute | solution.py:17
  73.3 31.7 %collective-permute-start.3 = (bf16[2,4,64,512]{3,2,1,0:T(8,128)(2,1)}, bf16[2,4,64,512]{3,2,1,0:T(8,128)(2,1)}, u32[]{:S(2)}, u32[]{:S(2)}) collective-permute-start(bf16[2,4,64,512]{3,2,1,0:T(8,128)(2,1)} %get-tuple-element.9), channel_id=1, source_target_pairs={{0,2},{2,4},{4,6},{6,0},{1,3},{3,5},{5,7},{7,1},{8,10},{10,12},{12... | collective-permute-start | bytes 1572872 | tf_op jit(solution)/shard_map/ppermute | solution.py:17
  75.5 32.7 %collective-permute-start.4 = (bf16[2,4,64,512]{3,2,1,0:T(8,128)(2,1)}, bf16[2,4,64,512]{3,2,1,0:T(8,128)(2,1)}, u32[]{:S(2)}, u32[]{:S(2)}) collective-permute-start(bf16[2,4,64,512]{3,2,1,0:T(8,128)(2,1)} %get-tuple-element.11), channel_id=1, source_target_pairs={{0,6},{2,0},{4,2},{6,4},{1,7},{3,1},{5,3},{7,5},{8,14},{10,8},{12,... | collective-permute-start | bytes 1572872 | tf_op jit(solution)/shard_map/ppermute | solution.py:17
  91.5 16.7 %collective-permute-start.5 = (bf16[2,4,64,512]{3,2,1,0:T(8,128)(2,1)}, bf16[2,4,64,512]{3,2,1,0:T(8,128)(2,1)}, u32[]{:S(2)}, u32[]{:S(2)}) collective-permute-start(bf16[2,4,64,512]{3,2,1,0:T(8,128)(2,1)} %get-tuple-element.10), channel_id=1, source_target_pairs={{0,4},{2,6},{4,0},{6,2},{1,5},{3,7},{5,1},{7,3},{8,12},{10,14},{12... | collective-permute-start | bytes 1572872 | tf_op jit(solution)/shard_map/ppermute | solution.py:17
  99.2 18.0 %collective-permute-start.12 = (bf16[2,64,512]{2,1,0:T(8,128)(2,1)S(1)}, bf16[2,64,512]{2,1,0:T(8,128)(2,1)S(1)}, u32[]{:S(2)}, u32[]{:S(2)}) collective-permute-start(bf16[2,64,512]{2,1,0:T(8,128)(2,1)S(1)} %get-tuple-element.14), channel_id=1, source_target_pairs={{0,2},{2,4},{4,6},{6,0},{1,3},{3,5},{5,7},{7,1},{8,10},{10,12},{12... | collective-permute-start | bytes 393224 | tf_op jit(solution)/shard_map/ppermute | solution.py:17
  101.4 18.4 %collective-permute-start.13 = (bf16[2,64,512]{2,1,0:T(8,128)(2,1)S(1)}, bf16[2,64,512]{2,1,0:T(8,128)(2,1)S(1)}, u32[]{:S(2)}, u32[]{:S(2)}) collective-permute-start(bf16[2,64,512]{2,1,0:T(8,128)(2,1)S(1)} %get-tuple-element.16), channel_id=1, source_target_pairs={{0,6},{2,0},{4,2},{6,4},{1,7},{3,1},{5,3},{7,5},{8,14},{10,8},{12,... | collective-permute-start | bytes 393224 | tf_op jit(solution)/shard_map/ppermute | solution.py:17
  105.1 14.7 %collective-permute-start.14 = (bf16[2,64,512]{2,1,0:T(8,128)(2,1)S(1)}, bf16[2,64,512]{2,1,0:T(8,128)(2,1)S(1)}, u32[]{:S(2)}, u32[]{:S(2)}) collective-permute-start(bf16[2,64,512]{2,1,0:T(8,128)(2,1)S(1)} %get-tuple-element.15), channel_id=1, source_target_pairs={{0,4},{2,6},{4,0},{6,2},{1,5},{3,7},{5,1},{7,3},{8,12},{10,14},{12... | collective-permute-start | bytes 393224 | tf_op jit(solution)/shard_map/ppermute | solution.py:17
  109.9 66.0 %copy-start.3 = (bf16[224,1024]{1,0:T(8,128)(2,1)S(1)}, bf16[224,1024]{1,0:T(8,128)(2,1)}, u32[]{:S(2)}) copy-start(bf16[224,1024]{1,0:T(8,128)(2,1)} %param.5) | copy-start | bytes 1376260
  109.9 10.0 %collective-permute-start.6 = (bf16[2,64,512]{2,1,0:T(8,128)(2,1)S(1)}, bf16[2,64,512]{2,1,0:T(8,128)(2,1)S(1)}, u32[]{:S(2)}, u32[]{:S(2)}) collective-permute-start(bf16[2,64,512]{2,1,0:T(8,128)(2,1)S(1)} %get-tuple-element.17), channel_id=1, source_target_pairs={{0,128},{128,256},{256,384},{384,0},{1,129},{129,257},{257,385},{3... | collective-permute-start | bytes 393224 | tf_op jit(solution)/shard_map/ppermute | solution.py:17
  112.0 11.7 %collective-permute-start.7 = (bf16[2,64,512]{2,1,0:T(8,128)(2,1)S(1)}, bf16[2,64,512]{2,1,0:T(8,128)(2,1)S(1)}, u32[]{:S(2)}, u32[]{:S(2)}) collective-permute-start(bf16[2,64,512]{2,1,0:T(8,128)(2,1)S(1)} %get-tuple-element.19), channel_id=1, source_target_pairs={{0,384},{128,0},{256,128},{384,256},{1,385},{129,1},{257,129},{385... | collective-permute-start | bytes 393224 | tf_op jit(solution)/shard_map/ppermute | solution.py:17
  117.1 11.7 %collective-permute-start.8 = (bf16[2,64,512]{2,1,0:T(8,128)(2,1)S(1)}, bf16[2,64,512]{2,1,0:T(8,128)(2,1)S(1)}, u32[]{:S(2)}, u32[]{:S(2)}) collective-permute-start(bf16[2,64,512]{2,1,0:T(8,128)(2,1)S(1)} %get-tuple-element.18), channel_id=1, source_target_pairs={{0,256},{128,384},{256,0},{384,128},{1,257},{129,385},{257,1},{385... | collective-permute-start | bytes 393224 | tf_op jit(solution)/shard_map/ppermute | solution.py:17
  128.9 16.0 %collective-permute-start.15 = (bf16[4,8,1024]{2,1,0:T(8,128)(2,1)S(1)}, bf16[4,8,1024]{2,1,0:T(8,128)(2,1)S(1)}, u32[]{:S(2)}, u32[]{:S(2)}) collective-permute-start(bf16[4,8,1024]{2,1,0:T(8,128)(2,1)S(1)} %get-tuple-element.20), channel_id=1, source_target_pairs={{0,16},{1,17},{2,18},{3,19},{4,20},{5,21},{6,22},{7,23},{16,32},{1... | collective-permute-start | bytes 196616 | tf_op jit(solution)/shard_map/ppermute | solution.py:31
  139.6 6.5 %collective-permute-start.16 = (bf16[4,8,1024]{2,1,0:T(8,128)(2,1)S(1)}, bf16[4,8,1024]{2,1,0:T(8,128)(2,1)S(1)}, u32[]{:S(2)}, u32[]{:S(2)}) collective-permute-start(bf16[4,8,1024]{2,1,0:T(8,128)(2,1)S(1)} %get-tuple-element.21), channel_id=1, source_target_pairs={{0,48},{1,49},{2,50},{3,51},{4,52},{5,53},{6,54},{7,55},{16,0},{17... | collective-permute-start | bytes 196616 | tf_op jit(solution)/shard_map/ppermute | solution.py:31
  141.5 7.1 %collective-permute-start.17 = (bf16[4,8,1024]{2,1,0:T(8,128)(2,1)S(1)}, bf16[4,8,1024]{2,1,0:T(8,128)(2,1)S(1)}, u32[]{:S(2)}, u32[]{:S(2)}) collective-permute-start(bf16[4,8,1024]{2,1,0:T(8,128)(2,1)S(1)} %get-tuple-element.22), channel_id=1, source_target_pairs={{0,32},{1,33},{2,34},{3,35},{4,36},{5,37},{6,38},{7,39},{16,48},{1... | collective-permute-start | bytes 196616 | tf_op jit(solution)/shard_map/ppermute | solution.py:31
  148.6 22.0 %collective-permute-start.18 = (f32[8,1024]{1,0:T(8,128)S(1)}, f32[8,1024]{1,0:T(8,128)S(1)}, u32[]{:S(2)}, u32[]{:S(2)}) collective-permute-start(f32[8,1024]{1,0:T(8,128)S(1)} %get-tuple-element.23), channel_id=1, source_target_pairs={{0,64},{1,65},{2,66},{3,67},{4,68},{5,69},{6,70},{7,71},{16,80},{1... | collective-permute-start | bytes 98312 | tf_op jit(solution)/shard_map/ppermute | solution.py:31
  156.4 14.2 %collective-permute-start.19 = (f32[8,1024]{1,0:T(8,128)S(1)}, f32[8,1024]{1,0:T(8,128)S(1)}, u32[]{:S(2)}, u32[]{:S(2)}) collective-permute-start(f32[8,1024]{1,0:T(8,128)S(1)} %get-tuple-element.25), channel_id=1, source_target_pairs={{0,72},{1,73},{2,74},{3,75},{4,76},{5,77},{6,78},{7,79},{16,88},{1... | collective-permute-start | bytes 98312 | tf_op jit(solution)/shard_map/ppermute | solution.py:31
  160.4 14.8 %collective-permute-start.20 = (f32[8,1024]{1,0:T(8,128)S(1)}, f32[8,1024]{1,0:T(8,128)S(1)}, u32[]{:S(2)}, u32[]{:S(2)}) collective-permute-start(f32[8,1024]{1,0:T(8,128)S(1)} %get-tuple-element.24), channel_id=1, source_target_pairs={{0,8},{1,9},{2,10},{3,11},{4,12},{5,13},{6,14},{7,15},{16,24},{17,... | collective-permute-start | bytes 98312 | tf_op jit(solution)/shard_map/ppermute | solution.py:31
  (3 other events, 17.1 us)
Sparse Core Ops, SparseCore 0:
  10.7 42.3 all-gather.2
  56.1 78.0 all-gather.4

commit v2 on v0

v2 whole, which is shorter than its diff:
```python
import functools
import math

import jax
import jax.numpy as jnp
from jax import lax
from jax.experimental import pallas as pl
from jax.experimental.pallas import tpu as pltpu
from jax.sharding import Mesh
from jax.sharding import PartitionSpec as P

BLOCK = 128
NX, NZL, NZH, NY, NC = 4, 8, 2, 4, 2
NZ = NZL * NZH
AXES = ("x", "zl", "zh", "y", "c")
VMEM_LIMIT = 40 * 1024 * 1024


def shift(value, axis, step):
    size = lax.axis_size(axis)
    return lax.ppermute(value, axis, [(i, (i + step) % size) for i in range(size)])


def chip_shift(value, move):
    def index(x, z, y, c):
        return (((x * NZL + z % NZL) * NZH + z // NZL) * NY + y) * NC + c

    pairs = []
    for x in range(NX):
        for z in range(NZ):
            to_x, to_z = move(x, z)
            for y in range(NY):
                for c in range(NC):
                    pairs.append((index(x, z, y, c), index(to_x, to_z, y, c)))
    return lax.ppermute(value, AXES, pairs)


def pick(array, index, axis):
    return lax.dynamic_index_in_dim(array, index, axis, keepdims=False)


def total_of(parts):
    total = parts[0].astype(jnp.float32)
    for part in parts[1:]:
        total = total + part.astype(jnp.float32)
    return total


def partial_kernel(factor, where, acts, acts_in, grads, grads_in, o0, o1, o2, o3, total):
    dims = (((0,), (0,)), ((), ()))
    value = lax.dot_general(acts[...], grads[...], dims, preferred_element_type=jnp.float32)
    value += lax.dot_general(acts_in[...], grads_in[...], dims, preferred_element_type=jnp.float32)
    total[...] = value * factor
    rows = total.shape[0] // NX
    for k, out in enumerate((o0, o1, o2, o3)):
        start = pl.multiple_of(lax.rem(where[1] + k, NX) * rows, rows)
        out[0] = total[pl.ds(start, rows), :].astype(out.dtype)


def partials(where, acts, acts_in, grads, grads_in, factor):
    tokens, width = acts.shape
    columns = grads.shape[1]
    blocks = NZH * NY
    own = width // (blocks * NC)
    rows = own // NX
    acts_spec = pl.BlockSpec((tokens, own), lambda j, where: (0, j * NC + where[0]))
    grads_spec = pl.BlockSpec((tokens, columns), lambda j, where: (0, 0))
    out_spec = pl.BlockSpec(
        (1, rows, columns),
        lambda j, where: (lax.rem(j % NY + NY - where[2], NY) * NZH + j // NY, 0, 0),
    )
    return pl.pallas_call(
        functools.partial(partial_kernel, factor),
        out_shape=[jax.ShapeDtypeStruct((blocks, rows, columns), jnp.bfloat16)] * NX,
        grid_spec=pltpu.PrefetchScalarGridSpec(
            num_scalar_prefetch=1,
            grid=(blocks,),
            in_specs=[acts_spec, acts_spec, grads_spec, grads_spec],
            out_specs=[out_spec] * NX,
            scratch_shapes=[pltpu.VMEM((own, columns), jnp.float32)],
        ),
        compiler_params=pltpu.CompilerParams(vmem_limit_bytes=VMEM_LIMIT),
        cost_estimate=pl.CostEstimate(
            flops=4 * tokens * columns * own * blocks,
            bytes_accessed=2 * blocks * own * columns + 4 * tokens * width,
            transcendentals=0,
        ),
        name="partials",
    )(where, acts, acts_in, grads, grads_in)


def input_kernel(where, grads, weight, *rest):
    out = rest[-1]
    out[...] = lax.dot_general(
        grads[...], weight[...], (((1,), (1,)), ((), ())), preferred_element_type=jnp.float32
    ).astype(out.dtype)


def input_half(where, grads, weight, width, before=None):
    tokens, columns = grads.shape
    rows = weight.shape[0]
    steps = 4
    block = rows // steps
    in_specs = [
        pl.BlockSpec((tokens, columns), lambda j, where: (0, 0)),
        pl.BlockSpec((block, columns), lambda j, where: (j, 0)),
    ]
    args = [where, grads, weight]
    aliases = {}
    if before is not None:
        in_specs.append(pl.BlockSpec(memory_space=pl.ANY))
        args.append(before)
        aliases = {3: 0}
    return pl.pallas_call(
        input_kernel,
        out_shape=jax.ShapeDtypeStruct((tokens, width), jnp.bfloat16),
        grid_spec=pltpu.PrefetchScalarGridSpec(
            num_scalar_prefetch=1,
            grid=(steps,),
            in_specs=in_specs,
            out_specs=pl.BlockSpec((tokens, block), lambda j, where: (0, where[0] * steps + j)),
        ),
        input_output_aliases=aliases,
        compiler_params=pltpu.CompilerParams(vmem_limit_bytes=VMEM_LIMIT),
        cost_estimate=pl.CostEstimate(
            flops=2 * tokens * columns * rows,
            bytes_accessed=2 * rows * columns + 2 * tokens * (columns + rows),
            transcendentals=0,
        ),
        name="input_half",
    )(*args)


def shards(acts, grads_out, quant, scales):
    tokens, width = acts.shape
    columns = grads_out.shape[1]
    shard_rows = quant.shape[0]
    total_tokens = tokens * lax.axis_size(AXES)
    x, zl, zh, y, c = (lax.axis_index(name) for name in AXES)
    bf16 = jnp.bfloat16

    acts_in = shift(acts, "c", 1)
    grads_in = shift(grads_out, "c", 1)

    blocked = (
        quant.astype(jnp.float32).reshape(shard_rows, columns // BLOCK, BLOCK) * scales[:, :, None]
    )
    weight = blocked.reshape(shard_rows, columns).astype(bf16)
    own_half = lax.all_gather(weight, ("y", "c"), axis=0, tiled=True)

    far = chip_shift(weight, lambda i, z: (i, (z + NZL) % NZ))

    where = jnp.stack([c, x, y]).astype(jnp.int32)
    parts = partials(where, acts, acts_in, grads_out, grads_in, 1.0 / math.sqrt(total_tokens))

    parts = [part.reshape(NY, NZH * NZL * 8, columns) for part in parts]
    received = [parts[0]] + [shift(parts[k], "x", k) for k in (1, 3, 2)]
    own = input_half(zh[None].astype(jnp.int32), grads_out, own_half, width)
    far, own, *received = lax.optimization_barrier((far, own, *received))
    other_half = lax.all_gather(far, ("y", "c"), axis=0, tiled=True)
    summed = [total_of([part[k] for part in received]).astype(bf16) for k in range(NY)]
    received = [summed[0]] + [shift(summed[k], "y", k) for k in (1, 3, 2)]
    rows = total_of(received).astype(bf16).reshape(NZ, 8, columns)
    rows = lax.all_to_all(rows, ("zh", "zl"), split_axis=0, concat_axis=0, tiled=True)
    grad_input = input_half((1 - zh)[None].astype(jnp.int32), grads_out, other_half, width, own)
    rows, grad_input = lax.optimization_barrier((rows, grad_input))
    weight_grad = jnp.sum(rows, axis=0, dtype=jnp.float32)
    return (grad_input, weight_grad)


def solution(mesh):
    fine = Mesh(mesh.devices.reshape(NX, NZL, NZH, NY, NC), AXES)
    tokens = P(AXES, None)
    rows = P(("zh", "y", "c"), None)
    return jax.shard_map(
        shards,
        mesh=fine,
        in_specs=(tokens, tokens, rows, rows),
        out_specs=(tokens, P(("zh", "y", "c", "x", "zl"), None)),
        check_vma=False,
    )
```

time: 608 us -> 158 us (0.26)
  starting transfers between devices: 364 us -> 72.7 us
  waiting for transfers between devices: 206 us -> 41.9 us
  Pallas kernels: 0 us -> 14.2 us
  matrix products: 13.9 us -> 0 us
    all_to_all x2 -> x1, starting transfers between devices: 364 us -> 29.5 us  [shards(): lax.all_to_all(rows, ('zh', 'zl'), split_axis=0, concat_axis=0, tiled=True)]
    all_to_all x2 -> x1, waiting for transfers between devices: 206 us -> 7.58 us  [shards(): lax.all_to_all(rows, ('zh', 'zl'), split_axis=0, concat_axis=0, tiled=True)]
    ppermute x0 -> x9, starting transfers between devices: none -> 43.2 us  [the longest x8 27.5 us: shift(): lax.ppermute(value, axis, [(i, (i + step) % size) for i in range(size)])]
    ppermute x0 -> x9, waiting for transfers between devices: none -> 28.7 us  [the longest x8 17.6 us: shift(): lax.ppermute(value, axis, [(i, (i + step) % size) for i in range(size)])]
    pallas_call x0 -> x3, Pallas kernels: none -> 14.2 us  [the longest x1 8.47 us: partials(): pl.pallas_call(functools.partial(partial_kernel, factor), out_shape=[jax....]
    dot_general x2 -> x0, matrix products: 13.9 us -> none  [the longest x1 7.25 us: shards(): lax.dot_general(grads_out, lax.all_gather(weight_shard, 'local', axis=0,...]
    reduce_sum x2 -> x1, other arithmetic: 7.04 us -> 0.66 us  [shards(): weight_grad = jnp.sum(rows, axis=0, dtype=jnp.float32)]
  transfers between devices with their start and end apart: 3 -> 12, of which waited for: 2 -> 7; matrix products, arithmetic and copies ran while one was open for 2% -> 3% of each run, Pallas kernels for 0% -> 9%
where the time goes in v2:
time: 158 us; the launch traced here: 157 us
  starting transfers between devices  72.7 us (46%)
  waiting for transfers between devices  41.9 us (27%)
  Pallas kernels  14.2 us (9%)
  between operations  14.2 us (9%)
  local copies, waits for them, and re-layouts  7.32 us (5%)
  other arithmetic  7.03 us (4%)
    all_to_all x1, starting transfers between devices, shards(): lax.all_to_all(rows, ('zh', 'zl'), split_axis=0, concat_axis=0, tiled=True)  29.5 us
    ppermute x8, starting transfers between devices, shift(): lax.ppermute(value, axis, [(i, (i + step) % size) for i in range(size)])  27.5 us
    ppermute x8, waiting for transfers between devices, shift(): lax.ppermute(value, axis, [(i, (i + step) % size) for i in range(size)])  17.6 us
    ppermute x1, starting transfers between devices, chip_shift(): return lax.ppermute(value, AXES, pairs)  15.7 us
    ppermute x1, waiting for transfers between devices, chip_shift(): return lax.ppermute(value, AXES, pairs)  11.1 us
    pallas_call x1, Pallas kernels, partials(): pl.pallas_call(functools.partial(partial_kernel, factor), out_shape=[jax....  8.47 us
    all_to_all x1, waiting for transfers between devices, shards(): lax.all_to_all(rows, ('zh', 'zl'), split_axis=0, concat_axis=0, tiled=True)  7.58 us
    unnamed x15, local copies, waits for them, and re-layouts  6.99 us
  transfers between devices with their start and end apart: 12, of which 7 were waited for; matrix products, arithmetic and copies ran while one was open for 3% of the time, Pallas kernels for 9%

profile of v2, /device:TPU:24, one launch (start us, length us, event | category | flops | bytes accessed | tf_op | source)
XLA Modules:
  0.0 157.3 jit_solution(1854538038983821641)
XLA Ops:
  8.4 2.3 %fusion = bf16[256,1024]{1,0:T(8,128)(2,1)} fusion(f32[32,8,8,128]{3,2,1,0:T(8,128)S(1)} %bitcast.31, bf16[256,1024]{1,0:T(8,128)(2,1)} %param.6), kind=kLoop, calls=%fused_computation.1 | loop fusion | flops 786432 | bytes 2097152 | tf_op jit(solution)/shard_map/convert_element_type | solution.py:148
  10.8 1.9 %collective-permute-start.1 = (bf16[224,4096]{1,0:T(8,128)(2,1)S(1)}, bf16[224,4096]{1,0:T(8,128)(2,1)}, u32[]{:S(2)}, u32[]{:S(2)}) collective-permute-start(bf16[224,4096]{1,0:T(8,128)(2,1)S(1)} %copy-done.3), channel_id=1, source_target_pairs={{0,1},{1,0},{2,3},{3,2},{4,5},{5,4},{6,7},{7,6},{8,9},{9,8},{10,11... | collective-permute-start | bytes 5505032 | tf_op jit(solution)/shard_map/ppermute | solution.py:21
  12.7 2.4 %collective-permute-start.2 = (bf16[224,1024]{1,0:T(8,128)(2,1)S(1)}, bf16[224,1024]{1,0:T(8,128)(2,1)S(1)}, u32[]{:S(2)}, u32[]{:S(2)}) collective-permute-start(bf16[224,1024]{1,0:T(8,128)(2,1)S(1)} %copy-done.2), channel_id=1, source_target_pairs={{0,1},{1,0},{2,3},{3,2},{4,5},{5,4},{6,7},{7,6},{8,9},{9,8},{10,11... | collective-permute-start | bytes 1376264 | tf_op jit(solution)/shard_map/ppermute | solution.py:21
  18.9 8.5 %partials.1 = (bf16[8,64,1024]{2,1,0:T(8,128)(2,1)S(1)}, bf16[8,64,1024]{2,1,0:T(8,128)(2,1)}, bf16[8,64,1024]{2,1,0:T(8,128)(2,1)}, bf16[8,64,1024]{2,1,0:T(8,128)(2,1)}) custom-call(s32[3]{0:T(128)S(1)} %pad_add_fusion.where, bf16[224,4096]{1,0:T(8,128)(2,1)S(1)} %copy-done.3, bf16[224,4096]{1,0:T(8,128)(2,1)} %collective-permute-done.1.acts_in, ...), custom_call_target="tpu_custom_call" | custom-call | flops 1879048192 | bytes 7864320 | tf_op jit(solution)/shard_map/partials/pallas_call | solution.py:72
  27.4 3.4 %collective-permute-start.3 = (bf16[4,128,1024]{2,1,0:T(8,128)(2,1)}, bf16[4,128,1024]{2,1,0:T(8,128)(2,1)S(1)}, u32[]{:S(2)}, u32[]{:S(2)}) collective-permute-start(bf16[4,128,1024]{2,1,0:T(8,128)(2,1)} %bitcast.5), channel_id=1, source_target_pairs={{0,128},{128,256},{256,384},{384,0},{1,129},{129,257},{257,385},{3... | collective-permute-start | bytes 3145736 | tf_op jit(solution)/shard_map/ppermute | solution.py:21
  30.8 3.7 %collective-permute-start.4 = (bf16[4,128,1024]{2,1,0:T(8,128)(2,1)}, bf16[4,128,1024]{2,1,0:T(8,128)(2,1)}, u32[]{:S(2)}, u32[]{:S(2)}) collective-permute-start(bf16[4,128,1024]{2,1,0:T(8,128)(2,1)} %bitcast.6), channel_id=1, source_target_pairs={{0,384},{128,0},{256,128},{384,256},{1,385},{129,1},{257,129},{385... | collective-permute-start | bytes 3145736 | tf_op jit(solution)/shard_map/ppermute | solution.py:21
  34.4 3.7 %collective-permute-start.5 = (bf16[4,128,1024]{2,1,0:T(8,128)(2,1)}, bf16[4,128,1024]{2,1,0:T(8,128)(2,1)}, u32[]{:S(2)}, u32[]{:S(2)}) collective-permute-start(bf16[4,128,1024]{2,1,0:T(8,128)(2,1)} %bitcast.7), channel_id=1, source_target_pairs={{0,256},{128,384},{256,0},{384,128},{1,257},{129,385},{257,1},{385... | collective-permute-start | bytes 3145736 | tf_op jit(solution)/shard_map/ppermute | solution.py:21
  38.2 15.7 %collective-permute-start = (bf16[256,1024]{1,0:T(8,128)(2,1)}, bf16[256,1024]{1,0:T(8,128)(2,1)S(1)}, u32[]{:S(2)}, u32[]{:S(2)}) collective-permute-start(bf16[256,1024]{1,0:T(8,128)(2,1)} %fusion), channel_id=1, source_target_pairs={{0,8},{1,9},{2,10},{3,11},{4,12},{5,13},{6,14},{7,15},{16,24},{17,... | collective-permute-start | bytes 1572872 | tf_op jit(solution)/shard_map/ppermute | solution.py:35
  53.9 2.2 %copy-done = bf16[2048,1024]{1,0:T(8,128)(2,1)S(1)} copy-done((bf16[2048,1024]{1,0:T(8,128)(2,1)S(1)}, bf16[2048,1024]{1,0:T(8,128)(2,1)}, u32[]{:S(2)}) %copy-start) | copy-done | bytes 4194328
  56.1 2.8 %input_half.2.rest_0_ = bf16[224,4096]{1,0:T(8,128)(2,1)} custom-call(s32[1]{0:T(128)} %bitcast.where, bf16[224,1024]{1,0:T(8,128)(2,1)S(1)} %copy-done.2, bf16[2048,1024]{1,0:T(8,128)(2,1)S(1)} %copy-done), custom_call_target="tpu_custom_call" | custom-call | flops 939524096 | bytes 5570560 | tf_op jit(solution)/shard_map/input_half/pallas_call | solution.py:114
  59.0 11.1 %collective-permute-done = bf16[256,1024]{1,0:T(8,128)(2,1)S(1)} collective-permute-done((bf16[256,1024]{1,0:T(8,128)(2,1)}, bf16[256,1024]{1,0:T(8,128)(2,1)S(1)}, u32[]{:S(2)}, u32[]{:S(2)}) %collective-permute-start) | collective-permute-done | bytes 524320 | tf_op jit(solution)/shard_map/ppermute | solution.py:35
  70.0 9.4 %collective-permute-done.5 = bf16[4,128,1024]{2,1,0:T(8,128)(2,1)} collective-permute-done((bf16[4,128,1024]{2,1,0:T(8,128)(2,1)}, bf16[4,128,1024]{2,1,0:T(8,128)(2,1)}, u32[]{:S(2)}, u32[]{:S(2)}) %collective-permute-start.5) | collective-permute-done | bytes 1048608 | tf_op jit(solution)/shard_map/ppermute | solution.py:21
  79.5 2.0 %fusion.5 = (bf16[128,1024]{1,0:T(8,128)(2,1)S(1)}, bf16[128,1024]{1,0:T(8,128)(2,1)S(1)}, bf16[128,1024]{1,0:T(8,128)(2,1)S(1)}) fusion(bf16[4,128,1024]{2,1,0:T(8,128)(2,1)} %collective-permute-done.5, bf16[4,128,1024]{2,1,0:T(8,128)(2,1)} %collective-permute-done.4, bf16[4,128,1024]{2,1,0:T(8,128)(2,1)S(1)} %collective-permute-done.3, ...), kind=kLoop, calls=%fused_computation.12 | loop fusion | flops 3145728 | bytes 3932160 | tf_op jit(solution)/shard_map/add | solution.py:45
  81.4 3.4 %collective-permute-start.8 = (bf16[128,1024]{1,0:T(8,128)(2,1)S(1)}, bf16[128,1024]{1,0:T(8,128)(2,1)S(1)}, u32[]{:S(2)}, u32[]{:S(2)}) collective-permute-start(bf16[128,1024]{1,0:T(8,128)(2,1)S(1)} %get-tuple-element.27), channel_id=1, source_target_pairs={{0,4},{2,6},{4,0},{6,2},{1,5},{3,7},{5,1},{7,3},{8,12},{10,14},{12... | collective-permute-start | bytes 786440 | tf_op jit(solution)/shard_map/ppermute | solution.py:21
  84.8 7.1 %collective-permute-start.7 = (bf16[128,1024]{1,0:T(8,128)(2,1)S(1)}, bf16[128,1024]{1,0:T(8,128)(2,1)S(1)}, u32[]{:S(2)}, u32[]{:S(2)}) collective-permute-start(bf16[128,1024]{1,0:T(8,128)(2,1)S(1)} %get-tuple-element.28), channel_id=1, source_target_pairs={{0,6},{2,0},{4,2},{6,4},{1,7},{3,1},{5,3},{7,5},{8,14},{10,8},{12,... | collective-permute-start | bytes 786440 | tf_op jit(solution)/shard_map/ppermute | solution.py:21
  91.9 1.9 %collective-permute-start.6 = (bf16[128,1024]{1,0:T(8,128)(2,1)S(1)}, bf16[128,1024]{1,0:T(8,128)(2,1)S(1)}, u32[]{:S(2)}, u32[]{:S(2)}) collective-permute-start(bf16[128,1024]{1,0:T(8,128)(2,1)S(1)} %get-tuple-element.26), channel_id=1, source_target_pairs={{0,2},{2,4},{4,6},{6,0},{1,3},{3,5},{5,7},{7,1},{8,10},{10,12},{12... | collective-permute-start | bytes 786440 | tf_op jit(solution)/shard_map/ppermute | solution.py:21
  93.9 4.1 %collective-permute-done.7 = bf16[128,1024]{1,0:T(8,128)(2,1)S(1)} collective-permute-done((bf16[128,1024]{1,0:T(8,128)(2,1)S(1)}, bf16[128,1024]{1,0:T(8,128)(2,1)S(1)}, u32[]{:S(2)}, u32[]{:S(2)}) %collective-permute-start.7) | collective-permute-done | bytes 262176 | tf_op jit(solution)/shard_map/ppermute | solution.py:21
  98.0 2.2 %collective-permute-done.6 = bf16[128,1024]{1,0:T(8,128)(2,1)S(1)} collective-permute-done((bf16[128,1024]{1,0:T(8,128)(2,1)S(1)}, bf16[128,1024]{1,0:T(8,128)(2,1)S(1)}, u32[]{:S(2)}, u32[]{:S(2)}) %collective-permute-start.6) | collective-permute-done | bytes 262176 | tf_op jit(solution)/shard_map/ppermute | solution.py:21
  100.2 2.0 %fusion.8 = bf16[16,8,1024]{2,1,0:T(8,128)(2,1)} fusion(bf16[128,1024]{1,0:T(8,128)(2,1)S(1)} %collective-permute-done.8, bf16[128,1024]{1,0:T(8,128)(2,1)S(1)} %collective-permute-done.7, bf16[128,1024]{1,0:T(8,128)(2,1)S(1)} %collective-permute-done.6, bf16[4,128,1024]{2,1,0:T(8,128)(2,1)} %collective-permute-done.5, ...), kind=kLoop, calls=%fused_computation.15 | loop fusion | flops 2097152 | bytes 2097152 | tf_op jit(solution)/shard_map/reshape | solution.py:163
  102.2 29.5 %all-to-all-start = ((bf16[16,8,1024]{2,1,0:T(8,128)(2,1)}), bf16[16,8,1024]{2,1,0:T(8,128)(2,1)S(1)}, u32[]{:S(2)}, u32[]{:S(2)}) async-start(bf16[16,8,1024]{2,1,0:T(8,128)(2,1)} %fusion.8), calls=%async_computation | async-start | bytes 524288 | tf_op jit(solution)/shard_map/all_to_all | solution.py:164
  131.7 5.5 %all-gather.5.cloned.1.call-done.weight = bf16[2048,1024]{1,0:T(8,128)(2,1)} async-done(((bf16[256,1024]{1,0:T(8,128)(2,1)}), bf16[2048,1024]{1,0:T(8,128)(2,1)}) %all-gather.5.cloned.1.call-update) | async-done | bytes 4194320 | tf_op jit(solution)/shard_map/all_gather | solution.py:160
  137.2 2.2 %copy-done.1 = bf16[2048,1024]{1,0:T(8,128)(2,1)S(1)} copy-done((bf16[2048,1024]{1,0:T(8,128)(2,1)S(1)}, bf16[2048,1024]{1,0:T(8,128)(2,1)}, u32[]{:S(2)}) %copy-start.1) | copy-done | bytes 4194328
  139.4 2.8 %input_half.3 = bf16[224,4096]{1,0:T(8,128)(2,1)} custom-call(s32[1]{0:T(128)} %bitcast.13.where, bf16[224,1024]{1,0:T(8,128)(2,1)S(1)} %copy-done.2, bf16[2048,1024]{1,0:T(8,128)(2,1)S(1)} %copy-done.1, bf16[224,4096]{1,0:T(8,128)(2,1)} %input_half.2.rest_0_), custom_call_target="tpu_custom_call", output_to_operand_aliasing={{}: (3, {})} | custom-call | flops 939524096 | bytes 5570560 | tf_op jit(solution)/shard_map/input_half/pallas_call | solution.py:114
  142.3 7.6 %all-to-all-done = bf16[16,8,1024]{2,1,0:T(8,128)(2,1)S(1)} async-done(((bf16[16,8,1024]{2,1,0:T(8,128)(2,1)}), bf16[16,8,1024]{2,1,0:T(8,128)(2,1)S(1)}, u32[]{:S(2)}, u32[]{:S(2)}) %all-to-all-start) | async-done | bytes 262176 | tf_op jit(solution)/shard_map/all_to_all | solution.py:164
  (26 shorter events, 5.7 us)
Async XLA Ops:
  7.2 46.8 %all-gather.3.cloned.1.call-start = ((), (), s32[]{:S(2)}) async-start(), calls=%async_computation.1 | async-start | bytes 4718592 | tf_op jit(solution)/shard_map/all_gather | solution.py:149
  8.0 2.7 %copy-start.3 = (bf16[224,4096]{1,0:T(8,128)(2,1)S(1)}, bf16[224,4096]{1,0:T(8,128)(2,1)}, u32[]{:S(2)}) copy-start(bf16[224,4096]{1,0:T(8,128)(2,1)} %acts.1) | copy-start | bytes 5505028
  8.0 4.7 %copy-start.2 = (bf16[224,1024]{1,0:T(8,128)(2,1)S(1)}, bf16[224,1024]{1,0:T(8,128)(2,1)}, u32[]{:S(2)}) copy-start(bf16[224,1024]{1,0:T(8,128)(2,1)} %grads.5) | copy-start | bytes 1376260
  10.7 126.5 %all-gather.5.cloned.1.call-start = ((), (), s32[]{:S(2)}) async-start(), calls=%async_computation.2 | async-start | bytes 4718592 | tf_op jit(solution)/shard_map/all_gather | solution.py:160
  10.8 7.1 %collective-permute-start.1 = (bf16[224,4096]{1,0:T(8,128)(2,1)S(1)}, bf16[224,4096]{1,0:T(8,128)(2,1)}, u32[]{:S(2)}, u32[]{:S(2)}) collective-permute-start(bf16[224,4096]{1,0:T(8,128)(2,1)S(1)} %copy-done.3), channel_id=1, source_target_pairs={{0,1},{1,0},{2,3},{3,2},{4,5},{5,4},{6,7},{7,6},{8,9},{9,8},{10,11... | collective-permute-start | bytes 5505032 | tf_op jit(solution)/shard_map/ppermute | solution.py:21
  12.7 4.4 %collective-permute-start.2 = (bf16[224,1024]{1,0:T(8,128)(2,1)S(1)}, bf16[224,1024]{1,0:T(8,128)(2,1)S(1)}, u32[]{:S(2)}, u32[]{:S(2)}) collective-permute-start(bf16[224,1024]{1,0:T(8,128)(2,1)S(1)} %copy-done.2), channel_id=1, source_target_pairs={{0,1},{1,0},{2,3},{3,2},{4,5},{5,4},{6,7},{7,6},{8,9},{9,8},{10,11... | collective-permute-start | bytes 1376264 | tf_op jit(solution)/shard_map/ppermute | solution.py:21
  17.1 0.8 copy-start.4
  17.9 1.0 copy-start.5
  27.4 42.7 %collective-permute-start.3 = (bf16[4,128,1024]{2,1,0:T(8,128)(2,1)}, bf16[4,128,1024]{2,1,0:T(8,128)(2,1)S(1)}, u32[]{:S(2)}, u32[]{:S(2)}) collective-permute-start(bf16[4,128,1024]{2,1,0:T(8,128)(2,1)} %bitcast.5), channel_id=1, source_target_pairs={{0,128},{128,256},{256,384},{384,0},{1,129},{129,257},{257,385},{3... | collective-permute-start | bytes 3145736 | tf_op jit(solution)/shard_map/ppermute | solution.py:21
  30.8 39.3 %collective-permute-start.4 = (bf16[4,128,1024]{2,1,0:T(8,128)(2,1)}, bf16[4,128,1024]{2,1,0:T(8,128)(2,1)}, u32[]{:S(2)}, u32[]{:S(2)}) collective-permute-start(bf16[4,128,1024]{2,1,0:T(8,128)(2,1)} %bitcast.6), channel_id=1, source_target_pairs={{0,384},{128,0},{256,128},{384,256},{1,385},{129,1},{257,129},{385... | collective-permute-start | bytes 3145736 | tf_op jit(solution)/shard_map/ppermute | solution.py:21
  34.4 45.0 %collective-permute-start.5 = (bf16[4,128,1024]{2,1,0:T(8,128)(2,1)}, bf16[4,128,1024]{2,1,0:T(8,128)(2,1)}, u32[]{:S(2)}, u32[]{:S(2)}) collective-permute-start(bf16[4,128,1024]{2,1,0:T(8,128)(2,1)} %bitcast.7), channel_id=1, source_target_pairs={{0,256},{128,384},{256,0},{384,128},{1,257},{129,385},{257,1},{385... | collective-permute-start | bytes 3145736 | tf_op jit(solution)/shard_map/ppermute | solution.py:21
  38.2 31.9 %collective-permute-start = (bf16[256,1024]{1,0:T(8,128)(2,1)}, bf16[256,1024]{1,0:T(8,128)(2,1)S(1)}, u32[]{:S(2)}, u32[]{:S(2)}) collective-permute-start(bf16[256,1024]{1,0:T(8,128)(2,1)} %fusion), channel_id=1, source_target_pairs={{0,8},{1,9},{2,10},{3,11},{4,12},{5,13},{6,14},{7,15},{16,24},{17,... | collective-permute-start | bytes 1572872 | tf_op jit(solution)/shard_map/ppermute | solution.py:35
  53.9 2.2 %copy-start = (bf16[2048,1024]{1,0:T(8,128)(2,1)S(1)}, bf16[2048,1024]{1,0:T(8,128)(2,1)}, u32[]{:S(2)}) copy-start(bf16[2048,1024]{1,0:T(8,128)(2,1)} %all-gather.3.cloned.1.call-done.weight) | copy-start | bytes 12582916
  70.0 9.4 %copy-start.6 = (bf16[256,1024]{1,0:T(8,128)(2,1)}, bf16[256,1024]{1,0:T(8,128)(2,1)S(1)}, u32[]{:S(2)}) copy-start(bf16[256,1024]{1,0:T(8,128)(2,1)S(1)} %collective-permute-done) | copy-start | bytes 1572868
  81.4 12.4 %collective-permute-start.8 = (bf16[128,1024]{1,0:T(8,128)(2,1)S(1)}, bf16[128,1024]{1,0:T(8,128)(2,1)S(1)}, u32[]{:S(2)}, u32[]{:S(2)}) collective-permute-start(bf16[128,1024]{1,0:T(8,128)(2,1)S(1)} %get-tuple-element.27), channel_id=1, source_target_pairs={{0,4},{2,6},{4,0},{6,2},{1,5},{3,7},{5,1},{7,3},{8,12},{10,14},{12... | collective-permute-start | bytes 786440 | tf_op jit(solution)/shard_map/ppermute | solution.py:21
  84.8 13.1 %collective-permute-start.7 = (bf16[128,1024]{1,0:T(8,128)(2,1)S(1)}, bf16[128,1024]{1,0:T(8,128)(2,1)S(1)}, u32[]{:S(2)}, u32[]{:S(2)}) collective-permute-start(bf16[128,1024]{1,0:T(8,128)(2,1)S(1)} %get-tuple-element.28), channel_id=1, source_target_pairs={{0,6},{2,0},{4,2},{6,4},{1,7},{3,1},{5,3},{7,5},{8,14},{10,8},{12,... | collective-permute-start | bytes 786440 | tf_op jit(solution)/shard_map/ppermute | solution.py:21
  91.9 8.3 %collective-permute-start.6 = (bf16[128,1024]{1,0:T(8,128)(2,1)S(1)}, bf16[128,1024]{1,0:T(8,128)(2,1)S(1)}, u32[]{:S(2)}, u32[]{:S(2)}) collective-permute-start(bf16[128,1024]{1,0:T(8,128)(2,1)S(1)} %get-tuple-element.26), channel_id=1, source_target_pairs={{0,2},{2,4},{4,6},{6,0},{1,3},{3,5},{5,7},{7,1},{8,10},{10,12},{12... | collective-permute-start | bytes 786440 | tf_op jit(solution)/shard_map/ppermute | solution.py:21
  102.2 47.6 %all-to-all-start = ((bf16[16,8,1024]{2,1,0:T(8,128)(2,1)}), bf16[16,8,1024]{2,1,0:T(8,128)(2,1)S(1)}, u32[]{:S(2)}, u32[]{:S(2)}) async-start(bf16[16,8,1024]{2,1,0:T(8,128)(2,1)} %fusion.8), calls=%async_computation | async-start | bytes 524288 | tf_op jit(solution)/shard_map/all_to_all | solution.py:164
  137.2 2.2 %copy-start.1 = (bf16[2048,1024]{1,0:T(8,128)(2,1)S(1)}, bf16[2048,1024]{1,0:T(8,128)(2,1)}, u32[]{:S(2)}) copy-start(bf16[2048,1024]{1,0:T(8,128)(2,1)} %all-gather.5.cloned.1.call-done.weight) | copy-start | bytes 12582916
Sparse Core Ops, SparseCore 0:
  10.8 42.0 all-gather.2
  79.6 57.5 all-gather.4

commit v3 on v2

v3 whole, which is shorter than its diff:
```python
import functools
import math

import jax
import jax.numpy as jnp
from jax import lax
from jax.experimental import pallas as pl
from jax.experimental.pallas import tpu as pltpu
from jax.sharding import Mesh
from jax.sharding import PartitionSpec as P

BLOCK = 128
NX, NZL, NZH, NY, NC = 4, 8, 2, 4, 2
NZ = NZL * NZH
AXES = ("x", "zl", "zh", "y", "c")
VMEM_LIMIT = 40 * 1024 * 1024


def shift(value, axis, step):
    size = lax.axis_size(axis)
    return lax.ppermute(value, axis, [(i, (i + step) % size) for i in range(size)])


def chip_shift(value, move):
    def index(x, z, y, c):
        return (((x * NZL + z % NZL) * NZH + z // NZL) * NY + y) * NC + c

    pairs = []
    for x in range(NX):
        for z in range(NZ):
            to_x, to_z = move(x, z)
            for y in range(NY):
                for c in range(NC):
                    pairs.append((index(x, z, y, c), index(to_x, to_z, y, c)))
    return lax.ppermute(value, AXES, pairs)


def pick(array, index, axis):
    return lax.dynamic_index_in_dim(array, index, axis, keepdims=False)


def total_of(parts):
    total = parts[0].astype(jnp.float32)
    for part in parts[1:]:
        total = total + part.astype(jnp.float32)
    return total


def weight_kernel(where, quant, scales, weight, quarter):
    rows, columns = quant.shape
    levels = quant[...].astype(jnp.float32)
    factors = scales[...].T
    for block in range(columns // BLOCK):
        run = slice(block * BLOCK, (block + 1) * BLOCK)
        weight[:, run] = (levels[:, run] * factors[:, block : block + 1]).astype(weight.dtype)
    part = quarter.shape[0]
    quarter[...] = weight[pl.ds(pl.multiple_of(where[1] * part, part), part), :]


def weights(where, quant, scales):
    rows, columns = quant.shape
    vmem = pl.BlockSpec(memory_space=pltpu.VMEM)
    return pl.pallas_call(
        weight_kernel,
        out_shape=[
            jax.ShapeDtypeStruct((rows, columns), jnp.bfloat16),
            jax.ShapeDtypeStruct((rows // NX, columns), jnp.bfloat16),
        ],
        in_specs=[pl.BlockSpec(memory_space=pltpu.SMEM), vmem, vmem],
        out_specs=[vmem, vmem],
        compiler_params=pltpu.CompilerParams(vmem_limit_bytes=VMEM_LIMIT),
        cost_estimate=pl.CostEstimate(
            flops=rows * columns, bytes_accessed=4 * rows * columns, transcendentals=0
        ),
        name="weights",
    )(where, quant, scales.T)


def partial_kernel(
    factor, where, acts, acts_in, grads, grads_in, own, right, left, far_a, far_b, lhs, rhs
):
    step = pl.program_id(0)
    tokens = acts.shape[0]
    blocks, rows, _ = own.shape
    span = rows * NX

    @pl.when(step == 0)
    def _():
        rhs[:tokens] = grads[...]
        rhs[tokens:] = grads_in[...]

    for t in range(blocks):
        j = step * blocks + t
        block = (j % NZH) * NY + lax.rem(where[2] + j // NZH, NY)
        start = pl.multiple_of((block * NC + where[0]) * span, span)
        lhs[:tokens, t * span : (t + 1) * span] = acts[:, pl.ds(start, span)]
        lhs[tokens:, t * span : (t + 1) * span] = acts_in[:, pl.ds(start, span)]
    value = lax.dot_general(
        lhs[...], rhs[...], (((0,), (0,)), ((), ())), preferred_element_type=jnp.float32
    )
    value = (value * factor).astype(own.dtype)

    def chunk(x, t, k):
        start = t * span + (x + k) % NX * rows
        return value[start : start + rows]

    for x in range(NX):

        @pl.when(where[1] == x)
        def _():
            for t in range(blocks):
                own[t] = chunk(x, t, 0)
                right[t] = chunk(x, t, 1)
                left[t] = chunk(x, t, 3)

            @pl.when(step == 0)
            def _():
                for t in range(blocks):
                    far_a[t] = chunk(x, t, 2)

            @pl.when(step == 1)
            def _():
                for t in range(blocks):
                    far_b[t] = chunk(x, t, 2)


def partials(where, acts, acts_in, grads, grads_in, factor):
    tokens, width = acts.shape
    columns = grads.shape[1]
    blocks = NZH * NY
    span = width // (blocks * NC)
    rows = span // NX
    half = blocks // 2
    vmem = pl.BlockSpec(memory_space=pltpu.VMEM)
    moving = pl.BlockSpec((half, rows, columns), lambda j, where: (j, 0, 0))
    still = pl.BlockSpec((half, rows, columns), lambda j, where: (0, 0, 0))
    whole = jax.ShapeDtypeStruct((blocks, rows, columns), jnp.bfloat16)
    part = jax.ShapeDtypeStruct((half, rows, columns), jnp.bfloat16)
    return pl.pallas_call(
        functools.partial(partial_kernel, factor),
        out_shape=[whole, whole, whole, part, part],
        grid_spec=pltpu.PrefetchScalarGridSpec(
            num_scalar_prefetch=1,
            grid=(2,),
            in_specs=[vmem] * 4,
            out_specs=[moving, moving, moving, still, still],
            scratch_shapes=[
                pltpu.VMEM((2 * tokens, half * span), jnp.bfloat16),
                pltpu.VMEM((2 * tokens, columns), jnp.bfloat16),
            ],
        ),
        compiler_params=pltpu.CompilerParams(vmem_limit_bytes=VMEM_LIMIT),
        cost_estimate=pl.CostEstimate(
            flops=4 * tokens * columns * span * blocks,
            bytes_accessed=2 * blocks * span * columns + 4 * tokens * width,
            transcendentals=0,
        ),
        name="partials",
    )(where, acts, acts_in, grads, grads_in)


def sum_kernel(own, right, left, *outs):
    total = own[...].astype(jnp.float32) + right[...].astype(jnp.float32)
    total = (total + left[...].astype(jnp.float32)).astype(own.dtype)
    for k, out in enumerate(outs):

        @pl.when(pl.program_id(0) == k)
        def _():
            out[...] = total


def sums(own, right, left):
    blocks, rows, columns = own.shape
    each = blocks // NY
    moving = pl.BlockSpec((each, rows, columns), lambda k: (k, 0, 0))
    still = pl.BlockSpec((each, rows, columns), lambda k: (0, 0, 0))
    return pl.pallas_call(
        sum_kernel,
        out_shape=[jax.ShapeDtypeStruct((each, rows, columns), own.dtype)] * NY,
        grid=(NY,),
        in_specs=[moving] * 3,
        out_specs=[still] * NY,
        compiler_params=pltpu.CompilerParams(vmem_limit_bytes=VMEM_LIMIT),
        cost_estimate=pl.CostEstimate(
            flops=2 * 10**10, bytes_accessed=8 * blocks * rows * columns, transcendentals=0
        ),
        name="sums",
    )(own, right, left)


def input_kernel(where, grads, weight, *rest):
    out = rest[-1]
    pieces, groups, rows, columns = weight.shape
    span = pieces * rows
    for group in range(groups):
        block = weight[:, group].reshape(span, columns)
        out[:, group * span : (group + 1) * span] = lax.dot_general(
            grads[...], block, (((1,), (1,)), ((), ())), preferred_element_type=jnp.float32
        ).astype(out.dtype)


def input_half(where, grads, weight, width, before=None):
    tokens, columns = grads.shape
    pieces, groups, rows, _ = weight.shape
    steps = 4
    each = groups // steps
    block = each * pieces * rows
    in_specs = [
        pl.BlockSpec((tokens, columns), lambda j, where: (0, 0)),
        pl.BlockSpec((pieces, each, rows, columns), lambda j, where: (0, j, 0, 0)),
    ]
    args = [where, grads, weight]
    aliases = {}
    if before is not None:
        in_specs.append(pl.BlockSpec(memory_space=pl.ANY))
        args.append(before)
        aliases = {3: 0}
    return pl.pallas_call(
        input_kernel,
        out_shape=jax.ShapeDtypeStruct((tokens, width), jnp.bfloat16),
        grid_spec=pltpu.PrefetchScalarGridSpec(
            num_scalar_prefetch=1,
            grid=(steps,),
            in_specs=in_specs,
            out_specs=pl.BlockSpec((tokens, block), lambda j, where: (0, where[0] * steps + j)),
        ),
        input_output_aliases=aliases,
        compiler_params=pltpu.CompilerParams(vmem_limit_bytes=VMEM_LIMIT),
        cost_estimate=pl.CostEstimate(
            flops=2 * tokens * columns * pieces * groups * rows,
            bytes_accessed=2 * pieces * groups * rows * columns + 4 * tokens * columns,
            transcendentals=0,
        ),
        name="input_half",
    )(*args)


def shards(acts, grads_out, quant, scales):
    tokens, width = acts.shape
    columns = grads_out.shape[1]
    shard_rows = quant.shape[0]
    total_tokens = tokens * lax.axis_size(AXES)
    x, zh, y, c = (lax.axis_index(name) for name in ("x", "zh", "y", "c"))
    bf16 = jnp.bfloat16
    where = jnp.stack([c, x, y]).astype(jnp.int32)
    groups = NY * NC

    acts_in = shift(acts, "c", 1)
    grads_in = shift(grads_out, "c", 1)
    weight, quarter = weights(where, quant, scales)
    own_half = lax.all_gather(weight, ("y", "c"), axis=0, tiled=True)

    own, right, left, far_a, far_b = partials(
        where, acts, acts_in, grads_out, grads_in, 1.0 / math.sqrt(total_tokens)
    )
    near_a, near_b = shift(far_a, "x", 1), shift(far_b, "x", -1)
    quarter = chip_shift(quarter, lambda i, z: (i, (z + NZL) % NZ))
    half = far_a.shape[0]
    right = jnp.concatenate([total_of([right[:half], near_a]).astype(bf16), right[half:]], axis=0)
    left = jnp.concatenate([left[:half], total_of([left[half:], near_b]).astype(bf16)], axis=0)
    grads_later, right, left = lax.optimization_barrier((grads_out, right, left))
    right, left = shift(right, "x", 1), shift(left, "x", -1)

    own_half = own_half.reshape(1, groups, shard_rows, columns)
    grad_input = input_half(zh[None].astype(jnp.int32), grads_later, own_half, width)
    quarter, grad_input = lax.optimization_barrier((quarter, grad_input))
    grad_input, right, left = lax.optimization_barrier((grad_input, right, left))
    other_half = lax.all_gather(quarter, ("x", "y", "c"), axis=0, tiled=True)

    summed = sums(own, right, left)
    received = [summed[0]] + [shift(summed[k], "y", k) for k in (1, 3, 2)]
    rows = total_of(received).astype(bf16).reshape(NZH, NZL, 8, columns)
    rows = lax.all_to_all(rows.swapaxes(0, 1), "zl", split_axis=0, concat_axis=0, tiled=True)
    rows = jnp.sum(rows, axis=0, dtype=jnp.float32)
    away = chip_shift(pick(rows, 1 - zh, 0), lambda i, z: (i, (z + NZL) % NZ))
    other_half = other_half.reshape(NX, groups, shard_rows // NX, columns)
    grad_input = input_half(
        (1 - zh)[None].astype(jnp.int32), grads_later, other_half, width, grad_input
    )
    grad_input, away = lax.optimization_barrier((grad_input, away))
    weight_grad = pick(rows, zh, 0) + away
    return (grad_input, weight_grad)


def solution(mesh):
    fine = Mesh(mesh.devices.reshape(NX, NZL, NZH, NY, NC), AXES)
    tokens = P(AXES, None)
    rows = P(("zh", "y", "c"), None)
    return jax.shard_map(
        shards,
        mesh=fine,
        in_specs=(tokens, tokens, rows, rows),
        out_specs=(tokens, P(("zh", "y", "c", "x", "zl"), None)),
        check_vma=False,
    )
```

time: 158 us -> 162 us (1.025)
  waiting for transfers between devices: 41.9 us -> 56.2 us
  starting transfers between devices: 72.7 us -> 60 us
  local copies, waits for them, and re-layouts: 7.32 us -> 10.4 us
    ppermute x8 -> x9, waiting for transfers between devices: 17.6 us -> 39.7 us  [shift(): lax.ppermute(value, axis, [(i, (i + step) % size) for i in range(size)])]
    all_to_all x1, starting transfers between devices: 29.5 us -> 10.1 us  [shards(): lax.all_to_all(rows.swapaxes(0, 1), 'zl', split_axis=0, concat_axis=0, ti...]
    ppermute x1 -> x2, waiting for transfers between devices: 11.1 us -> 3.07 us  [chip_shift(): return lax.ppermute(value, AXES, pairs)]
    ppermute x1 -> x2, starting transfers between devices: 15.7 us -> 21.9 us  [chip_shift(): return lax.ppermute(value, AXES, pairs)]
    all_gather x1, waiting for transfers between devices: 5.52 us -> 0.02 us  [shards(): other_half = lax.all_gather(quarter, ('x', 'y', 'c'), axis=0, tiled=True)]
    all_to_all x1, waiting for transfers between devices: 7.58 us -> 13.1 us  [shards(): lax.all_to_all(rows.swapaxes(0, 1), 'zl', split_axis=0, concat_axis=0, ti...]
    unnamed x15 -> x22, local copies, waits for them, and re-layouts: 6.99 us -> 10.3 us
    concatenate x0 -> x2, other arithmetic: none -> 2.12 us  [the longest x1 1.07 us: shards(): jnp.concatenate([left[:half], total_of([left[half:], near_b]).astype(bf16...]
  transfers between devices with their start and end apart: 12 -> 14, of which waited for: 7 -> 7; matrix products, arithmetic and copies ran while one was open for 3% -> 4% of each run, Pallas kernels for 9% -> 7%
where the time goes in v3:
time: 162 us; the launch traced here: 160 us
  starting transfers between devices  60 us (37%)
  waiting for transfers between devices  56.2 us (35%)
  between operations  14.2 us (9%)
  Pallas kernels  13.3 us (8%)
  local copies, waits for them, and re-layouts  10.4 us (6%)
  other arithmetic  6.26 us (4%)
    ppermute x9, waiting for transfers between devices, shift(): lax.ppermute(value, axis, [(i, (i + step) % size) for i in range(size)])  39.7 us
    ppermute x9, starting transfers between devices, shift(): lax.ppermute(value, axis, [(i, (i + step) % size) for i in range(size)])  28 us
    ppermute x2, starting transfers between devices, chip_shift(): return lax.ppermute(value, AXES, pairs)  21.9 us
    all_to_all x1, waiting for transfers between devices, shards(): lax.all_to_all(rows.swapaxes(0, 1), 'zl', split_axis=0, concat_axis=0, ti...  13.1 us
    unnamed x22, local copies, waits for them, and re-layouts  10.3 us
    all_to_all x1, starting transfers between devices, shards(): lax.all_to_all(rows.swapaxes(0, 1), 'zl', split_axis=0, concat_axis=0, ti...  10.1 us
    pallas_call x2, Pallas kernels, input_half(): pl.pallas_call(input_kernel, out_shape=jax.ShapeDtypeStruct((tokens, widt...  5.91 us
    pallas_call x1, Pallas kernels, partials(): pl.pallas_call(functools.partial(partial_kernel, factor), out_shape=[whol...  4.75 us
  transfers between devices with their start and end apart: 14, of which 7 were waited for; matrix products, arithmetic and copies ran while one was open for 4% of the time, Pallas kernels for 7%

profile of v3, /device:TPU:24, one launch (start us, length us, event | category | flops | bytes accessed | tf_op | source)
XLA Modules:
  0.0 160.3 jit_solution(7318901741634469563)
XLA Ops:
  9.0 1.8 %weights.1 = (bf16[256,1024]{1,0:T(8,128)(2,1)}, bf16[64,1024]{1,0:T(8,128)(2,1)S(1)}) custom-call(s32[3]{0:T(128)S(1)} %pad_add_fusion.where, bf16[256,1024]{1,0:T(8,128)(2,1)S(1)} %copy-done.4, f32[8,256]{1,0:T(8,128)S(1)} %bitcast.19), custom_call_target="tpu_custom_call" | custom-call | flops 262144 | bytes 1048576 | tf_op jit(solution)/shard_map/weights/pallas_call | solution.py:63
  11.0 1.9 %collective-permute-start = (bf16[224,4096]{1,0:T(8,128)(2,1)}, bf16[224,4096]{1,0:T(8,128)(2,1)S(1)}, u32[]{:S(2)}, u32[]{:S(2)}) collective-permute-start(bf16[224,4096]{1,0:T(8,128)(2,1)} %acts.1), channel_id=1, source_target_pairs={{0,1},{1,0},{2,3},{3,2},{4,5},{5,4},{6,7},{7,6},{8,9},{9,8},{10,11... | collective-permute-start | bytes 5505032 | tf_op jit(solution)/shard_map/ppermute | solution.py:21
  12.9 2.4 %collective-permute-start.1 = (bf16[224,1024]{1,0:T(8,128)(2,1)}, bf16[224,1024]{1,0:T(8,128)(2,1)S(1)}, u32[]{:S(2)}, u32[]{:S(2)}) collective-permute-start(bf16[224,1024]{1,0:T(8,128)(2,1)} %grads.3), channel_id=1, source_target_pairs={{0,1},{1,0},{2,3},{3,2},{4,5},{5,4},{6,7},{7,6},{8,9},{9,8},{10,11... | collective-permute-start | bytes 1376264 | tf_op jit(solution)/shard_map/ppermute | solution.py:21
  15.3 2.2 %collective-permute-done.1.grads_in = bf16[224,1024]{1,0:T(8,128)(2,1)S(1)} collective-permute-done((bf16[224,1024]{1,0:T(8,128)(2,1)}, bf16[224,1024]{1,0:T(8,128)(2,1)S(1)}, u32[]{:S(2)}, u32[]{:S(2)}) %collective-permute-start.1) | collective-permute-done | bytes 458784 | tf_op jit(solution)/shard_map/ppermute | solution.py:21
  20.0 4.7 %partials.1 = (bf16[8,64,1024]{2,1,0:T(8,128)(2,1)S(1)}, bf16[8,64,1024]{2,1,0:T(8,128)(2,1)S(1)}, bf16[8,64,1024]{2,1,0:T(8,128)(2,1)S(1)}, bf16[4,64,1024]{2,1,0:T(8,128)(2,1)S(1)}, bf16[4,64,1024]{2,1,0:T(8,128)(2,1)}) custom-call(s32[3]{0:T(128)S(1)} %pad_add_fusion.where, bf16[224,4096]{1,0:T(8,128)(2,1)S(1)} %copy-done.6, ...), custom_call_target="tpu_custom_call" | custom-call | flops 1879048192 | bytes 7864320 | tf_op jit(solution)/shard_map/partials/pallas_call | solution.py:139
  25.8 4.6 %collective-permute-start.3 = (bf16[4,64,1024]{2,1,0:T(8,128)(2,1)}, bf16[4,64,1024]{2,1,0:T(8,128)(2,1)}, u32[]{:S(2)}, u32[]{:S(2)}) collective-permute-start(bf16[4,64,1024]{2,1,0:T(8,128)(2,1)} %get-tuple-element.26), channel_id=1, source_target_pairs={{0,384},{128,0},{256,128},{384,256},{1,385},{129,1},{257,129},{385... | collective-permute-start | bytes 1572872 | tf_op jit(solution)/shard_map/ppermute | solution.py:21
  30.4 1.9 %collective-permute-start.2 = (bf16[4,64,1024]{2,1,0:T(8,128)(2,1)S(1)}, bf16[4,64,1024]{2,1,0:T(8,128)(2,1)}, u32[]{:S(2)}, u32[]{:S(2)}) collective-permute-start(bf16[4,64,1024]{2,1,0:T(8,128)(2,1)S(1)} %get-tuple-element.24), channel_id=1, source_target_pairs={{0,128},{128,256},{256,384},{384,0},{1,129},{129,257},{257,385},{3... | collective-permute-start | bytes 1572872 | tf_op jit(solution)/shard_map/ppermute | solution.py:21
  32.4 15.7 %collective-permute-start.4 = (bf16[64,1024]{1,0:T(8,128)(2,1)S(1)}, bf16[64,1024]{1,0:T(8,128)(2,1)S(1)}, u32[]{:S(2)}, u32[]{:S(2)}) collective-permute-start(bf16[64,1024]{1,0:T(8,128)(2,1)S(1)} %get-tuple-element.28), channel_id=1, source_target_pairs={{0,8},{1,9},{2,10},{3,11},{4,12},{5,13},{6,14},{7,15},{16,24},{17,... | collective-permute-start | bytes 393224 | tf_op jit(solution)/shard_map/ppermute | solution.py:35
  53.2 2.2 %copy-done.1 = bf16[2048,1024]{1,0:T(8,128)(2,1)S(1)} copy-done((bf16[2048,1024]{1,0:T(8,128)(2,1)S(1)}, bf16[2048,1024]{1,0:T(8,128)(2,1)}, u32[]{:S(2)}) %copy-start.1) | copy-done | bytes 4194328
  55.4 2.8 %input_half.2.rest_0_ = bf16[224,4096]{1,0:T(8,128)(2,1)} custom-call(s32[1]{0:T(128)} %bitcast.5.where, bf16[224,1024]{1,0:T(8,128)(2,1)S(1)} %copy-done.3, bf16[1,8,256,1024]{3,2,1,0:T(8,128)(2,1)S(1)} %bitcast.18), custom_call_target="tpu_custom_call" | custom-call | flops 939524096 | bytes 5111808 | tf_op jit(solution)/shard_map/input_half/pallas_call | solution.py:218
  58.9 3.4 %collective-permute-start.5 = (bf16[8,64,1024]{2,1,0:T(8,128)(2,1)}, bf16[8,64,1024]{2,1,0:T(8,128)(2,1)S(1)}, u32[]{:S(2)}, u32[]{:S(2)}) collective-permute-start(bf16[8,64,1024]{2,1,0:T(8,128)(2,1)} %pad_maximum_fusion), channel_id=1, source_target_pairs={{0,128},{128,256},{256,384},{384,0},{1,129},{129,257},{257,385},{3... | collective-permute-start | bytes 3145736 | tf_op jit(solution)/shard_map/ppermute | solution.py:21
  62.3 3.7 %collective-permute-start.6 = (bf16[8,64,1024]{2,1,0:T(8,128)(2,1)S(1)}, bf16[8,64,1024]{2,1,0:T(8,128)(2,1)S(1)}, u32[]{:S(2)}, u32[]{:S(2)}) collective-permute-start(bf16[8,64,1024]{2,1,0:T(8,128)(2,1)S(1)} %copy-done.9), channel_id=1, source_target_pairs={{0,384},{128,0},{256,128},{384,256},{1,385},{129,1},{257,129},{385... | collective-permute-start | bytes 3145736 | tf_op jit(solution)/shard_map/ppermute | solution.py:21
  65.9 23.2 %collective-permute-done.5.right = bf16[8,64,1024]{2,1,0:T(8,128)(2,1)S(1)} collective-permute-done((bf16[8,64,1024]{2,1,0:T(8,128)(2,1)}, bf16[8,64,1024]{2,1,0:T(8,128)(2,1)S(1)}, u32[]{:S(2)}, u32[]{:S(2)}) %collective-permute-start.5) | collective-permute-done | bytes 1048608 | tf_op jit(solution)/shard_map/ppermute | solution.py:21
  89.2 2.1 %collective-permute-done.6.left = bf16[8,64,1024]{2,1,0:T(8,128)(2,1)S(1)} collective-permute-done((bf16[8,64,1024]{2,1,0:T(8,128)(2,1)S(1)}, bf16[8,64,1024]{2,1,0:T(8,128)(2,1)S(1)}, u32[]{:S(2)}, u32[]{:S(2)}) %collective-permute-start.6) | collective-permute-done | bytes 1048608 | tf_op jit(solution)/shard_map/ppermute | solution.py:21
  92.1 4.3 %collective-permute-start.7 = (bf16[2,64,1024]{2,1,0:T(8,128)(2,1)S(1)}, bf16[2,64,1024]{2,1,0:T(8,128)(2,1)S(1)}, u32[]{:S(2)}, u32[]{:S(2)}) collective-permute-start(bf16[2,64,1024]{2,1,0:T(8,128)(2,1)S(1)} %get-tuple-element.39), channel_id=1, source_target_pairs={{0,2},{2,4},{4,6},{6,0},{1,3},{3,5},{5,7},{7,1},{8,10},{10,12},{12... | collective-permute-start | bytes 786440 | tf_op jit(solution)/shard_map/ppermute | solution.py:21
  96.4 1.9 %collective-permute-start.8 = (bf16[2,64,1024]{2,1,0:T(8,128)(2,1)S(1)}, bf16[2,64,1024]{2,1,0:T(8,128)(2,1)S(1)}, u32[]{:S(2)}, u32[]{:S(2)}) collective-permute-start(bf16[2,64,1024]{2,1,0:T(8,128)(2,1)S(1)} %get-tuple-element.40), channel_id=1, source_target_pairs={{0,6},{2,0},{4,2},{6,4},{1,7},{3,1},{5,3},{7,5},{8,14},{10,8},{12,... | collective-permute-start | bytes 786440 | tf_op jit(solution)/shard_map/ppermute | solution.py:21
  98.3 3.8 %collective-permute-start.9 = (bf16[2,64,1024]{2,1,0:T(8,128)(2,1)S(1)}, bf16[2,64,1024]{2,1,0:T(8,128)(2,1)S(1)}, u32[]{:S(2)}, u32[]{:S(2)}) collective-permute-start(bf16[2,64,1024]{2,1,0:T(8,128)(2,1)S(1)} %get-tuple-element.41), channel_id=1, source_target_pairs={{0,4},{2,6},{4,0},{6,2},{1,5},{3,7},{5,1},{7,3},{8,12},{10,14},{12... | collective-permute-start | bytes 786440 | tf_op jit(solution)/shard_map/ppermute | solution.py:21
  102.1 12.1 %collective-permute-done.8 = bf16[2,64,1024]{2,1,0:T(8,128)(2,1)S(1)} collective-permute-done((bf16[2,64,1024]{2,1,0:T(8,128)(2,1)S(1)}, bf16[2,64,1024]{2,1,0:T(8,128)(2,1)S(1)}, u32[]{:S(2)}, u32[]{:S(2)}) %collective-permute-start.8) | collective-permute-done | bytes 262176 | tf_op jit(solution)/shard_map/ppermute | solution.py:21
  115.1 10.1 %all-to-all-start = ((bf16[8,2,8,1024]{3,2,1,0:T(8,128)(2,1)}), bf16[8,2,8,1024]{3,2,1,0:T(8,128)(2,1)S(1)}, u32[]{:S(2)}, u32[]{:S(2)}) async-start(bf16[8,2,8,1024]{3,2,1,0:T(8,128)(2,1)} %copy_bitcast_fusion), calls=%async_computation | async-start | bytes 524288 | tf_op jit(solution)/shard_map/all_to_all | solution.py:273
  125.2 13.1 %all-to-all-done = bf16[8,2,8,1024]{3,2,1,0:T(8,128)(2,1)S(1)} async-done(((bf16[8,2,8,1024]{3,2,1,0:T(8,128)(2,1)}), bf16[8,2,8,1024]{3,2,1,0:T(8,128)(2,1)S(1)}, u32[]{:S(2)}, u32[]{:S(2)}) %all-to-all-start) | async-done | bytes 262176 | tf_op jit(solution)/shard_map/all_to_all | solution.py:273
  138.3 6.2 %collective-permute-start.10 = (f32[8,1024]{1,0:T(8,128)S(1)}, f32[8,1024]{1,0:T(8,128)S(1)}, u32[]{:S(2)}, u32[]{:S(2)}) collective-permute-start(f32[8,1024]{1,0:T(8,128)S(1)} %dynamic-slice_bitcast_fusion), channel_id=1, source_target_pairs={{0,8},{1,9},{2,10},{3,11},{4,12},{5,13},{6,14},{7,15},{16,24},{17,... | collective-permute-start | bytes 98312 | tf_op jit(solution)/shard_map/ppermute | solution.py:35
  144.5 2.2 %copy-done = bf16[2048,1024]{1,0:T(8,128)(2,1)S(1)} copy-done((bf16[2048,1024]{1,0:T(8,128)(2,1)S(1)}, bf16[2048,1024]{1,0:T(8,128)(2,1)}, u32[]{:S(2)}) %copy-start) | copy-done | bytes 4194328
  146.7 3.1 %input_half.3 = bf16[224,4096]{1,0:T(8,128)(2,1)} custom-call(s32[1]{0:T(128)} %bitcast.where, bf16[224,1024]{1,0:T(8,128)(2,1)S(1)} %copy-done.3, bf16[4,8,64,1024]{3,2,1,0:T(8,128)(2,1)S(1)} %bitcast.17, bf16[224,4096]{1,0:T(8,128)(2,1)} %input_half.2.rest_0_), custom_call_target="tpu_custom_call", output_to_operand_aliasing={{}: (3, {})} | custom-call | flops 939524096 | bytes 5111808 | tf_op jit(solution)/shard_map/input_half/pallas_call | solution.py:218
  149.8 3.1 %collective-permute-done.10 = f32[8,1024]{1,0:T(8,128)S(1)} collective-permute-done((f32[8,1024]{1,0:T(8,128)S(1)}, f32[8,1024]{1,0:T(8,128)S(1)}, u32[]{:S(2)}, u32[]{:S(2)}) %collective-permute-start.10) | collective-permute-done | bytes 32800 | tf_op jit(solution)/shard_map/ppermute | solution.py:35
  (44 shorter events, 13.5 us)
Async XLA Ops:
  7.2 46.0 %all-gather.3.cloned.1.call-start = ((), (), s32[]{:S(2)}) async-start(), calls=%async_computation.1 | async-start | bytes 4718592 | tf_op jit(solution)/shard_map/all_gather | solution.py:251
  7.3 1.0 copy-start.4
  8.3 0.7 copy-start.5
  10.9 133.6 %all-gather.5.cloned.1.call-start = ((), (), s32[]{:S(2)}) async-start(), calls=%async_computation.2 | async-start | bytes 4325376 | tf_op jit(solution)/shard_map/all_gather | solution.py:268
  11.0 6.6 %collective-permute-start = (bf16[224,4096]{1,0:T(8,128)(2,1)}, bf16[224,4096]{1,0:T(8,128)(2,1)S(1)}, u32[]{:S(2)}, u32[]{:S(2)}) collective-permute-start(bf16[224,4096]{1,0:T(8,128)(2,1)} %acts.1), channel_id=1, source_target_pairs={{0,1},{1,0},{2,3},{3,2},{4,5},{5,4},{6,7},{7,6},{8,9},{9,8},{10,11... | collective-permute-start | bytes 5505032 | tf_op jit(solution)/shard_map/ppermute | solution.py:21
  12.9 4.6 %collective-permute-start.1 = (bf16[224,1024]{1,0:T(8,128)(2,1)}, bf16[224,1024]{1,0:T(8,128)(2,1)S(1)}, u32[]{:S(2)}, u32[]{:S(2)}) collective-permute-start(bf16[224,1024]{1,0:T(8,128)(2,1)} %grads.3), channel_id=1, source_target_pairs={{0,1},{1,0},{2,3},{3,2},{4,5},{5,4},{6,7},{7,6},{8,9},{9,8},{10,11... | collective-permute-start | bytes 1376264 | tf_op jit(solution)/shard_map/ppermute | solution.py:21
  17.5 1.0 copy-start.2
  18.5 1.5 copy-start.6
  24.8 1.0 copy-start.7
  25.8 22.4 %collective-permute-start.3 = (bf16[4,64,1024]{2,1,0:T(8,128)(2,1)}, bf16[4,64,1024]{2,1,0:T(8,128)(2,1)}, u32[]{:S(2)}, u32[]{:S(2)}) collective-permute-start(bf16[4,64,1024]{2,1,0:T(8,128)(2,1)} %get-tuple-element.26), channel_id=1, source_target_pairs={{0,384},{128,0},{256,128},{384,256},{1,385},{129,1},{257,129},{385... | collective-permute-start | bytes 1572872 | tf_op jit(solution)/shard_map/ppermute | solution.py:21
  30.4 20.1 %collective-permute-start.2 = (bf16[4,64,1024]{2,1,0:T(8,128)(2,1)S(1)}, bf16[4,64,1024]{2,1,0:T(8,128)(2,1)}, u32[]{:S(2)}, u32[]{:S(2)}) collective-permute-start(bf16[4,64,1024]{2,1,0:T(8,128)(2,1)S(1)} %get-tuple-element.24), channel_id=1, source_target_pairs={{0,128},{128,256},{256,384},{384,0},{1,129},{129,257},{257,385},{3... | collective-permute-start | bytes 1572872 | tf_op jit(solution)/shard_map/ppermute | solution.py:21
  32.4 25.9 %collective-permute-start.4 = (bf16[64,1024]{1,0:T(8,128)(2,1)S(1)}, bf16[64,1024]{1,0:T(8,128)(2,1)S(1)}, u32[]{:S(2)}, u32[]{:S(2)}) collective-permute-start(bf16[64,1024]{1,0:T(8,128)(2,1)S(1)} %get-tuple-element.28), channel_id=1, source_target_pairs={{0,8},{1,9},{2,10},{3,11},{4,12},{5,13},{6,14},{7,15},{16,24},{17,... | collective-permute-start | bytes 393224 | tf_op jit(solution)/shard_map/ppermute | solution.py:35
  50.5 2.7 %copy-start.3 = (bf16[224,1024]{1,0:T(8,128)(2,1)S(1)}, bf16[224,1024]{1,0:T(8,128)(2,1)}, u32[]{:S(2)}) copy-start(bf16[224,1024]{1,0:T(8,128)(2,1)} %grads.3) | copy-start | bytes 1376260
  53.2 2.2 %copy-start.1 = (bf16[2048,1024]{1,0:T(8,128)(2,1)S(1)}, bf16[2048,1024]{1,0:T(8,128)(2,1)}, u32[]{:S(2)}) copy-start(bf16[2048,1024]{1,0:T(8,128)(2,1)} %all-gather.3.cloned.1.call-done) | copy-start | bytes 12582916
  55.4 6.9 %copy-start.9 = (bf16[8,64,1024]{2,1,0:T(8,128)(2,1)S(1)}, bf16[8,64,1024]{2,1,0:T(8,128)(2,1)}, u32[]{:S(2)}) copy-start(bf16[8,64,1024]{2,1,0:T(8,128)(2,1)} %pad_maximum_fusion.1) | copy-start | bytes 3145732
  55.4 35.9 %copy-start.8 = (bf16[8,64,1024]{2,1,0:T(8,128)(2,1)S(1)}, bf16[8,64,1024]{2,1,0:T(8,128)(2,1)}, u32[]{:S(2)}) copy-start(bf16[8,64,1024]{2,1,0:T(8,128)(2,1)} %copy-done.7) | copy-start | bytes 3145732
  58.9 30.3 %collective-permute-start.5 = (bf16[8,64,1024]{2,1,0:T(8,128)(2,1)}, bf16[8,64,1024]{2,1,0:T(8,128)(2,1)S(1)}, u32[]{:S(2)}, u32[]{:S(2)}) collective-permute-start(bf16[8,64,1024]{2,1,0:T(8,128)(2,1)} %pad_maximum_fusion), channel_id=1, source_target_pairs={{0,128},{128,256},{256,384},{384,0},{1,129},{129,257},{257,385},{3... | collective-permute-start | bytes 3145736 | tf_op jit(solution)/shard_map/ppermute | solution.py:21
  62.3 29.0 %collective-permute-start.6 = (bf16[8,64,1024]{2,1,0:T(8,128)(2,1)S(1)}, bf16[8,64,1024]{2,1,0:T(8,128)(2,1)S(1)}, u32[]{:S(2)}, u32[]{:S(2)}) collective-permute-start(bf16[8,64,1024]{2,1,0:T(8,128)(2,1)S(1)} %copy-done.9), channel_id=1, source_target_pairs={{0,384},{128,0},{256,128},{384,256},{1,385},{129,1},{257,129},{385... | collective-permute-start | bytes 3145736 | tf_op jit(solution)/shard_map/ppermute | solution.py:21
  92.1 10.1 %collective-permute-start.7 = (bf16[2,64,1024]{2,1,0:T(8,128)(2,1)S(1)}, bf16[2,64,1024]{2,1,0:T(8,128)(2,1)S(1)}, u32[]{:S(2)}, u32[]{:S(2)}) collective-permute-start(bf16[2,64,1024]{2,1,0:T(8,128)(2,1)S(1)} %get-tuple-element.39), channel_id=1, source_target_pairs={{0,2},{2,4},{4,6},{6,0},{1,3},{3,5},{5,7},{7,1},{8,10},{10,12},{12... | collective-permute-start | bytes 786440 | tf_op jit(solution)/shard_map/ppermute | solution.py:21
  96.4 17.8 %collective-permute-start.8 = (bf16[2,64,1024]{2,1,0:T(8,128)(2,1)S(1)}, bf16[2,64,1024]{2,1,0:T(8,128)(2,1)S(1)}, u32[]{:S(2)}, u32[]{:S(2)}) collective-permute-start(bf16[2,64,1024]{2,1,0:T(8,128)(2,1)S(1)} %get-tuple-element.40), channel_id=1, source_target_pairs={{0,6},{2,0},{4,2},{6,4},{1,7},{3,1},{5,3},{7,5},{8,14},{10,8},{12,... | collective-permute-start | bytes 786440 | tf_op jit(solution)/shard_map/ppermute | solution.py:21
  98.3 15.9 %collective-permute-start.9 = (bf16[2,64,1024]{2,1,0:T(8,128)(2,1)S(1)}, bf16[2,64,1024]{2,1,0:T(8,128)(2,1)S(1)}, u32[]{:S(2)}, u32[]{:S(2)}) collective-permute-start(bf16[2,64,1024]{2,1,0:T(8,128)(2,1)S(1)} %get-tuple-element.41), channel_id=1, source_target_pairs={{0,4},{2,6},{4,0},{6,2},{1,5},{3,7},{5,1},{7,3},{8,12},{10,14},{12... | collective-permute-start | bytes 786440 | tf_op jit(solution)/shard_map/ppermute | solution.py:21
  115.1 23.1 %all-to-all-start = ((bf16[8,2,8,1024]{3,2,1,0:T(8,128)(2,1)}), bf16[8,2,8,1024]{3,2,1,0:T(8,128)(2,1)S(1)}, u32[]{:S(2)}, u32[]{:S(2)}) async-start(bf16[8,2,8,1024]{3,2,1,0:T(8,128)(2,1)} %copy_bitcast_fusion), calls=%async_computation | async-start | bytes 524288 | tf_op jit(solution)/shard_map/all_to_all | solution.py:273
  138.3 14.5 %collective-permute-start.10 = (f32[8,1024]{1,0:T(8,128)S(1)}, f32[8,1024]{1,0:T(8,128)S(1)}, u32[]{:S(2)}, u32[]{:S(2)}) collective-permute-start(f32[8,1024]{1,0:T(8,128)S(1)} %dynamic-slice_bitcast_fusion), channel_id=1, source_target_pairs={{0,8},{1,9},{2,10},{3,11},{4,12},{5,13},{6,14},{7,15},{16,24},{17,... | collective-permute-start | bytes 98312 | tf_op jit(solution)/shard_map/ppermute | solution.py:35
  144.5 2.2 %copy-start = (bf16[2048,1024]{1,0:T(8,128)(2,1)S(1)}, bf16[2048,1024]{1,0:T(8,128)(2,1)}, u32[]{:S(2)}) copy-start(bf16[2048,1024]{1,0:T(8,128)(2,1)} %all-gather.5.cloned.1.call-done) | copy-start | bytes 12582916
  (1 other events, 0.6 us)
Sparse Core Ops, SparseCore 0:
  11.0 42.0 all-gather.2
  59.0 65.6 all-gather.4

commit v4 on v3

v4 whole, which is shorter than its diff:
```python
import functools
import math

import jax
import jax.numpy as jnp
from jax import lax
from jax.experimental import pallas as pl
from jax.experimental.pallas import tpu as pltpu
from jax.sharding import Mesh
from jax.sharding import PartitionSpec as P

BLOCK = 128
NX, NZL, NZH, NY, NC = 4, 8, 2, 4, 2
NZ = NZL * NZH
AXES = ("x", "zl", "zh", "y", "c")
MIB = 1024 * 1024


def shift(value, axis, step):
    size = lax.axis_size(axis)
    return lax.ppermute(value, axis, [(i, (i + step) % size) for i in range(size)])


def chip_shift(value, move):
    def index(x, z, y, c):
        return (((x * NZL + z % NZL) * NZH + z // NZL) * NY + y) * NC + c

    pairs = []
    for x in range(NX):
        for z in range(NZ):
            to_x, to_z = move(x, z)
            for y in range(NY):
                for c in range(NC):
                    pairs.append((index(x, z, y, c), index(to_x, to_z, y, c)))
    return lax.ppermute(value, AXES, pairs)


def weight_kernel(where, quant, scales, weight, quarter):
    rows, columns = quant.shape
    levels = quant[...].astype(jnp.float32)
    factors = scales[...].T
    for block in range(columns // BLOCK):
        run = slice(block * BLOCK, (block + 1) * BLOCK)
        weight[:, run] = (levels[:, run] * factors[:, block : block + 1]).astype(weight.dtype)
    part = quarter.shape[0]
    quarter[...] = weight[pl.ds(pl.multiple_of(where[1] * part, part), part), :]


def weights(where, quant, scales):
    rows, columns = quant.shape
    vmem = pl.BlockSpec(memory_space=pltpu.VMEM)
    return pl.pallas_call(
        weight_kernel,
        out_shape=[
            jax.ShapeDtypeStruct((rows, columns), jnp.bfloat16),
            jax.ShapeDtypeStruct((rows // NX, columns), jnp.bfloat16),
        ],
        in_specs=[pl.BlockSpec(memory_space=pltpu.SMEM), vmem, vmem],
        out_specs=[vmem, vmem],
        compiler_params=pltpu.CompilerParams(vmem_limit_bytes=58 * MIB),
        cost_estimate=pl.CostEstimate(
            flops=rows * columns, bytes_accessed=4 * rows * columns, transcendentals=0
        ),
        name="weights",
    )(where, quant, scales.T)


def partial_kernel(factor, where, acts, acts_in, grads, grads_in, out, lhs, rhs):
    step = pl.program_id(0)
    tokens = acts.shape[0]
    _, blocks, rows, _ = out.shape
    span = rows * NX

    @pl.when(step == 0)
    def _():
        rhs[:tokens] = grads[...]
        rhs[tokens:] = grads_in[...]

    for t in range(blocks):
        j = step * blocks + t
        block = (j % NZH) * NY + j // NZH
        start = pl.multiple_of((block * NC + where[0]) * span, span)
        lhs[:tokens, t * span : (t + 1) * span] = acts[:, pl.ds(start, span)]
        lhs[tokens:, t * span : (t + 1) * span] = acts_in[:, pl.ds(start, span)]
    value = lax.dot_general(
        lhs[...], rhs[...], (((0,), (0,)), ((), ())), preferred_element_type=jnp.float32
    )
    value = (value * factor).astype(out.dtype)
    for t in range(blocks):
        for x in range(NX):
            start = t * span + x * rows
            out[x, t] = value[start : start + rows]


def partials(where, acts, acts_in, grads, grads_in, factor):
    tokens, width = acts.shape
    columns = grads.shape[1]
    blocks = NZH * NY
    span = width // (blocks * NC)
    rows = span // NX
    half = blocks // 2
    vmem = pl.BlockSpec(memory_space=pltpu.VMEM)
    return pl.pallas_call(
        functools.partial(partial_kernel, factor),
        out_shape=jax.ShapeDtypeStruct((NX, blocks, rows, columns), jnp.bfloat16),
        grid_spec=pltpu.PrefetchScalarGridSpec(
            num_scalar_prefetch=1,
            grid=(2,),
            in_specs=[vmem] * 4,
            out_specs=pl.BlockSpec((NX, half, rows, columns), lambda j, where: (0, j, 0, 0)),
            scratch_shapes=[
                pltpu.VMEM((2 * tokens, half * span), jnp.bfloat16),
                pltpu.VMEM((2 * tokens, columns), jnp.bfloat16),
            ],
        ),
        compiler_params=pltpu.CompilerParams(vmem_limit_bytes=58 * MIB),
        cost_estimate=pl.CostEstimate(
            flops=4 * tokens * columns * span * blocks,
            bytes_accessed=2 * blocks * span * columns + 4 * tokens * width,
            transcendentals=0,
        ),
        name="partials",
    )(where, acts, acts_in, grads, grads_in)


def sum_kernel(parts, out):
    total = parts[0].astype(jnp.float32)
    for k in range(1, parts.shape[0]):
        total = total + parts[k].astype(jnp.float32)
    out[...] = total.astype(out.dtype)


def sums(parts):
    count, rows, columns = parts.shape
    each = min(rows, 128)
    return pl.pallas_call(
        sum_kernel,
        out_shape=jax.ShapeDtypeStruct((rows, columns), parts.dtype),
        grid=(rows // each,),
        in_specs=[pl.BlockSpec((count, each, columns), lambda k: (0, k, 0))],
        out_specs=pl.BlockSpec((each, columns), lambda k: (k, 0)),
        compiler_params=pltpu.CompilerParams(vmem_limit_bytes=16 * MIB),
        cost_estimate=pl.CostEstimate(
            flops=2 * 10**10, bytes_accessed=2 * count * rows * columns, transcendentals=0
        ),
        name="sums",
    )(parts)


def input_kernel(where, grads, weight, *rest):
    out = rest[-1]
    pieces, groups, rows, columns = weight.shape
    span = pieces * rows
    for group in range(groups):
        block = weight[:, group].reshape(span, columns)
        out[:, group * span : (group + 1) * span] = lax.dot_general(
            grads[...], block, (((1,), (1,)), ((), ())), preferred_element_type=jnp.float32
        ).astype(out.dtype)


def input_half(where, grads, weight, width, before=None):
    tokens, columns = grads.shape
    pieces, groups, rows, _ = weight.shape
    steps = 4
    each = groups // steps
    block = each * pieces * rows
    in_specs = [
        pl.BlockSpec((tokens, columns), lambda j, where: (0, 0)),
        pl.BlockSpec((pieces, each, rows, columns), lambda j, where: (0, j, 0, 0)),
    ]
    args = [where, grads, weight]
    aliases = {}
    if before is not None:
        in_specs.append(pl.BlockSpec(memory_space=pl.ANY))
        args.append(before)
        aliases = {3: 0}
    return pl.pallas_call(
        input_kernel,
        out_shape=jax.ShapeDtypeStruct((tokens, width), jnp.bfloat16),
        grid_spec=pltpu.PrefetchScalarGridSpec(
            num_scalar_prefetch=1,
            grid=(steps,),
            in_specs=in_specs,
            out_specs=pl.BlockSpec((tokens, block), lambda j, where: (0, where[0] * steps + j)),
        ),
        input_output_aliases=aliases,
        compiler_params=pltpu.CompilerParams(vmem_limit_bytes=58 * MIB),
        cost_estimate=pl.CostEstimate(
            flops=2 * tokens * columns * pieces * groups * rows,
            bytes_accessed=2 * pieces * groups * rows * columns + 4 * tokens * columns,
            transcendentals=0,
        ),
        name="input_half",
    )(*args)


def shards(acts, grads_out, quant, scales):
    tokens, width = acts.shape
    columns = grads_out.shape[1]
    shard_rows = quant.shape[0]
    total_tokens = tokens * lax.axis_size(AXES)
    x, zh, c = (lax.axis_index(name) for name in ("x", "zh", "c"))
    where = jnp.stack([c, x]).astype(jnp.int32)
    groups = NY * NC

    acts_in = shift(acts, "c", 1)
    grads_in = shift(grads_out, "c", 1)
    weight, quarter = weights(where, quant, scales)
    own_half = lax.all_gather(weight, ("y", "c"), axis=0, tiled=True)

    parts = partials(where, acts, acts_in, grads_out, grads_in, 1.0 / math.sqrt(total_tokens))
    received = lax.all_to_all(parts, "x", split_axis=0, concat_axis=0, tiled=True)
    quarter = chip_shift(quarter, lambda i, z: (i, (z + NZL) % NZ))
    other_half = lax.all_gather(quarter, ("x", "y", "c"), axis=0, tiled=True)
    own_half = own_half.reshape(1, groups, shard_rows, columns)
    grad_input = input_half(zh[None].astype(jnp.int32), grads_out, own_half, width)
    grad_input, received = lax.optimization_barrier((grad_input, received))
    chunk = NZH * NZL * 8
    summed = sums(received.reshape(NX, NY * chunk, columns)).reshape(NY, chunk, columns)
    received = lax.all_to_all(summed, "y", split_axis=0, concat_axis=0, tiled=True)
    rows = sums(received).reshape(NZ, 8, columns)
    rows = lax.all_to_all(rows, ("zh", "zl"), split_axis=0, concat_axis=0, tiled=True)
    other_half = other_half.reshape(NX, groups, shard_rows // NX, columns)
    grad_input = input_half(
        (1 - zh)[None].astype(jnp.int32), grads_out, other_half, width, grad_input
    )
    grad_input, rows = lax.optimization_barrier((grad_input, rows))
    weight_grad = jnp.sum(rows, axis=0, dtype=jnp.float32)
    return (grad_input, weight_grad)


def solution(mesh):
    fine = Mesh(mesh.devices.reshape(NX, NZL, NZH, NY, NC), AXES)
    tokens = P(AXES, None)
    rows = P(("zh", "y", "c"), None)
    return jax.shard_map(
        shards,
        mesh=fine,
        in_specs=(tokens, tokens, rows, rows),
        out_specs=(tokens, P(("zh", "y", "c", "x", "zl"), None)),
        check_vma=False,
    )
```

time: 162 us -> 144 us (0.89)
  the two profiles are of different devices: /device:TPU:24 before, /device:TPU:32 now
where the time goes in v4:
time: 144 us; the launch traced here: 143 us
  waiting for transfers between devices  43.2 us (30%)
  starting transfers between devices  40 us (28%)
  Pallas kernels  23.3 us (16%)
  blocking collectives  18.9 us (13%)
  between operations  14.1 us (10%)
  local copies, waits for them, and re-layouts  2.68 us (2%)
    all_to_all x1, blocking collectives, shards(): lax.all_to_all(summed, 'y', split_axis=0, concat_axis=0, tiled=True)  18.9 us
    all_to_all x1, waiting for transfers between devices, shards(): lax.all_to_all(parts, 'x', split_axis=0, concat_axis=0, tiled=True)  16.4 us
    all_to_all x1, starting transfers between devices, shards(): lax.all_to_all(rows, ('zh', 'zl'), split_axis=0, concat_axis=0, tiled=True)  15.7 us
    ppermute x1, starting transfers between devices, chip_shift(): return lax.ppermute(value, AXES, pairs)  14.9 us
    ppermute x1, waiting for transfers between devices, chip_shift(): return lax.ppermute(value, AXES, pairs)  12.4 us
    pallas_call x2, Pallas kernels, input_half(): pl.pallas_call(input_kernel, out_shape=jax.ShapeDtypeStruct((tokens, widt...  9.98 us
    all_to_all x1, waiting for transfers between devices, shards(): lax.all_to_all(rows, ('zh', 'zl'), split_axis=0, concat_axis=0, tiled=True)  8.8 us
    pallas_call x1, Pallas kernels, partials(): pl.pallas_call(functools.partial(partial_kernel, factor), out_shape=jax.S...  6.96 us
  transfers between devices with their start and end apart: 7, of which 5 were waited for; matrix products, arithmetic and copies ran while one was open for 0% of the time, Pallas kernels for 15%

profile of v4, /device:TPU:32, one launch (start us, length us, event | category | flops | bytes accessed | tf_op | source)
XLA Modules:
  0.0 143.5 jit_solution(12186187618874908939)
XLA Ops:
  7.2 0.0 all-gather.5.cloned.1.call-start
  7.2 0.7 pad_add_fusion.where
  7.9 2.4 %weights.1 = (bf16[256,1024]{1,0:T(8,128)(2,1)}, bf16[64,1024]{1,0:T(8,128)(2,1)}) custom-call(s32[2]{0:T(128)} %pad_add_fusion.where, bf16[256,1024]{1,0:T(8,128)(2,1)} %quant.1, f32[8,256]{1,0:T(8,128)} %bitcast.13), custom_call_target="tpu_custom_call" | custom-call | flops 262144 | bytes 1048576 | tf_op jit(solution)/shard_map/weights/pallas_call | solution.py:52
  10.3 1.9 %collective-permute-start.1 = (bf16[224,4096]{1,0:T(8,128)(2,1)}, bf16[224,4096]{1,0:T(8,128)(2,1)S(1)}, u32[]{:S(2)}, u32[]{:S(2)}) collective-permute-start(bf16[224,4096]{1,0:T(8,128)(2,1)} %acts.1), channel_id=1, source_target_pairs={{0,1},{1,0},{2,3},{3,2},{4,5},{5,4},{6,7},{7,6},{8,9},{9,8},{10,11... | collective-permute-start | bytes 5505032 | tf_op jit(solution)/shard_map/ppermute | solution.py:21
  12.2 2.4 %collective-permute-start.2 = (bf16[224,1024]{1,0:T(8,128)(2,1)}, bf16[224,1024]{1,0:T(8,128)(2,1)S(1)}, u32[]{:S(2)}, u32[]{:S(2)}) collective-permute-start(bf16[224,1024]{1,0:T(8,128)(2,1)} %grads.5), channel_id=1, source_target_pairs={{0,1},{1,0},{2,3},{3,2},{4,5},{5,4},{6,7},{7,6},{8,9},{9,8},{10,11... | collective-permute-start | bytes 1376264 | tf_op jit(solution)/shard_map/ppermute | solution.py:21
  14.7 2.2 %collective-permute-done.2.grads_in = bf16[224,1024]{1,0:T(8,128)(2,1)S(1)} collective-permute-done((bf16[224,1024]{1,0:T(8,128)(2,1)}, bf16[224,1024]{1,0:T(8,128)(2,1)S(1)}, u32[]{:S(2)}, u32[]{:S(2)}) %collective-permute-start.2) | collective-permute-done | bytes 458784 | tf_op jit(solution)/shard_map/ppermute | solution.py:21
  16.9 0.8 copy-done.1
  17.7 1.2 copy-done
  18.9 7.0 %partials.1 = bf16[4,8,64,1024]{3,2,1,0:T(8,128)(2,1)} custom-call(s32[2]{0:T(128)} %pad_add_fusion.where, bf16[224,4096]{1,0:T(8,128)(2,1)} %acts.1, bf16[224,4096]{1,0:T(8,128)(2,1)} %copy-done, bf16[224,1024]{1,0:T(8,128)(2,1)} %grads.5, bf16[224,1024]{1,0:T(8,128)(2,1)} %copy-done.1), custom_call_target="tpu_custom_call" | custom-call | flops 1879048192 | bytes 7864320 | tf_op jit(solution)/shard_map/partials/pallas_call | solution.py:103
  25.8 5.1 %all-to-all-start = ((bf16[4,8,64,1024]{3,2,1,0:T(8,128)(2,1)}), bf16[4,8,64,1024]{3,2,1,0:T(8,128)(2,1)}, u32[]{:S(2)}, u32[]{:S(2)}) async-start(bf16[4,8,64,1024]{3,2,1,0:T(8,128)(2,1)} %partials.1), calls=%async_computation | async-start | bytes 8388608 | tf_op jit(solution)/shard_map/all_to_all | solution.py:212
  30.9 0.0 all-gather.3.cloned.1.call-start
  31.0 14.9 %collective-permute-start = (bf16[64,1024]{1,0:T(8,128)(2,1)S(1)}, bf16[64,1024]{1,0:T(8,128)(2,1)S(1)}, u32[]{:S(2)}, u32[]{:S(2)}) collective-permute-start(bf16[64,1024]{1,0:T(8,128)(2,1)S(1)} %copy-done.3), channel_id=1, source_target_pairs={{0,8},{1,9},{2,10},{3,11},{4,12},{5,13},{6,14},{7,15},{16,24},{17,... | collective-permute-start | bytes 393224 | tf_op jit(solution)/shard_map/ppermute | solution.py:35
  45.9 12.4 %collective-permute-done = bf16[64,1024]{1,0:T(8,128)(2,1)S(1)} collective-permute-done((bf16[64,1024]{1,0:T(8,128)(2,1)S(1)}, bf16[64,1024]{1,0:T(8,128)(2,1)S(1)}, u32[]{:S(2)}, u32[]{:S(2)}) %collective-permute-start) | collective-permute-done | bytes 131104 | tf_op jit(solution)/shard_map/ppermute | solution.py:35
  58.2 0.6 copy-done.2
  59.0 5.0 %input_half.2.rest_0_ = bf16[224,4096]{1,0:T(8,128)(2,1)} custom-call(s32[1]{0:T(128)} %bitcast.5.where, bf16[224,1024]{1,0:T(8,128)(2,1)} %grads.5, bf16[1,8,256,1024]{3,2,1,0:T(8,128)(2,1)} %bitcast.11), custom_call_target="tpu_custom_call" | custom-call | flops 939524096 | bytes 5111808 | tf_op jit(solution)/shard_map/input_half/pallas_call | solution.py:177
  64.0 16.4 %all-to-all-done = bf16[4,8,64,1024]{3,2,1,0:T(8,128)(2,1)} async-done(((bf16[4,8,64,1024]{3,2,1,0:T(8,128)(2,1)}), bf16[4,8,64,1024]{3,2,1,0:T(8,128)(2,1)}, u32[]{:S(2)}, u32[]{:S(2)}) %all-to-all-start) | async-done | bytes 4194336 | tf_op jit(solution)/shard_map/all_to_all | solution.py:212
  80.4 3.1 %sums.2 = bf16[512,1024]{1,0:T(8,128)(2,1)S(1)} custom-call(bf16[4,512,1024]{2,1,0:T(8,128)(2,1)} %bitcast.7.parts), custom_call_target="tpu_custom_call" | custom-call | flops 20000000000 | bytes 4194304 | tf_op jit(solution)/shard_map/sums/pallas_call | solution.py:136
  83.5 18.9 %all_to_all.15.parts = bf16[4,128,1024]{2,1,0:T(8,128)(2,1)S(1)} all-to-all(bf16[4,128,1024]{2,1,0:T(8,128)(2,1)S(1)} %bitcast.10), channel_id=1, replica_groups=mesh['x'=4,'zl'=8,'zh'=2,'y'=4,'c'=2] {'y'}, dimensions={0} | all-to-all | bytes 2097152 | tf_op jit(solution)/shard_map/all_to_all | solution.py:220
  102.4 0.8 sums.3
  103.2 15.7 %all-to-all-start.2 = ((bf16[16,8,1024]{2,1,0:T(8,128)(2,1)}), bf16[16,8,1024]{2,1,0:T(8,128)(2,1)S(1)}, u32[]{:S(2)}, u32[]{:S(2)}) async-start(bf16[16,8,1024]{2,1,0:T(8,128)(2,1)} %bitcast.9), calls=%async_computation.2 | async-start | bytes 524288 | tf_op jit(solution)/shard_map/all_to_all | solution.py:222
  118.9 3.3 %all-gather.3.cloned.1.call-done = bf16[2048,1024]{1,0:T(8,128)(2,1)} async-done(((bf16[64,1024]{1,0:T(8,128)(2,1)}), bf16[2048,1024]{1,0:T(8,128)(2,1)}) %all-gather.3.cloned.1.call-update) | async-done | bytes 4194320 | tf_op jit(solution)/shard_map/all_gather | solution.py:214
  122.2 5.0 %input_half.3 = bf16[224,4096]{1,0:T(8,128)(2,1)} custom-call(s32[1]{0:T(128)} %bitcast.where, bf16[224,1024]{1,0:T(8,128)(2,1)} %grads.5, bf16[4,8,64,1024]{3,2,1,0:T(8,128)(2,1)} %bitcast.12, bf16[224,4096]{1,0:T(8,128)(2,1)} %input_half.2.rest_0_), custom_call_target="tpu_custom_call", output_to_operand_aliasing={{}: (3, {})} | custom-call | flops 939524096 | bytes 5111808 | tf_op jit(solution)/shard_map/input_half/pallas_call | solution.py:177
  127.2 8.8 %all-to-all-done.2 = bf16[16,8,1024]{2,1,0:T(8,128)(2,1)S(1)} async-done(((bf16[16,8,1024]{2,1,0:T(8,128)(2,1)}), bf16[16,8,1024]{2,1,0:T(8,128)(2,1)S(1)}, u32[]{:S(2)}, u32[]{:S(2)}) %all-to-all-start.2) | async-done | bytes 262176 | tf_op jit(solution)/shard_map/all_to_all | solution.py:222
  136.0 0.7 convert_reduce_fusion
  (9 shorter events, 0.1 us)
Async XLA Ops:
  7.2 51.8 %all-gather.5.cloned.1.call-start = ((), (), s32[]{:S(2)}) async-start(), calls=%async_computation.4 | async-start | bytes 4718592 | tf_op jit(solution)/shard_map/all_gather | solution.py:209
  10.3 6.6 %collective-permute-start.1 = (bf16[224,4096]{1,0:T(8,128)(2,1)}, bf16[224,4096]{1,0:T(8,128)(2,1)S(1)}, u32[]{:S(2)}, u32[]{:S(2)}) collective-permute-start(bf16[224,4096]{1,0:T(8,128)(2,1)} %acts.1), channel_id=1, source_target_pairs={{0,1},{1,0},{2,3},{3,2},{4,5},{5,4},{6,7},{7,6},{8,9},{9,8},{10,11... | collective-permute-start | bytes 5505032 | tf_op jit(solution)/shard_map/ppermute | solution.py:21
  12.2 4.6 %collective-permute-start.2 = (bf16[224,1024]{1,0:T(8,128)(2,1)}, bf16[224,1024]{1,0:T(8,128)(2,1)S(1)}, u32[]{:S(2)}, u32[]{:S(2)}) collective-permute-start(bf16[224,1024]{1,0:T(8,128)(2,1)} %grads.5), channel_id=1, source_target_pairs={{0,1},{1,0},{2,3},{3,2},{4,5},{5,4},{6,7},{7,6},{8,9},{9,8},{10,11... | collective-permute-start | bytes 1376264 | tf_op jit(solution)/shard_map/ppermute | solution.py:21
  16.9 0.8 copy-start.1
  17.7 1.2 copy-start
  25.8 5.1 %copy-start.3 = (bf16[64,1024]{1,0:T(8,128)(2,1)S(1)}, bf16[64,1024]{1,0:T(8,128)(2,1)}, u32[]{:S(2)}) copy-start(bf16[64,1024]{1,0:T(8,128)(2,1)} %get-tuple-element.8) | copy-start | bytes 393220
  25.8 54.5 %all-to-all-start = ((bf16[4,8,64,1024]{3,2,1,0:T(8,128)(2,1)}), bf16[4,8,64,1024]{3,2,1,0:T(8,128)(2,1)}, u32[]{:S(2)}, u32[]{:S(2)}) async-start(bf16[4,8,64,1024]{3,2,1,0:T(8,128)(2,1)} %partials.1), calls=%async_computation | async-start | bytes 8388608 | tf_op jit(solution)/shard_map/all_to_all | solution.py:212
  30.9 91.3 %all-gather.3.cloned.1.call-start = ((), (), s32[]{:S(2)}) async-start(), calls=%async_computation.3 | async-start | bytes 4325376 | tf_op jit(solution)/shard_map/all_gather | solution.py:214
  31.0 27.3 %collective-permute-start = (bf16[64,1024]{1,0:T(8,128)(2,1)S(1)}, bf16[64,1024]{1,0:T(8,128)(2,1)S(1)}, u32[]{:S(2)}, u32[]{:S(2)}) collective-permute-start(bf16[64,1024]{1,0:T(8,128)(2,1)S(1)} %copy-done.3), channel_id=1, source_target_pairs={{0,8},{1,9},{2,10},{3,11},{4,12},{5,13},{6,14},{7,15},{16,24},{17,... | collective-permute-start | bytes 393224 | tf_op jit(solution)/shard_map/ppermute | solution.py:35
  58.2 0.7 copy-start.2
  103.2 32.8 %all-to-all-start.2 = ((bf16[16,8,1024]{2,1,0:T(8,128)(2,1)}), bf16[16,8,1024]{2,1,0:T(8,128)(2,1)S(1)}, u32[]{:S(2)}, u32[]{:S(2)}) async-start(bf16[16,8,1024]{2,1,0:T(8,128)(2,1)} %bitcast.9), calls=%async_computation.2 | async-start | bytes 524288 | tf_op jit(solution)/shard_map/all_to_all | solution.py:222
Sparse Core Ops, SparseCore 0:
  10.4 43.9 all-gather.4
  59.0 63.0 all-gather.2

commit v5 on v4

v5 whole, which is shorter than its diff:
```python
import functools
import math

import jax
import jax.numpy as jnp
from jax import lax
from jax.experimental import pallas as pl
from jax.experimental.pallas import tpu as pltpu
from jax.sharding import Mesh
from jax.sharding import PartitionSpec as P

BLOCK = 128
NX, NZL, NZH, NY, NC = 4, 8, 2, 4, 2
NZ = NZL * NZH
AXES = ("x", "zl", "zh", "y", "c")
MIB = 1024 * 1024


def shift(value, axis, step):
    size = lax.axis_size(axis)
    return lax.ppermute(value, axis, [(i, (i + step) % size) for i in range(size)])


def chip_shift(value, move):
    def index(x, z, y, c):
        return (((x * NZL + z % NZL) * NZH + z // NZL) * NY + y) * NC + c

    pairs = []
    for x in range(NX):
        for z in range(NZ):
            to_x, to_z = move(x, z)
            for y in range(NY):
                for c in range(NC):
                    pairs.append((index(x, z, y, c), index(to_x, to_z, y, c)))
    return lax.ppermute(value, AXES, pairs)


def weight_kernel(odd, quant, scales, weight, half):
    rows, columns = quant.shape
    levels = quant[...].astype(jnp.float32)
    factors = scales[...].T
    for block in range(columns // BLOCK):
        run = slice(block * BLOCK, (block + 1) * BLOCK)
        weight[:, run] = (levels[:, run] * factors[:, block : block + 1]).astype(weight.dtype)
    part = half.shape[0]
    half[...] = weight[pl.ds(pl.multiple_of(odd[0] * part, part), part), :]


def weights(odd, quant, scales):
    rows, columns = quant.shape
    vmem = pl.BlockSpec(memory_space=pltpu.VMEM)
    quant, scales = (
        pltpu.with_memory_space_constraint(v, pltpu.HBM) for v in (quant, scales.T)
    )
    return pl.pallas_call(
        weight_kernel,
        out_shape=[
            jax.ShapeDtypeStruct((rows, columns), jnp.bfloat16),
            jax.ShapeDtypeStruct((rows // 2, columns), jnp.bfloat16),
        ],
        in_specs=[pl.BlockSpec(memory_space=pltpu.SMEM), vmem, vmem],
        out_specs=[vmem, vmem],
        compiler_params=pltpu.CompilerParams(vmem_limit_bytes=8 * MIB),
        cost_estimate=pl.CostEstimate(
            flops=rows * columns, bytes_accessed=4 * rows * columns, transcendentals=0
        ),
        name="weights",
    )(odd, quant, scales)


def partial_kernel(factor, core, acts, acts_in, grads, grads_in, out, lhs, rhs, sems):
    step = pl.program_id(0)
    tokens = acts.shape[0]
    _, blocks, rows, _ = out.shape
    span = rows * NX

    def copies(at):
        found = []
        for t in range(blocks):
            j = at * blocks + t
            block = (j % NZH) * NY + j // NZH
            start = pl.multiple_of((block * NC + core[0]) * span, span)
            for half, source in enumerate((acts, acts_in)):
                found.append(
                    pltpu.make_async_copy(
                        source.at[:, pl.ds(start, span)],
                        lhs.at[at, pl.ds(half * tokens, tokens), pl.ds(t * span, span)],
                        sems.at[2 * j + half],
                    )
                )
        return found

    base = 4 * blocks
    right = [
        pltpu.make_async_copy(
            source, rhs.at[pl.ds(half * tokens, tokens)], sems.at[base + half]
        )
        for half, source in enumerate((grads, grads_in))
    ]

    @pl.when(step == 0)
    def _():
        for copy in right + copies(0) + copies(1):
            copy.start()
        for copy in right + copies(0):
            copy.wait()

    @pl.when(step == 1)
    def _():
        for copy in copies(1):
            copy.wait()

    value = lax.dot_general(
        lhs[step], rhs[...], (((0,), (0,)), ((), ())), preferred_element_type=jnp.float32
    )
    value = (value * factor).astype(out.dtype)
    for t in range(blocks):
        for x in range(NX):
            start = t * span + x * rows
            out[x, t] = value[start : start + rows]


def partials(core, acts, acts_in, grads, grads_in, factor):
    tokens, width = acts.shape
    columns = grads.shape[1]
    blocks = NZH * NY
    span = width // (blocks * NC)
    rows = span // NX
    half = blocks // 2
    acts, grads = (pltpu.with_memory_space_constraint(v, pltpu.HBM) for v in (acts, grads))
    return pl.pallas_call(
        functools.partial(partial_kernel, factor),
        out_shape=pltpu.HBM((NX, blocks, rows, columns), jnp.bfloat16),
        grid_spec=pltpu.PrefetchScalarGridSpec(
            num_scalar_prefetch=1,
            grid=(2,),
            in_specs=[pl.BlockSpec(memory_space=pl.ANY)] * 4,
            out_specs=pl.BlockSpec((NX, half, rows, columns), lambda j, core: (0, j, 0, 0)),
            scratch_shapes=[
                pltpu.VMEM((2, 2 * tokens, half * span), jnp.bfloat16),
                pltpu.VMEM((2 * tokens, columns), jnp.bfloat16),
                pltpu.SemaphoreType.DMA((2 * blocks + 2,)),
            ],
        ),
        compiler_params=pltpu.CompilerParams(vmem_limit_bytes=24 * MIB),
        cost_estimate=pl.CostEstimate(
            flops=4 * tokens * columns * span * blocks,
            bytes_accessed=2 * blocks * span * columns + 4 * tokens * width,
            transcendentals=0,
        ),
        name="partials",
    )(core, acts, acts_in, grads, grads_in)


def sum_kernel(parts, out, held, sems):
    count = parts.shape[0]
    pieces, _, rows, _ = held.shape
    copies = [
        pltpu.make_async_copy(parts.at[:, pl.ds(q * rows, rows)], held.at[q], sems.at[q])
        for q in range(pieces)
    ]
    for copy in copies:
        copy.start()
    for q, copy in enumerate(copies):
        copy.wait()
        total = held[q, 0].astype(jnp.float32)
        for k in range(1, count):
            total = total + held[q, k].astype(jnp.float32)
        out[q * rows : (q + 1) * rows] = total.astype(out.dtype)


def sums(parts):
    count, rows, columns = parts.shape
    each = min(rows, 64)
    pieces = rows // each
    return pl.pallas_call(
        sum_kernel,
        out_shape=jax.ShapeDtypeStruct((rows, columns), parts.dtype),
        in_specs=[pl.BlockSpec(memory_space=pl.ANY)],
        out_specs=pl.BlockSpec(memory_space=pltpu.VMEM),
        scratch_shapes=[
            pltpu.VMEM((pieces, count, each, columns), parts.dtype),
            pltpu.SemaphoreType.DMA((pieces,)),
        ],
        compiler_params=pltpu.CompilerParams(vmem_limit_bytes=16 * MIB),
        cost_estimate=pl.CostEstimate(
            flops=2 * 10**10, bytes_accessed=2 * count * rows * columns, transcendentals=0
        ),
        name="sums",
    )(parts)


def input_kernel(where, grads, weight, *rest):
    out, held, lhs, result, in_sems, out_sems = rest[-6:]
    groups, pieces, rows, _ = weight.shape
    span = pieces * rows
    width = groups * span
    first = pltpu.make_async_copy(grads, lhs, in_sems.at[groups])
    first.start()
    copies = [
        pltpu.make_async_copy(weight.at[group], held.at[group], in_sems.at[group])
        for group in range(groups)
    ]
    for copy in copies:
        copy.start()
    first.wait()
    done = []
    for group, copy in enumerate(copies):
        copy.wait()
        for piece in range(pieces):
            start = group * span + piece * rows
            block = held[group, lax.rem(piece + where[1], pieces)]
            result[:, start : start + rows] = lax.dot_general(
                lhs[...], block, (((1,), (1,)), ((), ())), preferred_element_type=jnp.float32
            ).astype(result.dtype)
        start = pl.multiple_of(where[0] * width + group * span, span)
        done.append(
            pltpu.make_async_copy(
                result.at[:, pl.ds(group * span, span)],
                out.at[:, pl.ds(start, span)],
                out_sems.at[group],
            )
        )
        done[-1].start()
    for copy in done:
        copy.wait()


def input_half(where, grads, weight, width, before=None):
    tokens, columns = grads.shape
    groups, pieces, rows, _ = weight.shape
    weight = pltpu.with_memory_space_constraint(weight, pltpu.HBM)
    args = [where, grads, weight]
    aliases = {}
    if before is not None:
        args.append(before)
        aliases = {3: 0}
    anywhere = pl.BlockSpec(memory_space=pl.ANY)
    return pl.pallas_call(
        input_kernel,
        out_shape=jax.ShapeDtypeStruct((tokens, width), jnp.bfloat16),
        in_specs=[pl.BlockSpec(memory_space=pltpu.SMEM)] + [anywhere] * (len(args) - 1),
        out_specs=anywhere,
        scratch_shapes=[
            pltpu.VMEM((groups, pieces, rows, columns), jnp.bfloat16),
            pltpu.VMEM((tokens, columns), jnp.bfloat16),
            pltpu.VMEM((tokens, groups * pieces * rows), jnp.bfloat16),
            pltpu.SemaphoreType.DMA((groups + 1,)),
            pltpu.SemaphoreType.DMA((groups,)),
        ],
        input_output_aliases=aliases,
        compiler_params=pltpu.CompilerParams(vmem_limit_bytes=16 * MIB),
        cost_estimate=pl.CostEstimate(
            flops=2 * tokens * columns * pieces * groups * rows,
            bytes_accessed=2 * pieces * groups * rows * columns + 4 * tokens * columns,
            transcendentals=0,
        ),
        name="input_half",
    )(*args)


def shards(acts, grads_out, quant, scales):
    tokens, width = acts.shape
    columns = grads_out.shape[1]
    shard_rows = quant.shape[0]
    total_tokens = tokens * lax.axis_size(AXES)
    zl, zh, c = (lax.axis_index(name) for name in ("zl", "zh", "c"))
    odd = zl % 2
    groups = NY * NC

    acts_in = shift(acts, "c", 1)
    grads_in = shift(grads_out, "c", 1)
    weight, piece = weights(odd[None].astype(jnp.int32), quant, scales)
    own_half = lax.all_gather(weight, ("y", "c"), axis=0, tiled=True)
    factor = 1.0 / math.sqrt(total_tokens)
    parts = partials(c[None].astype(jnp.int32), acts, acts_in, grads_out, grads_in, factor)
    received = lax.all_to_all(parts, "x", split_axis=0, concat_axis=0, tiled=True)
    first = chip_shift(piece, lambda i, z: (i, (z + NZL) % NZ))
    second = chip_shift(first, lambda i, z: (i, z ^ 1))
    other_half = lax.all_gather(
        jnp.concatenate([first, second], axis=0), ("y", "c"), axis=0, tiled=True
    )
    chunk = NZH * NZL * 8
    summed = sums(received.reshape(NX, NY * chunk, columns)).reshape(NY, chunk, columns)
    grads_later, summed = lax.optimization_barrier((grads_out, summed))
    received = lax.all_to_all(summed, "y", split_axis=0, concat_axis=0, tiled=True)
    own_half = own_half.reshape(groups, 1, shard_rows, columns)
    place = jnp.stack([zh, 0 * odd]).astype(jnp.int32)
    grad_input = input_half(place, grads_later, own_half, width)
    grad_input, received = lax.optimization_barrier((grad_input, received))
    rows = sums(received).reshape(NZ, 8, columns)
    rows = lax.all_to_all(rows, ("zh", "zl"), split_axis=0, concat_axis=0, tiled=True)
    other_half = other_half.reshape(groups, 2, shard_rows // 2, columns)
    place = jnp.stack([1 - zh, odd]).astype(jnp.int32)
    grad_input = input_half(place, grads_later, other_half, width, grad_input)
    grad_input, rows = lax.optimization_barrier((grad_input, rows))
    weight_grad = jnp.sum(rows, axis=0, dtype=jnp.float32)
    return (grad_input, weight_grad)


def solution(mesh):
    fine = Mesh(mesh.devices.reshape(NX, NZL, NZH, NY, NC), AXES)
    tokens = P(AXES, None)
    rows = P(("zh", "y", "c"), None)
    return jax.shard_map(
        shards,
        mesh=fine,
        in_specs=(tokens, tokens, rows, rows),
        out_specs=(tokens, P(("zh", "y", "c", "x", "zl"), None)),
        check_vma=False,
    )
```

time: 144 us -> 142 us (0.986)
  blocking collectives: 18.9 us -> 0 us
  starting transfers between devices: 40 us -> 49.8 us
  waiting for transfers between devices: 43.2 us -> 51.8 us
  local copies, waits for them, and re-layouts: 2.68 us -> 0.01 us
    ppermute x1 -> x2, waiting for transfers between devices: 12.4 us -> 31.3 us  [chip_shift(): return lax.ppermute(value, AXES, pairs)]
    all_to_all x1 -> x0, blocking collectives: 18.9 us -> none  [shards(): lax.all_to_all(summed, 'y', split_axis=0, concat_axis=0, tiled=True)]
    all_to_all x1, waiting for transfers between devices: 16.4 us -> 0.52 us  [shards(): lax.all_to_all(parts, 'x', split_axis=0, concat_axis=0, tiled=True)]
    all_to_all x0 -> x1, waiting for transfers between devices: none -> 9.18 us  [shards(): lax.all_to_all(summed, 'y', split_axis=0, concat_axis=0, tiled=True)]
    all_to_all x0 -> x1, starting transfers between devices: none -> 4.47 us  [shards(): lax.all_to_all(summed, 'y', split_axis=0, concat_axis=0, tiled=True)]
    all_to_all x1, starting transfers between devices: 15.7 us -> 19.2 us  [shards(): lax.all_to_all(rows, ('zh', 'zl'), split_axis=0, concat_axis=0, tiled=True)]
    all_gather x1, waiting for transfers between devices: 3.33 us -> 0.01 us  [shards(): lax.all_gather(jnp.concatenate([first, second], axis=0), ('y', 'c'), axis...]
    unnamed x8 -> x2, local copies, waits for them, and re-layouts: 2.68 us -> 0.01 us
  transfers between devices with their start and end apart: 7 -> 9, of which waited for: 5 -> 6; matrix products, arithmetic and copies ran while one was open for 0% -> 1% of each run, Pallas kernels for 15% -> 15%
where the time goes in v5:
time: 142 us
  waiting for transfers between devices  51.8 us (36%)
  starting transfers between devices  49.8 us (35%)
  Pallas kernels  24.3 us (17%)
  between operations  14.1 us (10%)
  other arithmetic  1.63 us (1%)
    ppermute x2, waiting for transfers between devices, chip_shift(): return lax.ppermute(value, AXES, pairs)  31.3 us
    all_to_all x1, starting transfers between devices, shards(): lax.all_to_all(rows, ('zh', 'zl'), split_axis=0, concat_axis=0, tiled=True)  19.2 us
    ppermute x2, starting transfers between devices, chip_shift(): return lax.ppermute(value, AXES, pairs)  16.7 us
    pallas_call x2, Pallas kernels, input_half(): pl.pallas_call(input_kernel, out_shape=jax.ShapeDtypeStruct((tokens, widt...  12.1 us
    all_to_all x1, waiting for transfers between devices, shards(): lax.all_to_all(summed, 'y', split_axis=0, concat_axis=0, tiled=True)  9.18 us
    all_to_all x1, waiting for transfers between devices, shards(): lax.all_to_all(rows, ('zh', 'zl'), split_axis=0, concat_axis=0, tiled=True)  8.63 us
    pallas_call x1, Pallas kernels, partials(): pl.pallas_call(functools.partial(partial_kernel, factor), out_shape=pltpu...  5.51 us
    all_to_all x1, starting transfers between devices, shards(): lax.all_to_all(parts, 'x', split_axis=0, concat_axis=0, tiled=True)  4.94 us
  transfers between devices with their start and end apart: 9, of which 6 were waited for; matrix products, arithmetic and copies ran while one was open for 1% of the time, Pallas kernels for 15%

profile of v5, /device:TPU:32, one launch (start us, length us, event | category | flops | bytes accessed | tf_op | source)
XLA Modules:
  0.0 141.7 jit_solution(12407734522470985657)
XLA Ops:
  7.2 2.4 %weights.1 = (bf16[256,1024]{1,0:T(8,128)(2,1)}, bf16[128,1024]{1,0:T(8,128)(2,1)S(1)}) custom-call(s32[1]{0:T(128)} %bitcast.1.odd, bf16[256,1024]{1,0:T(8,128)(2,1)} %quant.1, f32[8,256]{1,0:T(8,128)} %bitcast.12), custom_call_target="tpu_custom_call" | custom-call | flops 262144 | bytes 1048576 | tf_op jit(solution)/shard_map/weights/pallas_call | solution.py:55
  9.6 1.9 %collective-permute-start = (bf16[224,4096]{1,0:T(8,128)(2,1)}, bf16[224,4096]{1,0:T(8,128)(2,1)S(1)}, u32[]{:S(2)}, u32[]{:S(2)}) collective-permute-start(bf16[224,4096]{1,0:T(8,128)(2,1)} %acts.1), channel_id=1, source_target_pairs={{0,1},{1,0},{2,3},{3,2},{4,5},{5,4},{6,7},{7,6},{8,9},{9,8},{10,11... | collective-permute-start | bytes 5505032 | tf_op jit(solution)/shard_map/ppermute | solution.py:21
  11.5 2.4 %collective-permute-start.1 = (bf16[224,1024]{1,0:T(8,128)(2,1)}, bf16[224,1024]{1,0:T(8,128)(2,1)S(1)}, u32[]{:S(2)}, u32[]{:S(2)}) collective-permute-start(bf16[224,1024]{1,0:T(8,128)(2,1)} %grads.3), channel_id=1, source_target_pairs={{0,1},{1,0},{2,3},{3,2},{4,5},{5,4},{6,7},{7,6},{8,9},{9,8},{10,11... | collective-permute-start | bytes 1376264 | tf_op jit(solution)/shard_map/ppermute | solution.py:21
  13.9 2.2 %collective-permute-done.1.grads_in = bf16[224,1024]{1,0:T(8,128)(2,1)S(1)} collective-permute-done((bf16[224,1024]{1,0:T(8,128)(2,1)}, bf16[224,1024]{1,0:T(8,128)(2,1)S(1)}, u32[]{:S(2)}, u32[]{:S(2)}) %collective-permute-start.1) | collective-permute-done | bytes 458784 | tf_op jit(solution)/shard_map/ppermute | solution.py:21
  16.1 5.5 %partials.1 = bf16[4,8,64,1024]{3,2,1,0:T(8,128)(2,1)} custom-call(s32[1]{0:T(128)} %bitcast.2.core, bf16[224,4096]{1,0:T(8,128)(2,1)} %acts.1, bf16[224,4096]{1,0:T(8,128)(2,1)S(1)} %collective-permute-done.acts_in, bf16[224,1024]{1,0:T(8,128)(2,1)} %grads.3, bf16[224,1024]{1,0:T(8,128)(2,1)S(1)} %collective-permute-done.1.grads_in), custom_call_target="tpu_custom_call" | custom-call | flops 1879048192 | bytes 7864320 | tf_op jit(solution)/shard_map/partials/pallas_call | solution.py:131
  21.7 4.9 %all-to-all-start = ((bf16[4,8,64,1024]{3,2,1,0:T(8,128)(2,1)}), bf16[4,8,64,1024]{3,2,1,0:T(8,128)(2,1)}, u32[]{:S(2)}, u32[]{:S(2)}) async-start(bf16[4,8,64,1024]{3,2,1,0:T(8,128)(2,1)} %partials.1), calls=%async_computation | async-start | bytes 8388608 | tf_op jit(solution)/shard_map/all_to_all | solution.py:277
  26.6 0.0 all-gather.3.cloned.1.call-start
  26.7 14.8 %collective-permute-start.2 = (bf16[128,1024]{1,0:T(8,128)(2,1)S(1)}, bf16[128,1024]{1,0:T(8,128)(2,1)S(1)}, u32[]{:S(2)}, u32[]{:S(2)}) collective-permute-start(bf16[128,1024]{1,0:T(8,128)(2,1)S(1)} %get-tuple-element.11), channel_id=1, source_target_pairs={{0,8},{1,9},{2,10},{3,11},{4,12},{5,13},{6,14},{7,15},{16,24},{17,... | collective-permute-start | bytes 786440 | tf_op jit(solution)/shard_map/ppermute | solution.py:35
  41.5 23.7 %collective-permute-done.2 = bf16[128,1024]{1,0:T(8,128)(2,1)S(1)} collective-permute-done((bf16[128,1024]{1,0:T(8,128)(2,1)S(1)}, bf16[128,1024]{1,0:T(8,128)(2,1)S(1)}, u32[]{:S(2)}, u32[]{:S(2)}) %collective-permute-start.2) | collective-permute-done | bytes 262176 | tf_op jit(solution)/shard_map/ppermute | solution.py:35
  65.2 1.9 %collective-permute-start.3 = (bf16[128,1024]{1,0:T(8,128)(2,1)S(1)}, bf16[128,1024]{1,0:T(8,128)(2,1)S(1)}, u32[]{:S(2)}, u32[]{:S(2)}) collective-permute-start(bf16[128,1024]{1,0:T(8,128)(2,1)S(1)} %collective-permute-done.2), channel_id=1, source_target_pairs={{0,16},{1,17},{2,18},{3,19},{4,20},{5,21},{6,22},{7,23},{16,0},{17... | collective-permute-start | bytes 786440 | tf_op jit(solution)/shard_map/ppermute | solution.py:35
  67.1 7.6 %collective-permute-done.3 = bf16[128,1024]{1,0:T(8,128)(2,1)S(1)} collective-permute-done((bf16[128,1024]{1,0:T(8,128)(2,1)S(1)}, bf16[128,1024]{1,0:T(8,128)(2,1)S(1)}, u32[]{:S(2)}, u32[]{:S(2)}) %collective-permute-start.3) | collective-permute-done | bytes 262176 | tf_op jit(solution)/shard_map/ppermute | solution.py:35
  74.7 0.8 pad_maximum_fusion
  75.5 0.5 all-to-all-done
  76.1 3.4 %sums.2 = bf16[512,1024]{1,0:T(8,128)(2,1)} custom-call(bf16[4,512,1024]{2,1,0:T(8,128)(2,1)} %bitcast.3.parts), custom_call_target="tpu_custom_call" | custom-call | flops 20000000000 | bytes 4194304 | tf_op jit(solution)/shard_map/sums/pallas_call | solution.py:176
  79.4 4.5 %all-to-all-start.1 = ((bf16[4,128,1024]{2,1,0:T(8,128)(2,1)}), bf16[4,128,1024]{2,1,0:T(8,128)(2,1)S(1)}, u32[]{:S(2)}, u32[]{:S(2)}) async-start(bf16[4,128,1024]{2,1,0:T(8,128)(2,1)} %bitcast.4), calls=%async_computation.1 | async-start | bytes 2097152 | tf_op jit(solution)/shard_map/all_to_all | solution.py:286
  83.9 0.1 pad_add_fusion.1.where
  84.0 6.2 %input_half.2.rest_0_ = bf16[224,4096]{1,0:T(8,128)(2,1)} custom-call(s32[2]{0:T(128)S(1)} %pad_add_fusion.1.where, bf16[224,1024]{1,0:T(8,128)(2,1)S(1)} %copy-done, bf16[8,1,256,1024]{3,2,1,0:T(8,128)(2,1)} %bitcast.10), custom_call_target="tpu_custom_call" | custom-call | flops 939524096 | bytes 5111808 | tf_op jit(solution)/shard_map/input_half/pallas_call | solution.py:239
  90.2 9.2 %all-to-all-done.1.parts = bf16[4,128,1024]{2,1,0:T(8,128)(2,1)S(1)} async-done(((bf16[4,128,1024]{2,1,0:T(8,128)(2,1)}), bf16[4,128,1024]{2,1,0:T(8,128)(2,1)S(1)}, u32[]{:S(2)}, u32[]{:S(2)}) %all-to-all-start.1) | async-done | bytes 1048608 | tf_op jit(solution)/shard_map/all_to_all | solution.py:286
  99.4 0.9 sums.3
  100.3 19.2 %all-to-all-start.2 = ((bf16[16,8,1024]{2,1,0:T(8,128)(2,1)}), bf16[16,8,1024]{2,1,0:T(8,128)(2,1)S(1)}, u32[]{:S(2)}, u32[]{:S(2)}) async-start(bf16[16,8,1024]{2,1,0:T(8,128)(2,1)} %bitcast.9), calls=%async_computation.2 | async-start | bytes 524288 | tf_op jit(solution)/shard_map/all_to_all | solution.py:292
  119.6 0.1 pad_add_fusion.where
  119.7 5.9 %input_half.3 = bf16[224,4096]{1,0:T(8,128)(2,1)} custom-call(s32[2]{0:T(128)S(1)} %pad_add_fusion.where, bf16[224,1024]{1,0:T(8,128)(2,1)S(1)} %copy-done, bf16[8,2,128,1024]{3,2,1,0:T(8,128)(2,1)} %bitcast.11, bf16[224,4096]{1,0:T(8,128)(2,1)} %input_half.2.rest_0_), custom_call_target="tpu_custom_call", output_to_operand_aliasing={{}: (3, {})} | custom-call | flops 939524096 | bytes 5111808 | tf_op jit(solution)/shard_map/input_half/pallas_call | solution.py:239
  125.6 8.6 %all-to-all-done.2 = bf16[16,8,1024]{2,1,0:T(8,128)(2,1)S(1)} async-done(((bf16[16,8,1024]{2,1,0:T(8,128)(2,1)}), bf16[16,8,1024]{2,1,0:T(8,128)(2,1)S(1)}, u32[]{:S(2)}, u32[]{:S(2)}) %all-to-all-start.2) | async-done | bytes 262176 | tf_op jit(solution)/shard_map/all_to_all | solution.py:292
  134.2 0.7 convert_reduce_fusion
  (8 shorter events, 0.1 us)
Async XLA Ops:
  7.2 76.8 %all-gather.5.cloned.1.call-start = ((), (), s32[]{:S(2)}) async-start(), calls=%async_computation.4 | async-start | bytes 4718592 | tf_op jit(solution)/shard_map/all_gather | solution.py:274
  9.6 6.6 %collective-permute-start = (bf16[224,4096]{1,0:T(8,128)(2,1)}, bf16[224,4096]{1,0:T(8,128)(2,1)S(1)}, u32[]{:S(2)}, u32[]{:S(2)}) collective-permute-start(bf16[224,4096]{1,0:T(8,128)(2,1)} %acts.1), channel_id=1, source_target_pairs={{0,1},{1,0},{2,3},{3,2},{4,5},{5,4},{6,7},{7,6},{8,9},{9,8},{10,11... | collective-permute-start | bytes 5505032 | tf_op jit(solution)/shard_map/ppermute | solution.py:21
  11.5 4.6 %collective-permute-start.1 = (bf16[224,1024]{1,0:T(8,128)(2,1)}, bf16[224,1024]{1,0:T(8,128)(2,1)S(1)}, u32[]{:S(2)}, u32[]{:S(2)}) collective-permute-start(bf16[224,1024]{1,0:T(8,128)(2,1)} %grads.3), channel_id=1, source_target_pairs={{0,1},{1,0},{2,3},{3,2},{4,5},{5,4},{6,7},{7,6},{8,9},{9,8},{10,11... | collective-permute-start | bytes 1376264 | tf_op jit(solution)/shard_map/ppermute | solution.py:21
  21.7 54.4 %all-to-all-start = ((bf16[4,8,64,1024]{3,2,1,0:T(8,128)(2,1)}), bf16[4,8,64,1024]{3,2,1,0:T(8,128)(2,1)}, u32[]{:S(2)}, u32[]{:S(2)}) async-start(bf16[4,8,64,1024]{3,2,1,0:T(8,128)(2,1)} %partials.1), calls=%async_computation | async-start | bytes 8388608 | tf_op jit(solution)/shard_map/all_to_all | solution.py:277
  26.6 93.0 %all-gather.3.cloned.1.call-start = ((), (), s32[]{:S(2)}) async-start(), calls=%async_computation.3 | async-start | bytes 4718592 | tf_op jit(solution)/shard_map/all_gather | solution.py:280
  26.7 38.5 %collective-permute-start.2 = (bf16[128,1024]{1,0:T(8,128)(2,1)S(1)}, bf16[128,1024]{1,0:T(8,128)(2,1)S(1)}, u32[]{:S(2)}, u32[]{:S(2)}) collective-permute-start(bf16[128,1024]{1,0:T(8,128)(2,1)S(1)} %get-tuple-element.11), channel_id=1, source_target_pairs={{0,8},{1,9},{2,10},{3,11},{4,12},{5,13},{6,14},{7,15},{16,24},{17,... | collective-permute-start | bytes 786440 | tf_op jit(solution)/shard_map/ppermute | solution.py:35
  65.2 9.5 %collective-permute-start.3 = (bf16[128,1024]{1,0:T(8,128)(2,1)S(1)}, bf16[128,1024]{1,0:T(8,128)(2,1)S(1)}, u32[]{:S(2)}, u32[]{:S(2)}) collective-permute-start(bf16[128,1024]{1,0:T(8,128)(2,1)S(1)} %collective-permute-done.2), channel_id=1, source_target_pairs={{0,16},{1,17},{2,18},{3,19},{4,20},{5,21},{6,22},{7,23},{16,0},{17... | collective-permute-start | bytes 786440 | tf_op jit(solution)/shard_map/ppermute | solution.py:35
  76.1 7.9 %copy-start = (bf16[224,1024]{1,0:T(8,128)(2,1)S(1)}, bf16[224,1024]{1,0:T(8,128)(2,1)}, u32[]{:S(2)}) copy-start(bf16[224,1024]{1,0:T(8,128)(2,1)} %grads.3) | copy-start | bytes 1376260
  79.4 20.0 %all-to-all-start.1 = ((bf16[4,128,1024]{2,1,0:T(8,128)(2,1)}), bf16[4,128,1024]{2,1,0:T(8,128)(2,1)S(1)}, u32[]{:S(2)}, u32[]{:S(2)}) async-start(bf16[4,128,1024]{2,1,0:T(8,128)(2,1)} %bitcast.4), calls=%async_computation.1 | async-start | bytes 2097152 | tf_op jit(solution)/shard_map/all_to_all | solution.py:286
  100.3 33.9 %all-to-all-start.2 = ((bf16[16,8,1024]{2,1,0:T(8,128)(2,1)}), bf16[16,8,1024]{2,1,0:T(8,128)(2,1)S(1)}, u32[]{:S(2)}, u32[]{:S(2)}) async-start(bf16[16,8,1024]{2,1,0:T(8,128)(2,1)} %bitcast.9), calls=%async_computation.2 | async-start | bytes 524288 | tf_op jit(solution)/shard_map/all_to_all | solution.py:292
Sparse Core Ops, SparseCore 0:
  10.7 43.9 all-gather.4
  75.7 41.3 all-gather.2

commit v6 on v5

v6 whole, which is shorter than its diff:
```python
import functools
import math

import jax
import jax.numpy as jnp
from jax import lax
from jax.experimental import pallas as pl
from jax.experimental.pallas import tpu as pltpu
from jax.sharding import Mesh
from jax.sharding import PartitionSpec as P

BLOCK = 128
NX, NZL, NZH, NY, NC = 4, 8, 2, 4, 2
NZ = NZL * NZH
AXES = ("x", "zl", "zh", "y", "c")
MIB = 1024 * 1024
AHEAD = 3
LEFT = 640
CHAIN = 3 * 10**10


def shift(value, axis, step):
    size = lax.axis_size(axis)
    return lax.ppermute(value, axis, [(i, (i + step) % size) for i in range(size)])


def chip_shift(value, move):
    def index(x, z, y, c):
        return (((x * NZL + z % NZL) * NZH + z // NZL) * NY + y) * NC + c

    pairs = []
    for x in range(NX):
        for z in range(NZ):
            to_x, to_z = move(x, z)
            for y in range(NY):
                for c in range(NC):
                    pairs.append((index(x, z, y, c), index(to_x, to_z, y, c)))
    return lax.ppermute(value, AXES, pairs)


def total_of(parts, dtype):
    total = parts[0].astype(jnp.float32)
    for part in parts[1:]:
        total = total + part.astype(jnp.float32)
    return total.astype(dtype)


def weight_kernel(odd, quant, scales, weight, half):
    rows, columns = quant.shape
    levels = quant[...].astype(jnp.float32)
    factors = scales[...].T
    for block in range(columns // BLOCK):
        run = slice(block * BLOCK, (block + 1) * BLOCK)
        weight[:, run] = (levels[:, run] * factors[:, block : block + 1]).astype(weight.dtype)
    part = half.shape[0]
    half[...] = weight[pl.ds(pl.multiple_of(odd[0] * part, part), part), :]


def weights(odd, quant, scales):
    rows, columns = quant.shape
    vmem = pl.BlockSpec(memory_space=pltpu.VMEM)
    quant, scales = (
        pltpu.with_memory_space_constraint(v, pltpu.HBM) for v in (quant, scales.T)
    )
    return pl.pallas_call(
        weight_kernel,
        out_shape=[
            jax.ShapeDtypeStruct((rows, columns), jnp.bfloat16),
            jax.ShapeDtypeStruct((rows // 2, columns), jnp.bfloat16),
        ],
        in_specs=[pl.BlockSpec(memory_space=pltpu.SMEM), vmem, vmem],
        out_specs=[vmem, vmem],
        compiler_params=pltpu.CompilerParams(vmem_limit_bytes=8 * MIB),
        cost_estimate=pl.CostEstimate(
            flops=rows * columns, bytes_accessed=4 * rows * columns, transcendentals=0
        ),
        name="weights",
    )(odd, quant, scales)


def partial_kernel(
    factor, where, acts, acts_in, grads, grads_in, left, r0, r1, r2, r3, *scratch
):
    lhs, rhs, lbuf, rbuf, in_sems, out_sems = scratch
    tokens = acts.shape[0]
    steps = lhs.shape[0]
    each = NY * NZH // steps
    _, _, rows, cut = left.shape
    span = rows * NX
    core, x, y = where[0], where[1], where[2]
    row_group = [lax.rem(k + NX - x, NX) for k in range(NX)]

    first = [
        pltpu.make_async_copy(
            source, rhs.at[pl.ds(half * tokens, tokens)], in_sems.at[2 * NY * NZH + half]
        )
        for half, source in enumerate((grads, grads_in))
    ]
    for copy in first:
        copy.start()
    loads = []
    for j in range(NY * NZH):
        block = j % NZH * NY + lax.rem(y + j // NZH, NY)
        start = pl.multiple_of((block * NC + core) * span, span)
        for half, source in enumerate((acts, acts_in)):
            loads.append(
                pltpu.make_async_copy(
                    source.at[:, pl.ds(start, span)],
                    lhs.at[j // each, pl.ds(half * tokens, tokens), pl.ds(j % each * span, span)],
                    in_sems.at[2 * j + half],
                )
            )
            loads[-1].start()
    for copy in first:
        copy.wait()
    stores = []
    for step in range(steps):
        for copy in loads[2 * each * step : 2 * each * (step + 1)]:
            copy.wait()
        value = lax.dot_general(
            lhs[step], rhs[...], (((0,), (0,)), ((), ())), preferred_element_type=jnp.float32
        )
        value = (value * factor).astype(left.dtype)
        for t in range(each):
            j = step * each + t
            k, z_hi = j // NZH, j % NZH
            for group in range(NX):
                start = t * span + group * rows
                lbuf[j, group] = value[start : start + rows, :cut]
                rbuf[k, row_group[group] * NZH + z_hi] = value[start : start + rows, cut:]
            place = lax.rem(y + k, NY) * NZH + z_hi
            stores.append(
                pltpu.make_async_copy(lbuf.at[j], left.at[:, place], out_sems.at[NY + j])
            )
            stores[-1].start()
            if z_hi == NZH - 1:
                stores.append(
                    pltpu.make_async_copy(rbuf.at[k], (r0, r1, r2, r3)[k], out_sems.at[k])
                )
                stores[-1].start()
    for copy in stores:
        copy.wait()


def partials(where, acts, acts_in, grads, grads_in, factor):
    tokens, width = acts.shape
    columns = grads.shape[1]
    blocks = NZH * NY
    span = width // (blocks * NC)
    rows = span // NX
    steps = 2
    cut = LEFT
    acts, grads = (pltpu.with_memory_space_constraint(v, pltpu.HBM) for v in (acts, grads))
    anywhere = pl.BlockSpec(memory_space=pl.ANY)
    right = (NX * NZH, rows, columns - cut)
    return pl.pallas_call(
        functools.partial(partial_kernel, factor),
        out_shape=[pltpu.HBM((NX, blocks, rows, cut), jnp.bfloat16)]
        + [pltpu.HBM(right, jnp.bfloat16)] * NY,
        in_specs=[pl.BlockSpec(memory_space=pltpu.SMEM)] + [anywhere] * 4,
        out_specs=[anywhere] * (1 + NY),
        scratch_shapes=[
            pltpu.VMEM((steps, 2 * tokens, blocks // steps * span), jnp.bfloat16),
            pltpu.VMEM((2 * tokens, columns), jnp.bfloat16),
            pltpu.VMEM((blocks, NX, rows, cut), jnp.bfloat16),
            pltpu.VMEM((NY, *right), jnp.bfloat16),
            pltpu.SemaphoreType.DMA((2 * blocks + 2,)),
            pltpu.SemaphoreType.DMA((blocks + NY,)),
        ],
        compiler_params=pltpu.CompilerParams(vmem_limit_bytes=24 * MIB),
        cost_estimate=pl.CostEstimate(
            flops=4 * tokens * columns * span * blocks,
            bytes_accessed=2 * blocks * span * columns + 4 * tokens * width,
            transcendentals=0,
        ),
        name="partials",
    )(where, acts, acts_in, grads, grads_in)


def left_kernel(parts, out, held, sems):
    pieces, terms, rows, columns = held.shape
    copies = [
        pltpu.make_async_copy(parts.at[:, pl.ds(q * rows, rows)], held.at[q], sems.at[q])
        for q in range(pieces)
    ]
    for copy in copies[:AHEAD]:
        copy.start()
    for q, copy in enumerate(copies):
        if q + AHEAD < pieces:
            copies[q + AHEAD].start()
        copy.wait()
        out[q * rows : (q + 1) * rows] = total_of([held[q, k] for k in range(terms)], out.dtype)


def left_sums(parts):
    terms, rows, columns = parts.shape
    pieces = 4
    return pl.pallas_call(
        left_kernel,
        out_shape=jax.ShapeDtypeStruct((rows, columns), parts.dtype),
        in_specs=[pl.BlockSpec(memory_space=pl.ANY)],
        out_specs=pl.BlockSpec(memory_space=pltpu.VMEM),
        scratch_shapes=[
            pltpu.VMEM((pieces, terms, rows // pieces, columns), parts.dtype),
            pltpu.SemaphoreType.DMA((pieces,)),
        ],
        compiler_params=pltpu.CompilerParams(vmem_limit_bytes=16 * MIB),
        cost_estimate=pl.CostEstimate(
            flops=CHAIN, bytes_accessed=2 * terms * rows * columns, transcendentals=0
        ),
        name="left_sums",
    )(parts)


def right_kernel(*refs):
    count = len(refs) // 2
    parts, outs = refs[:count], refs[count:]
    rows = outs[0].shape[0]
    for k, out in enumerate(outs):
        run = slice(k * rows, (k + 1) * rows)
        out[...] = total_of([part[run] for part in parts], out.dtype)


def right_sums(parts):
    rows, columns = parts[0].shape
    vmem = pl.BlockSpec(memory_space=pltpu.VMEM)
    count = len(parts)
    return pl.pallas_call(
        right_kernel,
        out_shape=[jax.ShapeDtypeStruct((rows // count, columns), parts[0].dtype)] * count,
        in_specs=[vmem] * count,
        out_specs=[vmem] * count,
        compiler_params=pltpu.CompilerParams(vmem_limit_bytes=16 * MIB),
        cost_estimate=pl.CostEstimate(
            flops=CHAIN, bytes_accessed=2 * count * rows * columns, transcendentals=0
        ),
        name="right_sums",
    )(*parts)


def joined_kernel(left, *refs):
    parts, out = refs[:-1], refs[-1]
    cut = left.shape[2]
    out[:, :cut] = total_of([left[k] for k in range(left.shape[0])], out.dtype)
    out[:, cut:] = total_of([part[...] for part in parts], out.dtype)


def joined_sums(left, parts):
    _, rows, cut = left.shape
    vmem = pl.BlockSpec(memory_space=pltpu.VMEM)
    return pl.pallas_call(
        joined_kernel,
        out_shape=jax.ShapeDtypeStruct((rows, cut + parts[0].shape[1]), left.dtype),
        in_specs=[vmem] * (1 + len(parts)),
        out_specs=vmem,
        compiler_params=pltpu.CompilerParams(vmem_limit_bytes=16 * MIB),
        cost_estimate=pl.CostEstimate(
            flops=CHAIN, bytes_accessed=10 * rows * 1024, transcendentals=0
        ),
        name="joined_sums",
    )(left, *parts)


def input_kernel(where, grads, weight, *rest):
    out, held, lhs, result, in_sems, out_sems = rest[-6:]
    units, each, rows, columns = held.shape
    pitch = out.shape[1] // (NZH * units * each)
    first = pltpu.make_async_copy(grads, lhs, in_sems.at[units])
    first.start()
    copies = [
        pltpu.make_async_copy(weight.at[unit], held.at[unit], in_sems.at[unit])
        for unit in range(units)
    ]
    for copy in copies[:AHEAD]:
        copy.start()
    first.wait()
    done = []
    for unit, copy in enumerate(copies):
        if unit + AHEAD < units:
            copies[unit + AHEAD].start()
        copy.wait()
        span = each * rows
        result[:, unit * span : (unit + 1) * span] = lax.dot_general(
            lhs[...],
            held[unit].reshape(span, columns),
            (((1,), (1,)), ((), ())),
            preferred_element_type=jnp.float32,
        ).astype(result.dtype)
        for group in range(unit * each, (unit + 1) * each):
            start = pl.multiple_of(where[0] * rows, rows) + group * pitch
            done.append(
                pltpu.make_async_copy(
                    result.at[:, pl.ds(group * rows, rows)],
                    out.at[:, pl.ds(pl.multiple_of(start, rows), rows)],
                    out_sems.at[group],
                )
            )
            done[-1].start()
    for copy in done:
        copy.wait()


def input_part(place, grads, weight, width, before=None):
    tokens, columns = grads.shape
    groups, rows, _ = weight.shape
    each = max(1, 256 // rows)
    units = groups // each
    weight = weight.reshape(units, each, rows, columns)
    weight = pltpu.with_memory_space_constraint(weight, pltpu.HBM)
    args = [place[None].astype(jnp.int32), grads, weight]
    aliases = {}
    if before is not None:
        args.append(before)
        aliases = {3: 0}
    anywhere = pl.BlockSpec(memory_space=pl.ANY)
    return pl.pallas_call(
        input_kernel,
        out_shape=jax.ShapeDtypeStruct((tokens, width), jnp.bfloat16),
        in_specs=[pl.BlockSpec(memory_space=pltpu.SMEM)] + [anywhere] * (len(args) - 1),
        out_specs=anywhere,
        scratch_shapes=[
            pltpu.VMEM((units, each, rows, columns), jnp.bfloat16),
            pltpu.VMEM((tokens, columns), jnp.bfloat16),
            pltpu.VMEM((tokens, groups * rows), jnp.bfloat16),
            pltpu.SemaphoreType.DMA((units + 1,)),
            pltpu.SemaphoreType.DMA((groups,)),
        ],
        input_output_aliases=aliases,
        compiler_params=pltpu.CompilerParams(vmem_limit_bytes=16 * MIB),
        cost_estimate=pl.CostEstimate(
            flops=2 * tokens * columns * groups * rows,
            bytes_accessed=2 * groups * rows * columns + 4 * tokens * columns,
            transcendentals=0,
        ),
        name="input_part",
    )(*args)


def shards(acts, grads_out, quant, scales):
    tokens, width = acts.shape
    columns = grads_out.shape[1]
    shard_rows = quant.shape[0]
    total_tokens = tokens * lax.axis_size(AXES)
    x, zl, zh, y, c = (lax.axis_index(name) for name in AXES)
    odd = zl % 2
    groups = NY * NC
    chunk = NZH * NZL * 8

    acts_in = shift(acts, "c", 1)
    grads_in = shift(grads_out, "c", 1)
    weight, piece = weights(odd[None].astype(jnp.int32), quant, scales)
    own_half = lax.all_gather(weight, ("y", "c"), axis=0, tiled=True)
    fetched = chip_shift(piece, lambda i, z: (i, (z + NZL) % NZ))

    factor = 1.0 / math.sqrt(total_tokens)
    where = jnp.stack([c, x, y]).astype(jnp.int32)
    where, _ = lax.optimization_barrier((where, weight))
    left, *right = partials(where, acts, acts_in, grads_out, grads_in, factor)
    left = lax.all_to_all(left, "x", split_axis=0, concat_axis=0, tiled=True)
    right = [right[0]] + [shift(right[k], "y", k) for k in (1, 3, 2)]

    fetched, _ = lax.optimization_barrier((fetched, right[1]))
    fetched_all = lax.all_gather(fetched, ("y", "c"), axis=0, tiled=True)
    fetched, *_ = lax.optimization_barrier((fetched, left, *right))
    swapped = chip_shift(fetched, lambda i, z: (i, z ^ 1))
    swapped_all = lax.all_gather(swapped, ("y", "c"), axis=0, tiled=True)

    left = left_sums(left.reshape(NX, NY * chunk, LEFT)).reshape(NY, chunk, LEFT)
    right = right_sums([part.reshape(NX * chunk, columns - LEFT) for part in right])
    grads_later, _ = lax.optimization_barrier((grads_out, left))
    left = lax.all_to_all(left, "y", split_axis=0, concat_axis=0, tiled=True)
    right = [right[0]] + [shift(right[k], "x", k) for k in (1, 3, 2)]
    own_half = own_half.reshape(groups, shard_rows, columns)
    grad_input = input_part(zh * groups, grads_later, own_half, width)
    grad_input, left = lax.optimization_barrier((grad_input, left))
    rows = joined_sums(left, right).reshape(NZ, 8, columns)
    rows = lax.all_to_all(rows, ("zh", "zl"), split_axis=0, concat_axis=0, tiled=True)
    base = 2 * groups * (1 - zh)
    for gathered, place in ((fetched_all, base + odd), (swapped_all, base + 1 - odd)):
        gathered = gathered.reshape(groups, shard_rows // 2, columns)
        grad_input = input_part(place, grads_later, gathered, width, grad_input)
    grad_input, rows = lax.optimization_barrier((grad_input, rows))
    weight_grad = jnp.sum(rows, axis=0, dtype=jnp.float32)
    return (grad_input, weight_grad)


def solution(mesh):
    fine = Mesh(mesh.devices.reshape(NX, NZL, NZH, NY, NC), AXES)
    tokens = P(AXES, None)
    rows = P(("zh", "y", "c"), None)
    return jax.shard_map(
        shards,
        mesh=fine,
        in_specs=(tokens, tokens, rows, rows),
        out_specs=(tokens, P(("zh", "y", "c", "x", "zl"), None)),
        check_vma=False,
    )
```

time: 142 us -> 155 us (1.092)
  the two profiles are of different devices: /device:TPU:32 before, /device:TPU:1 now
where the time goes in v6:
time: 155 us; the launch traced here: 154 us
  starting transfers between devices  68 us (44%)
  waiting for transfers between devices  44.5 us (29%)
  Pallas kernels  25.4 us (16%)
  between operations  14 us (9%)
  local copies, waits for them, and re-layouts  1.69 us (1%)
    all_gather x1, waiting for transfers between devices, shards(): swapped_all = lax.all_gather(swapped, ('y', 'c'), axis=0, tiled=True)  31 us
    ppermute x8, starting transfers between devices, shift(): lax.ppermute(value, axis, [(i, (i + step) % size) for i in range(size)])  29.7 us
    ppermute x2, starting transfers between devices, chip_shift(): return lax.ppermute(value, AXES, pairs)  19.6 us
    pallas_call x3, Pallas kernels, input_part(): pl.pallas_call(input_kernel, out_shape=jax.ShapeDtypeStruct((tokens, widt...  13.4 us
    all_to_all x1, starting transfers between devices, shards(): lax.all_to_all(rows, ('zh', 'zl'), split_axis=0, concat_axis=0, tiled=True)  11.4 us
    all_to_all x1, waiting for transfers between devices, shards(): left = lax.all_to_all(left, 'x', split_axis=0, concat_axis=0, tiled=True)  9.42 us
    pallas_call x1, Pallas kernels, partials(): pl.pallas_call(functools.partial(partial_kernel, factor), out_shape=[pltp...  5.92 us
    ppermute x8, waiting for transfers between devices, shift(): lax.ppermute(value, axis, [(i, (i + step) % size) for i in range(size)])  3.99 us
  transfers between devices with their start and end apart: 16, of which 4 were waited for; matrix products, arithmetic and copies ran while one was open for 0% of the time, Pallas kernels for 15%

profile of v6, /device:TPU:1, one launch (start us, length us, event | category | flops | bytes accessed | tf_op | source)
XLA Modules:
  0.0 154.4 jit_solution(14631039432794981310)
XLA Ops:
  7.2 2.5 %weights.1 = (bf16[256,1024]{1,0:T(8,128)(2,1)}, bf16[128,1024]{1,0:T(8,128)(2,1)}) custom-call(s32[1]{0:T(128)} %bitcast.4.odd, bf16[256,1024]{1,0:T(8,128)(2,1)} %quant.1, f32[8,256]{1,0:T(8,128)} %bitcast.25), custom_call_target="tpu_custom_call" | custom-call | flops 262144 | bytes 1048576 | tf_op jit(solution)/shard_map/weights/pallas_call | solution.py:65
  9.7 8.8 %collective-permute-start = (bf16[224,4096]{1,0:T(8,128)(2,1)}, bf16[224,4096]{1,0:T(8,128)(2,1)S(1)}, u32[]{:S(2)}, u32[]{:S(2)}) collective-permute-start(bf16[224,4096]{1,0:T(8,128)(2,1)} %acts.1), channel_id=1, source_target_pairs={{0,1},{1,0},{2,3},{3,2},{4,5},{5,4},{6,7},{7,6},{8,9},{9,8},{10,11... | collective-permute-start | bytes 5505032 | tf_op jit(solution)/shard_map/ppermute | solution.py:24
  18.5 1.9 %collective-permute-start.1 = (bf16[224,1024]{1,0:T(8,128)(2,1)}, bf16[224,1024]{1,0:T(8,128)(2,1)S(1)}, u32[]{:S(2)}, u32[]{:S(2)}) collective-permute-start(bf16[224,1024]{1,0:T(8,128)(2,1)} %grads.4), channel_id=1, source_target_pairs={{0,1},{1,0},{2,3},{3,2},{4,5},{5,4},{6,7},{7,6},{8,9},{9,8},{10,11... | collective-permute-start | bytes 1376264 | tf_op jit(solution)/shard_map/ppermute | solution.py:24
  20.5 2.2 %collective-permute-done.1.grads_in = bf16[224,1024]{1,0:T(8,128)(2,1)S(1)} collective-permute-done((bf16[224,1024]{1,0:T(8,128)(2,1)}, bf16[224,1024]{1,0:T(8,128)(2,1)S(1)}, u32[]{:S(2)}, u32[]{:S(2)}) %collective-permute-start.1) | collective-permute-done | bytes 458784 | tf_op jit(solution)/shard_map/ppermute | solution.py:24
  22.8 5.9 %partials.1 = (bf16[4,8,64,640]{3,2,1,0:T(8,128)(2,1)}, bf16[8,64,384]{2,1,0:T(8,128)(2,1)}, bf16[8,64,384]{2,1,0:T(8,128)(2,1)}, bf16[8,64,384]{2,1,0:T(8,128)(2,1)}, bf16[8,64,384]{2,1,0:T(8,128)(2,1)}) custom-call(s32[3]{0:T(128)S(1)} %pad_add_fusion.where, bf16[224,4096]{1,0:T(8,128)(2,1)} %acts.1, bf16[224,4096]{1,0:T(8,128)(2,1)S(1)} %collective-permute-done.acts_in, ...), custom_call_target="tpu_custom_call" | custom-call | flops 1879048192 | bytes 7864320 | tf_op jit(solution)/shard_map/partials/pallas_call | solution.py:156
  28.7 3.7 %all-to-all-start = ((bf16[4,8,64,640]{3,2,1,0:T(8,128)(2,1)}), bf16[4,8,64,640]{3,2,1,0:T(8,128)(2,1)S(1)}, u32[]{:S(2)}, u32[]{:S(2)}) async-start(bf16[4,8,64,640]{3,2,1,0:T(8,128)(2,1)} %get-tuple-element.23), calls=%async_computation | async-start | bytes 5242880 | tf_op jit(solution)/shard_map/all_to_all | solution.py:359
  32.4 1.9 %collective-permute-start.3 = (bf16[8,64,384]{2,1,0:T(8,128)(2,1)}, bf16[8,64,384]{2,1,0:T(8,128)(2,1)S(1)}, u32[]{:S(2)}, u32[]{:S(2)}) collective-permute-start(bf16[8,64,384]{2,1,0:T(8,128)(2,1)} %get-tuple-element.26), channel_id=1, source_target_pairs={{0,2},{2,4},{4,6},{6,0},{1,3},{3,5},{5,7},{7,1},{8,10},{10,12},{12... | collective-permute-start | bytes 1179656 | tf_op jit(solution)/shard_map/ppermute | solution.py:24
  34.3 11.6 %collective-permute-start.2 = (bf16[128,1024]{1,0:T(8,128)(2,1)}, bf16[128,1024]{1,0:T(8,128)(2,1)}, u32[]{:S(2)}, u32[]{:S(2)}) collective-permute-start(bf16[128,1024]{1,0:T(8,128)(2,1)} %get-tuple-element.25), channel_id=1, source_target_pairs={{0,8},{1,9},{2,10},{3,11},{4,12},{5,13},{6,14},{7,15},{16,24},{17,... | collective-permute-start | bytes 786440 | tf_op jit(solution)/shard_map/ppermute | solution.py:38
  46.0 3.4 %collective-permute-start.4 = (bf16[8,64,384]{2,1,0:T(8,128)(2,1)}, bf16[8,64,384]{2,1,0:T(8,128)(2,1)S(1)}, u32[]{:S(2)}, u32[]{:S(2)}) collective-permute-start(bf16[8,64,384]{2,1,0:T(8,128)(2,1)} %get-tuple-element.29), channel_id=1, source_target_pairs={{0,6},{2,0},{4,2},{6,4},{1,7},{3,1},{5,3},{7,5},{8,14},{10,8},{12,... | collective-permute-start | bytes 1179656 | tf_op jit(solution)/shard_map/ppermute | solution.py:24
  49.4 3.6 %collective-permute-start.5 = (bf16[8,64,384]{2,1,0:T(8,128)(2,1)}, bf16[8,64,384]{2,1,0:T(8,128)(2,1)}, u32[]{:S(2)}, u32[]{:S(2)}) collective-permute-start(bf16[8,64,384]{2,1,0:T(8,128)(2,1)} %get-tuple-element.30), channel_id=1, source_target_pairs={{0,4},{2,6},{4,0},{6,2},{1,5},{3,7},{5,1},{7,3},{8,12},{10,14},{12... | collective-permute-start | bytes 1179656 | tf_op jit(solution)/shard_map/ppermute | solution.py:24
  52.9 1.7 %collective-permute-done.3 = bf16[8,64,384]{2,1,0:T(8,128)(2,1)S(1)} collective-permute-done((bf16[8,64,384]{2,1,0:T(8,128)(2,1)}, bf16[8,64,384]{2,1,0:T(8,128)(2,1)S(1)}, u32[]{:S(2)}, u32[]{:S(2)}) %collective-permute-start.3) | collective-permute-done | bytes 393248 | tf_op jit(solution)/shard_map/ppermute | solution.py:24
  54.7 9.4 %all-to-all-done = bf16[4,8,64,640]{3,2,1,0:T(8,128)(2,1)S(1)} async-done(((bf16[4,8,64,640]{3,2,1,0:T(8,128)(2,1)}), bf16[4,8,64,640]{3,2,1,0:T(8,128)(2,1)S(1)}, u32[]{:S(2)}, u32[]{:S(2)}) %all-to-all-start) | async-done | bytes 2621472 | tf_op jit(solution)/shard_map/all_to_all | solution.py:359
  64.1 1.6 %left_sums.1 = bf16[512,640]{1,0:T(8,128)(2,1)} custom-call(bf16[4,512,640]{2,1,0:T(8,128)(2,1)S(1)} %bitcast.18), custom_call_target="tpu_custom_call" | custom-call | flops 30000001024 | bytes 2621440 | tf_op jit(solution)/shard_map/left_sums/pallas_call | solution.py:198
  65.7 3.5 %all-to-all-start.1 = ((bf16[4,128,640]{2,1,0:T(8,128)(2,1)}), bf16[4,128,640]{2,1,0:T(8,128)(2,1)S(1)}, u32[]{:S(2)}, u32[]{:S(2)}) async-start(bf16[4,128,640]{2,1,0:T(8,128)(2,1)} %bitcast.7), calls=%async_computation.1 | async-start | bytes 1310720 | tf_op jit(solution)/shard_map/all_to_all | solution.py:371
  69.3 7.9 %collective-permute-start.6 = (bf16[128,1024]{1,0:T(8,128)(2,1)}, bf16[128,1024]{1,0:T(8,128)(2,1)S(1)}, u32[]{:S(2)}, u32[]{:S(2)}) collective-permute-start(bf16[128,1024]{1,0:T(8,128)(2,1)} %collective-permute-done.2), channel_id=1, source_target_pairs={{0,16},{1,17},{2,18},{3,19},{4,20},{5,21},{6,22},{7,23},{16,0},{17... | collective-permute-start | bytes 786440 | tf_op jit(solution)/shard_map/ppermute | solution.py:38
  78.2 1.2 right_sums.1
  79.5 3.3 %collective-permute-start.7 = (bf16[128,384]{1,0:T(8,128)(2,1)S(1)}, bf16[128,384]{1,0:T(8,128)(2,1)S(1)}, u32[]{:S(2)}, u32[]{:S(2)}) collective-permute-start(bf16[128,384]{1,0:T(8,128)(2,1)S(1)} %get-tuple-element.35), channel_id=1, source_target_pairs={{0,128},{128,256},{256,384},{384,0},{1,129},{129,257},{257,385},{3... | collective-permute-start | bytes 294920 | tf_op jit(solution)/shard_map/ppermute | solution.py:24
  82.8 3.2 %collective-permute-start.8 = (bf16[128,384]{1,0:T(8,128)(2,1)S(1)}, bf16[128,384]{1,0:T(8,128)(2,1)S(1)}, u32[]{:S(2)}, u32[]{:S(2)}) collective-permute-start(bf16[128,384]{1,0:T(8,128)(2,1)S(1)} %get-tuple-element.36), channel_id=1, source_target_pairs={{0,384},{128,0},{256,128},{384,256},{1,385},{129,1},{257,129},{385... | collective-permute-start | bytes 294920 | tf_op jit(solution)/shard_map/ppermute | solution.py:24
  86.0 3.6 %collective-permute-start.9 = (bf16[128,384]{1,0:T(8,128)(2,1)S(1)}, bf16[128,384]{1,0:T(8,128)(2,1)S(1)}, u32[]{:S(2)}, u32[]{:S(2)}) collective-permute-start(bf16[128,384]{1,0:T(8,128)(2,1)S(1)} %get-tuple-element.37), channel_id=1, source_target_pairs={{0,256},{128,384},{256,0},{384,128},{1,257},{129,385},{257,1},{385... | collective-permute-start | bytes 294920 | tf_op jit(solution)/shard_map/ppermute | solution.py:24
  90.4 5.7 %input_part.3.rest_0_ = bf16[224,4096]{1,0:T(8,128)(2,1)} custom-call(s32[1]{0:T(128)} %bitcast.11.where, bf16[224,1024]{1,0:T(8,128)(2,1)S(1)} %copy-done, bf16[8,1,256,1024]{3,2,1,0:T(8,128)(2,1)} %bitcast.22), custom_call_target="tpu_custom_call" | custom-call | flops 939524096 | bytes 5111808 | tf_op jit(solution)/shard_map/input_part/pallas_call | solution.py:316
  97.0 11.4 %all-to-all-start.2 = ((bf16[16,8,1024]{2,1,0:T(8,128)(2,1)}), bf16[16,8,1024]{2,1,0:T(8,128)(2,1)S(1)}, u32[]{:S(2)}, u32[]{:S(2)}) async-start(bf16[16,8,1024]{2,1,0:T(8,128)(2,1)} %bitcast.17), calls=%async_computation.2 | async-start | bytes 524288 | tf_op jit(solution)/shard_map/all_to_all | solution.py:377
  108.5 3.9 %input_part.4.rest_0_ = bf16[224,4096]{1,0:T(8,128)(2,1)} custom-call(s32[1]{0:T(128)} %bitcast.9.where, bf16[224,1024]{1,0:T(8,128)(2,1)S(1)} %copy-done, bf16[4,2,128,1024]{3,2,1,0:T(8,128)(2,1)} %bitcast.23, bf16[224,4096]{1,0:T(8,128)(2,1)} %input_part.3.rest_0_), custom_call_target="tpu_custom_call", output_to_operand_aliasing={{}: (3, {})} | custom-call | flops 469762048 | bytes 3014656 | tf_op jit(solution)/shard_map/input_part/pallas_call | solution.py:316
  112.3 31.0 %all-gather.4.cloned.1.call-done = bf16[1024,1024]{1,0:T(8,128)(2,1)} async-done(((bf16[128,1024]{1,0:T(8,128)(2,1)}), bf16[1024,1024]{1,0:T(8,128)(2,1)}) %all-gather.4.cloned.1.call-update) | async-done | bytes 2097168 | tf_op jit(solution)/shard_map/all_gather | solution.py:366
  143.3 3.8 %input_part.5 = bf16[224,4096]{1,0:T(8,128)(2,1)} custom-call(s32[1]{0:T(128)} %bitcast.where, bf16[224,1024]{1,0:T(8,128)(2,1)S(1)} %copy-done, bf16[4,2,128,1024]{3,2,1,0:T(8,128)(2,1)} %bitcast.24, bf16[224,4096]{1,0:T(8,128)(2,1)} %input_part.4.rest_0_), custom_call_target="tpu_custom_call", output_to_operand_aliasing={{}: (3, {})} | custom-call | flops 469762048 | bytes 3014656 | tf_op jit(solution)/shard_map/input_part/pallas_call | solution.py:316
  (27 shorter events, 3.5 us)
Async XLA Ops:
  7.2 83.2 %all-gather.8.cloned.1.call-start = ((), (), s32[]{:S(2)}) async-start(), calls=%async_computation.5 | async-start | bytes 4718592 | tf_op jit(solution)/shard_map/all_gather | solution.py:352
  9.7 13.1 %collective-permute-start = (bf16[224,4096]{1,0:T(8,128)(2,1)}, bf16[224,4096]{1,0:T(8,128)(2,1)S(1)}, u32[]{:S(2)}, u32[]{:S(2)}) collective-permute-start(bf16[224,4096]{1,0:T(8,128)(2,1)} %acts.1), channel_id=1, source_target_pairs={{0,1},{1,0},{2,3},{3,2},{4,5},{5,4},{6,7},{7,6},{8,9},{9,8},{10,11... | collective-permute-start | bytes 5505032 | tf_op jit(solution)/shard_map/ppermute | solution.py:24
  18.5 4.3 %collective-permute-start.1 = (bf16[224,1024]{1,0:T(8,128)(2,1)}, bf16[224,1024]{1,0:T(8,128)(2,1)S(1)}, u32[]{:S(2)}, u32[]{:S(2)}) collective-permute-start(bf16[224,1024]{1,0:T(8,128)(2,1)} %grads.4), channel_id=1, source_target_pairs={{0,1},{1,0},{2,3},{3,2},{4,5},{5,4},{6,7},{7,6},{8,9},{9,8},{10,11... | collective-permute-start | bytes 1376264 | tf_op jit(solution)/shard_map/ppermute | solution.py:24
  28.7 35.4 %all-to-all-start = ((bf16[4,8,64,640]{3,2,1,0:T(8,128)(2,1)}), bf16[4,8,64,640]{3,2,1,0:T(8,128)(2,1)S(1)}, u32[]{:S(2)}, u32[]{:S(2)}) async-start(bf16[4,8,64,640]{3,2,1,0:T(8,128)(2,1)} %get-tuple-element.23), calls=%async_computation | async-start | bytes 5242880 | tf_op jit(solution)/shard_map/all_to_all | solution.py:359
  32.4 76.1 %all-gather.6.cloned.1.call-start = ((), (), s32[]{:S(2)}) async-start(), calls=%async_computation.4 | async-start | bytes 2359296 | tf_op jit(solution)/shard_map/all_gather | solution.py:363
  32.4 22.3 %collective-permute-start.3 = (bf16[8,64,384]{2,1,0:T(8,128)(2,1)}, bf16[8,64,384]{2,1,0:T(8,128)(2,1)S(1)}, u32[]{:S(2)}, u32[]{:S(2)}) collective-permute-start(bf16[8,64,384]{2,1,0:T(8,128)(2,1)} %get-tuple-element.26), channel_id=1, source_target_pairs={{0,2},{2,4},{4,6},{6,0},{1,3},{3,5},{5,7},{7,1},{8,10},{10,12},{12... | collective-permute-start | bytes 1179656 | tf_op jit(solution)/shard_map/ppermute | solution.py:24
  34.3 18.6 %collective-permute-start.2 = (bf16[128,1024]{1,0:T(8,128)(2,1)}, bf16[128,1024]{1,0:T(8,128)(2,1)}, u32[]{:S(2)}, u32[]{:S(2)}) collective-permute-start(bf16[128,1024]{1,0:T(8,128)(2,1)} %get-tuple-element.25), channel_id=1, source_target_pairs={{0,8},{1,9},{2,10},{3,11},{4,12},{5,13},{6,14},{7,15},{16,24},{17,... | collective-permute-start | bytes 786440 | tf_op jit(solution)/shard_map/ppermute | solution.py:38
  46.0 23.2 %collective-permute-start.4 = (bf16[8,64,384]{2,1,0:T(8,128)(2,1)}, bf16[8,64,384]{2,1,0:T(8,128)(2,1)S(1)}, u32[]{:S(2)}, u32[]{:S(2)}) collective-permute-start(bf16[8,64,384]{2,1,0:T(8,128)(2,1)} %get-tuple-element.29), channel_id=1, source_target_pairs={{0,6},{2,0},{4,2},{6,4},{1,7},{3,1},{5,3},{7,5},{8,14},{10,8},{12,... | collective-permute-start | bytes 1179656 | tf_op jit(solution)/shard_map/ppermute | solution.py:24
  49.4 19.9 %collective-permute-start.5 = (bf16[8,64,384]{2,1,0:T(8,128)(2,1)}, bf16[8,64,384]{2,1,0:T(8,128)(2,1)}, u32[]{:S(2)}, u32[]{:S(2)}) collective-permute-start(bf16[8,64,384]{2,1,0:T(8,128)(2,1)} %get-tuple-element.30), channel_id=1, source_target_pairs={{0,4},{2,6},{4,0},{6,2},{1,5},{3,7},{5,1},{7,3},{8,12},{10,14},{12... | collective-permute-start | bytes 1179656 | tf_op jit(solution)/shard_map/ppermute | solution.py:24
  65.7 30.4 %all-to-all-start.1 = ((bf16[4,128,640]{2,1,0:T(8,128)(2,1)}), bf16[4,128,640]{2,1,0:T(8,128)(2,1)S(1)}, u32[]{:S(2)}, u32[]{:S(2)}) async-start(bf16[4,128,640]{2,1,0:T(8,128)(2,1)} %bitcast.7), calls=%async_computation.1 | async-start | bytes 1310720 | tf_op jit(solution)/shard_map/all_to_all | solution.py:371
  69.2 74.1 %all-gather.4.cloned.1.call-start = ((), (), s32[]{:S(2)}) async-start(), calls=%async_computation.3 | async-start | bytes 2359296 | tf_op jit(solution)/shard_map/all_gather | solution.py:366
  69.3 20.4 %collective-permute-start.6 = (bf16[128,1024]{1,0:T(8,128)(2,1)}, bf16[128,1024]{1,0:T(8,128)(2,1)S(1)}, u32[]{:S(2)}, u32[]{:S(2)}) collective-permute-start(bf16[128,1024]{1,0:T(8,128)(2,1)} %collective-permute-done.2), channel_id=1, source_target_pairs={{0,16},{1,17},{2,18},{3,19},{4,20},{5,21},{6,22},{7,23},{16,0},{17... | collective-permute-start | bytes 786440 | tf_op jit(solution)/shard_map/ppermute | solution.py:38
  77.2 1.0 copy-start.1
  78.2 12.2 %copy-start = (bf16[224,1024]{1,0:T(8,128)(2,1)S(1)}, bf16[224,1024]{1,0:T(8,128)(2,1)}, u32[]{:S(2)}) copy-start(bf16[224,1024]{1,0:T(8,128)(2,1)} %grads.4) | copy-start | bytes 1376260
  79.5 16.6 %collective-permute-start.7 = (bf16[128,384]{1,0:T(8,128)(2,1)S(1)}, bf16[128,384]{1,0:T(8,128)(2,1)S(1)}, u32[]{:S(2)}, u32[]{:S(2)}) collective-permute-start(bf16[128,384]{1,0:T(8,128)(2,1)S(1)} %get-tuple-element.35), channel_id=1, source_target_pairs={{0,128},{128,256},{256,384},{384,0},{1,129},{129,257},{257,385},{3... | collective-permute-start | bytes 294920 | tf_op jit(solution)/shard_map/ppermute | solution.py:24
  82.8 13.3 %collective-permute-start.8 = (bf16[128,384]{1,0:T(8,128)(2,1)S(1)}, bf16[128,384]{1,0:T(8,128)(2,1)S(1)}, u32[]{:S(2)}, u32[]{:S(2)}) collective-permute-start(bf16[128,384]{1,0:T(8,128)(2,1)S(1)} %get-tuple-element.36), channel_id=1, source_target_pairs={{0,384},{128,0},{256,128},{384,256},{1,385},{129,1},{257,129},{385... | collective-permute-start | bytes 294920 | tf_op jit(solution)/shard_map/ppermute | solution.py:24
  86.0 10.1 %collective-permute-start.9 = (bf16[128,384]{1,0:T(8,128)(2,1)S(1)}, bf16[128,384]{1,0:T(8,128)(2,1)S(1)}, u32[]{:S(2)}, u32[]{:S(2)}) collective-permute-start(bf16[128,384]{1,0:T(8,128)(2,1)S(1)} %get-tuple-element.37), channel_id=1, source_target_pairs={{0,256},{128,384},{256,0},{384,128},{1,257},{129,385},{257,1},{385... | collective-permute-start | bytes 294920 | tf_op jit(solution)/shard_map/ppermute | solution.py:24
  89.6 0.7 copy-start.2
  97.0 50.2 %all-to-all-start.2 = ((bf16[16,8,1024]{2,1,0:T(8,128)(2,1)}), bf16[16,8,1024]{2,1,0:T(8,128)(2,1)S(1)}, u32[]{:S(2)}, u32[]{:S(2)}) async-start(bf16[16,8,1024]{2,1,0:T(8,128)(2,1)} %bitcast.17), calls=%async_computation.2 | async-start | bytes 524288 | tf_op jit(solution)/shard_map/all_to_all | solution.py:377
Sparse Core Ops, SparseCore 0:
  10.7 62.3 all-gather.7
  75.3 32.5 all-gather.5
  110.0 33.2 all-gather.3

commit v7 on v6

--- a/solution.py
+++ b/solution.py
@@ -15,8 +15,8 @@
 AXES = ("x", "zl", "zh", "y", "c")
 MIB = 1024 * 1024
 AHEAD = 3
-LEFT = 640
-CHAIN = 3 * 10**10
+LEFT = 768
+CHAIN = 16 * 10**9
 
 
 def shift(value, axis, step):
@@ -263,51 +263,53 @@
 
 def input_kernel(where, grads, weight, *rest):
     out, held, lhs, result, in_sems, out_sems = rest[-6:]
-    units, each, rows, columns = held.shape
-    pitch = out.shape[1] // (NZH * units * each)
-    first = pltpu.make_async_copy(grads, lhs, in_sems.at[units])
+    groups, rows, _ = held.shape
+    first = pltpu.make_async_copy(grads, lhs, in_sems.at[2 * groups])
     first.start()
-    copies = [
-        pltpu.make_async_copy(weight.at[unit], held.at[unit], in_sems.at[unit])
-        for unit in range(units)
-    ]
-    for copy in copies[:AHEAD]:
-        copy.start()
+    half = rows // 2
+    copies = []
+    for group in range(groups):
+        copies.append(
+            [
+                pltpu.make_async_copy(
+                    weight.at[group, pl.ds(i * half, half)],
+                    held.at[group, pl.ds(pl.multiple_of((where[1] ^ i) * half, half), half)],
+                    in_sems.at[2 * group + i],
+                )
+                for i in range(2)
+            ]
+        )
+    for pair in copies[:AHEAD]:
+        for copy in pair:
+            copy.start()
     first.wait()
     done = []
-    for unit, copy in enumerate(copies):
-        if unit + AHEAD < units:
-            copies[unit + AHEAD].start()
-        copy.wait()
-        span = each * rows
-        result[:, unit * span : (unit + 1) * span] = lax.dot_general(
-            lhs[...],
-            held[unit].reshape(span, columns),
-            (((1,), (1,)), ((), ())),
-            preferred_element_type=jnp.float32,
+    for group, pair in enumerate(copies):
+        if group + AHEAD < groups:
+            for copy in copies[group + AHEAD]:
+                copy.start()
+        for copy in pair:
+            copy.wait()
+        run = pl.ds(group * rows, rows)
+        result[:, run] = lax.dot_general(
+            lhs[...], held[group], (((1,), (1,)), ((), ())), preferred_element_type=jnp.float32
         ).astype(result.dtype)
-        for group in range(unit * each, (unit + 1) * each):
-            start = pl.multiple_of(where[0] * rows, rows) + group * pitch
-            done.append(
-                pltpu.make_async_copy(
-                    result.at[:, pl.ds(group * rows, rows)],
-                    out.at[:, pl.ds(pl.multiple_of(start, rows), rows)],
-                    out_sems.at[group],
-                )
+        start = pl.multiple_of((where[0] + group) * rows, rows)
+        done.append(
+            pltpu.make_async_copy(
+                result.at[:, run], out.at[:, pl.ds(start, rows)], out_sems.at[group]
             )
-            done[-1].start()
+        )
+        done[-1].start()
     for copy in done:
         copy.wait()
 
 
-def input_part(place, grads, weight, width, before=None):
+def input_part(place, turn, grads, weight, width, before=None):
     tokens, columns = grads.shape
     groups, rows, _ = weight.shape
-    each = max(1, 256 // rows)
-    units = groups // each
-    weight = weight.reshape(units, each, rows, columns)
     weight = pltpu.with_memory_space_constraint(weight, pltpu.HBM)
-    args = [place[None].astype(jnp.int32), grads, weight]
+    args = [jnp.stack([place, turn]).astype(jnp.int32), grads, weight]
     aliases = {}
     if before is not None:
         args.append(before)
@@ -319,10 +321,10 @@
         in_specs=[pl.BlockSpec(memory_space=pltpu.SMEM)] + [anywhere] * (len(args) - 1),
         out_specs=anywhere,
         scratch_shapes=[
-            pltpu.VMEM((units, each, rows, columns), jnp.bfloat16),
+            pltpu.VMEM((groups, rows, columns), jnp.bfloat16),
             pltpu.VMEM((tokens, columns), jnp.bfloat16),
             pltpu.VMEM((tokens, groups * rows), jnp.bfloat16),
-            pltpu.SemaphoreType.DMA((units + 1,)),
+            pltpu.SemaphoreType.DMA((2 * groups + 1,)),
             pltpu.SemaphoreType.DMA((groups,)),
         ],
         input_output_aliases=aliases,
@@ -359,11 +361,10 @@
     left = lax.all_to_all(left, "x", split_axis=0, concat_axis=0, tiled=True)
     right = [right[0]] + [shift(right[k], "y", k) for k in (1, 3, 2)]
 
-    fetched, _ = lax.optimization_barrier((fetched, right[1]))
-    fetched_all = lax.all_gather(fetched, ("y", "c"), axis=0, tiled=True)
-    fetched, *_ = lax.optimization_barrier((fetched, left, *right))
     swapped = chip_shift(fetched, lambda i, z: (i, z ^ 1))
-    swapped_all = lax.all_gather(swapped, ("y", "c"), axis=0, tiled=True)
+    other_half = lax.all_gather(
+        jnp.concatenate([fetched, swapped], axis=0), ("y", "c"), axis=0, tiled=True
+    )
 
     left = left_sums(left.reshape(NX, NY * chunk, LEFT)).reshape(NY, chunk, LEFT)
     right = right_sums([part.reshape(NX * chunk, columns - LEFT) for part in right])
@@ -371,14 +372,14 @@
     left = lax.all_to_all(left, "y", split_axis=0, concat_axis=0, tiled=True)
     right = [right[0]] + [shift(right[k], "x", k) for k in (1, 3, 2)]
     own_half = own_half.reshape(groups, shard_rows, columns)
-    grad_input = input_part(zh * groups, grads_later, own_half, width)
+    grad_input = input_part(zh * groups, 0 * odd, grads_later, own_half, width)
     grad_input, left = lax.optimization_barrier((grad_input, left))
     rows = joined_sums(left, right).reshape(NZ, 8, columns)
     rows = lax.all_to_all(rows, ("zh", "zl"), split_axis=0, concat_axis=0, tiled=True)
-    base = 2 * groups * (1 - zh)
-    for gathered, place in ((fetched_all, base + odd), (swapped_all, base + 1 - odd)):
-        gathered = gathered.reshape(groups, shard_rows // 2, columns)
-        grad_input = input_part(place, grads_later, gathered, width, grad_input)
+    other_half = other_half.reshape(groups, shard_rows, columns)
+    grad_input = input_part(
+        (1 - zh) * groups, odd, grads_later, other_half, width, grad_input
+    )
     grad_input, rows = lax.optimization_barrier((grad_input, rows))
     weight_grad = jnp.sum(rows, axis=0, dtype=jnp.float32)
     return (grad_input, weight_grad)

time: 155 us -> 139 us (0.90)
  the two profiles are of different devices: /device:TPU:1 before, /device:TPU:24 now
where the time goes in v7:
time: 139 us
  starting transfers between devices  74.9 us (54%)
  Pallas kernels  23.6 us (17%)
  waiting for transfers between devices  21.3 us (15%)
  between operations  14.2 us (10%)
  other arithmetic  2.65 us (2%)
  local copies, waits for them, and re-layouts  1.91 us (1%)
    ppermute x2, starting transfers between devices, chip_shift(): return lax.ppermute(value, AXES, pairs)  31.9 us
    ppermute x8, starting transfers between devices, shift(): lax.ppermute(value, axis, [(i, (i + step) % size) for i in range(size)])  22.4 us
    pallas_call x2, Pallas kernels, input_part(): pl.pallas_call(input_kernel, out_shape=jax.ShapeDtypeStruct((tokens, widt...  12.6 us
    all_to_all x1, starting transfers between devices, shards(): lax.all_to_all(rows, ('zh', 'zl'), split_axis=0, concat_axis=0, tiled=True)  11.7 us
    all_to_all x1, waiting for transfers between devices, shards(): lax.all_to_all(rows, ('zh', 'zl'), split_axis=0, concat_axis=0, tiled=True)  10.1 us
    pallas_call x1, Pallas kernels, partials(): pl.pallas_call(functools.partial(partial_kernel, factor), out_shape=[pltp...  5.97 us
    ppermute x2, waiting for transfers between devices, chip_shift(): return lax.ppermute(value, AXES, pairs)  5.95 us
    all_to_all x1, starting transfers between devices, shards(): left = lax.all_to_all(left, 'y', split_axis=0, concat_axis=0, tiled=True)  4.64 us
  transfers between devices with their start and end apart: 15, of which 4 were waited for; matrix products, arithmetic and copies ran while one was open for 1% of the time, Pallas kernels for 15%

profile of v7, /device:TPU:24, one launch (start us, length us, event | category | flops | bytes accessed | tf_op | source)
XLA Modules:
  0.0 138.7 jit_solution(1507019550354605621)
XLA Ops:
  7.2 2.4 %weights.1 = (bf16[256,1024]{1,0:T(8,128)(2,1)}, bf16[128,1024]{1,0:T(8,128)(2,1)S(1)}) custom-call(s32[1]{0:T(128)} %bitcast.1.odd, bf16[256,1024]{1,0:T(8,128)(2,1)} %quant.1, f32[8,256]{1,0:T(8,128)} %bitcast.22), custom_call_target="tpu_custom_call" | custom-call | flops 262144 | bytes 1048576 | tf_op jit(solution)/shard_map/weights/pallas_call | solution.py:65
  9.6 1.9 %collective-permute-start = (bf16[224,4096]{1,0:T(8,128)(2,1)}, bf16[224,4096]{1,0:T(8,128)(2,1)S(1)}, u32[]{:S(2)}, u32[]{:S(2)}) collective-permute-start(bf16[224,4096]{1,0:T(8,128)(2,1)} %acts.1), channel_id=1, source_target_pairs={{0,1},{1,0},{2,3},{3,2},{4,5},{5,4},{6,7},{7,6},{8,9},{9,8},{10,11... | collective-permute-start | bytes 5505032 | tf_op jit(solution)/shard_map/ppermute | solution.py:24
  11.5 2.4 %collective-permute-start.1 = (bf16[224,1024]{1,0:T(8,128)(2,1)}, bf16[224,1024]{1,0:T(8,128)(2,1)S(1)}, u32[]{:S(2)}, u32[]{:S(2)}) collective-permute-start(bf16[224,1024]{1,0:T(8,128)(2,1)} %grads.3), channel_id=1, source_target_pairs={{0,1},{1,0},{2,3},{3,2},{4,5},{5,4},{6,7},{7,6},{8,9},{9,8},{10,11... | collective-permute-start | bytes 1376264 | tf_op jit(solution)/shard_map/ppermute | solution.py:24
  13.9 15.7 %collective-permute-start.2 = (bf16[128,1024]{1,0:T(8,128)(2,1)S(1)}, bf16[128,1024]{1,0:T(8,128)(2,1)}, u32[]{:S(2)}, u32[]{:S(2)}) collective-permute-start(bf16[128,1024]{1,0:T(8,128)(2,1)S(1)} %get-tuple-element.23), channel_id=1, source_target_pairs={{0,8},{1,9},{2,10},{3,11},{4,12},{5,13},{6,14},{7,15},{16,24},{17,... | collective-permute-start | bytes 786440 | tf_op jit(solution)/shard_map/ppermute | solution.py:38
  29.8 6.0 %partials.1 = (bf16[4,8,64,768]{3,2,1,0:T(8,128)(2,1)}, bf16[8,64,256]{2,1,0:T(8,128)(2,1)}, bf16[8,64,256]{2,1,0:T(8,128)(2,1)}, bf16[8,64,256]{2,1,0:T(8,128)(2,1)}, bf16[8,64,256]{2,1,0:T(8,128)(2,1)}) custom-call(s32[3]{0:T(128)S(1)} %pad_add_fusion.1.where, bf16[224,4096]{1,0:T(8,128)(2,1)} %acts.1, bf16[224,4096]{1,0:T(8,128)(2,1)S(1)} %collective-permute-done.acts_in, ...), custom_call_target="tpu_custom_call" | custom-call | flops 1879048192 | bytes 7864320 | tf_op jit(solution)/shard_map/partials/pallas_call | solution.py:156
  35.7 4.3 %all-to-all-start = ((bf16[4,8,64,768]{3,2,1,0:T(8,128)(2,1)}), bf16[4,8,64,768]{3,2,1,0:T(8,128)(2,1)S(1)}, u32[]{:S(2)}, u32[]{:S(2)}) async-start(bf16[4,8,64,768]{3,2,1,0:T(8,128)(2,1)} %get-tuple-element.21), calls=%async_computation | async-start | bytes 6291456 | tf_op jit(solution)/shard_map/all_to_all | solution.py:361
  40.1 16.2 %collective-permute-start.3 = (bf16[128,1024]{1,0:T(8,128)(2,1)}, bf16[128,1024]{1,0:T(8,128)(2,1)S(1)}, u32[]{:S(2)}, u32[]{:S(2)}) collective-permute-start(bf16[128,1024]{1,0:T(8,128)(2,1)} %collective-permute-done.2), channel_id=1, source_target_pairs={{0,16},{1,17},{2,18},{3,19},{4,20},{5,21},{6,22},{7,23},{16,0},{17... | collective-permute-start | bytes 786440 | tf_op jit(solution)/shard_map/ppermute | solution.py:38
  56.3 5.9 %collective-permute-done.3 = bf16[128,1024]{1,0:T(8,128)(2,1)S(1)} collective-permute-done((bf16[128,1024]{1,0:T(8,128)(2,1)}, bf16[128,1024]{1,0:T(8,128)(2,1)S(1)}, u32[]{:S(2)}, u32[]{:S(2)}) %collective-permute-start.3) | collective-permute-done | bytes 262176 | tf_op jit(solution)/shard_map/ppermute | solution.py:38
  62.2 1.8 %pad_maximum_fusion = bf16[256,1024]{1,0:T(8,128)(2,1)} fusion(bf16[128,1024]{1,0:T(8,128)(2,1)S(1)} %collective-permute-done.3, bf16[128,1024]{1,0:T(8,128)(2,1)} %collective-permute-done.2), kind=kLoop, calls=%fused_computation | loop fusion | flops 1048576 | bytes 1048576 | tf_op jit(solution)/shard_map/concatenate | solution.py:366
  64.1 2.1 %collective-permute-start.4 = (bf16[8,64,256]{2,1,0:T(8,128)(2,1)}, bf16[8,64,256]{2,1,0:T(8,128)(2,1)S(1)}, u32[]{:S(2)}, u32[]{:S(2)}) collective-permute-start(bf16[8,64,256]{2,1,0:T(8,128)(2,1)} %get-tuple-element.27), channel_id=1, source_target_pairs={{0,2},{2,4},{4,6},{6,0},{1,3},{3,5},{5,7},{7,1},{8,10},{10,12},{12... | collective-permute-start | bytes 786440 | tf_op jit(solution)/shard_map/ppermute | solution.py:24
  66.2 3.7 %collective-permute-start.5 = (bf16[8,64,256]{2,1,0:T(8,128)(2,1)}, bf16[8,64,256]{2,1,0:T(8,128)(2,1)}, u32[]{:S(2)}, u32[]{:S(2)}) collective-permute-start(bf16[8,64,256]{2,1,0:T(8,128)(2,1)} %get-tuple-element.28), channel_id=1, source_target_pairs={{0,6},{2,0},{4,2},{6,4},{1,7},{3,1},{5,3},{7,5},{8,14},{10,8},{12,... | collective-permute-start | bytes 786440 | tf_op jit(solution)/shard_map/ppermute | solution.py:24
  69.9 3.1 %collective-permute-start.6 = (bf16[8,64,256]{2,1,0:T(8,128)(2,1)}, bf16[8,64,256]{2,1,0:T(8,128)(2,1)}, u32[]{:S(2)}, u32[]{:S(2)}) collective-permute-start(bf16[8,64,256]{2,1,0:T(8,128)(2,1)} %get-tuple-element.29), channel_id=1, source_target_pairs={{0,4},{2,6},{4,0},{6,2},{1,5},{3,7},{5,1},{7,3},{8,12},{10,14},{12... | collective-permute-start | bytes 786440 | tf_op jit(solution)/shard_map/ppermute | solution.py:24
  73.1 4.4 %all-to-all-done = bf16[4,8,64,768]{3,2,1,0:T(8,128)(2,1)S(1)} async-done(((bf16[4,8,64,768]{3,2,1,0:T(8,128)(2,1)}), bf16[4,8,64,768]{3,2,1,0:T(8,128)(2,1)S(1)}, u32[]{:S(2)}, u32[]{:S(2)}) %all-to-all-start) | async-done | bytes 3145760 | tf_op jit(solution)/shard_map/all_to_all | solution.py:361
  78.2 1.0 copy-done.1
  79.1 4.6 %all-to-all-start.1 = ((bf16[4,128,768]{2,1,0:T(8,128)(2,1)}), bf16[4,128,768]{2,1,0:T(8,128)(2,1)S(1)}, u32[]{:S(2)}, u32[]{:S(2)}) async-start(bf16[4,128,768]{2,1,0:T(8,128)(2,1)} %bitcast.17), calls=%async_computation.1 | async-start | bytes 1572864 | tf_op jit(solution)/shard_map/all_to_all | solution.py:372
  83.8 0.9 copy-done.2
  84.7 1.2 right_sums.1
  85.9 2.5 %collective-permute-start.7 = (bf16[128,256]{1,0:T(8,128)(2,1)S(1)}, bf16[128,256]{1,0:T(8,128)(2,1)S(1)}, u32[]{:S(2)}, u32[]{:S(2)}) collective-permute-start(bf16[128,256]{1,0:T(8,128)(2,1)S(1)} %get-tuple-element.31), channel_id=1, source_target_pairs={{0,128},{128,256},{256,384},{384,0},{1,129},{129,257},{257,385},{3... | collective-permute-start | bytes 196616 | tf_op jit(solution)/shard_map/ppermute | solution.py:24
  88.5 4.5 %collective-permute-start.8 = (bf16[128,256]{1,0:T(8,128)(2,1)S(1)}, bf16[128,256]{1,0:T(8,128)(2,1)S(1)}, u32[]{:S(2)}, u32[]{:S(2)}) collective-permute-start(bf16[128,256]{1,0:T(8,128)(2,1)S(1)} %get-tuple-element.32), channel_id=1, source_target_pairs={{0,384},{128,0},{256,128},{384,256},{1,385},{129,1},{257,129},{385... | collective-permute-start | bytes 196616 | tf_op jit(solution)/shard_map/ppermute | solution.py:24
  93.0 2.0 %collective-permute-start.9 = (bf16[128,256]{1,0:T(8,128)(2,1)S(1)}, bf16[128,256]{1,0:T(8,128)(2,1)S(1)}, u32[]{:S(2)}, u32[]{:S(2)}) collective-permute-start(bf16[128,256]{1,0:T(8,128)(2,1)S(1)} %get-tuple-element.33), channel_id=1, source_target_pairs={{0,256},{128,384},{256,0},{384,128},{1,257},{129,385},{257,1},{385... | collective-permute-start | bytes 196616 | tf_op jit(solution)/shard_map/ppermute | solution.py:24
  95.1 6.3 %input_part.2.rest_0_ = bf16[224,4096]{1,0:T(8,128)(2,1)} custom-call(s32[2]{0:T(128)S(1)} %pad_add_fusion.2.where, bf16[224,1024]{1,0:T(8,128)(2,1)S(1)} %copy-done, bf16[8,256,1024]{2,1,0:T(8,128)(2,1)} %bitcast.20), custom_call_target="tpu_custom_call" | custom-call | flops 939524096 | bytes 5111808 | tf_op jit(solution)/shard_map/input_part/pallas_call | solution.py:318
  103.1 11.7 %all-to-all-start.2 = ((bf16[16,8,1024]{2,1,0:T(8,128)(2,1)}), bf16[16,8,1024]{2,1,0:T(8,128)(2,1)S(1)}, u32[]{:S(2)}, u32[]{:S(2)}) async-start(bf16[16,8,1024]{2,1,0:T(8,128)(2,1)} %bitcast.15), calls=%async_computation.2 | async-start | bytes 524288 | tf_op jit(solution)/shard_map/all_to_all | solution.py:378
  114.8 6.3 %input_part.3 = bf16[224,4096]{1,0:T(8,128)(2,1)} custom-call(s32[2]{0:T(128)S(1)} %pad_add_fusion.where, bf16[224,1024]{1,0:T(8,128)(2,1)S(1)} %copy-done, bf16[8,256,1024]{2,1,0:T(8,128)(2,1)} %bitcast.21, bf16[224,4096]{1,0:T(8,128)(2,1)} %input_part.2.rest_0_), custom_call_target="tpu_custom_call", output_to_operand_aliasing={{}: (3, {})} | custom-call | flops 939524096 | bytes 5111808 | tf_op jit(solution)/shard_map/input_part/pallas_call | solution.py:318
  121.1 10.1 %all-to-all-done.2 = bf16[16,8,1024]{2,1,0:T(8,128)(2,1)S(1)} async-done(((bf16[16,8,1024]{2,1,0:T(8,128)(2,1)}), bf16[16,8,1024]{2,1,0:T(8,128)(2,1)S(1)}, u32[]{:S(2)}, u32[]{:S(2)}) %all-to-all-start.2) | async-done | bytes 262176 | tf_op jit(solution)/shard_map/all_to_all | solution.py:378
  (26 shorter events, 3.3 us)
Async XLA Ops:
  7.2 87.9 %all-gather.5.cloned.1.call-start = ((), (), s32[]{:S(2)}) async-start(), calls=%async_computation.4 | async-start | bytes 4718592 | tf_op jit(solution)/shard_map/all_gather | solution.py:354
  9.6 20.2 %collective-permute-start = (bf16[224,4096]{1,0:T(8,128)(2,1)}, bf16[224,4096]{1,0:T(8,128)(2,1)S(1)}, u32[]{:S(2)}, u32[]{:S(2)}) collective-permute-start(bf16[224,4096]{1,0:T(8,128)(2,1)} %acts.1), channel_id=1, source_target_pairs={{0,1},{1,0},{2,3},{3,2},{4,5},{5,4},{6,7},{7,6},{8,9},{9,8},{10,11... | collective-permute-start | bytes 5505032 | tf_op jit(solution)/shard_map/ppermute | solution.py:24
  11.5 18.2 %collective-permute-start.1 = (bf16[224,1024]{1,0:T(8,128)(2,1)}, bf16[224,1024]{1,0:T(8,128)(2,1)S(1)}, u32[]{:S(2)}, u32[]{:S(2)}) collective-permute-start(bf16[224,1024]{1,0:T(8,128)(2,1)} %grads.3), channel_id=1, source_target_pairs={{0,1},{1,0},{2,3},{3,2},{4,5},{5,4},{6,7},{7,6},{8,9},{9,8},{10,11... | collective-permute-start | bytes 1376264 | tf_op jit(solution)/shard_map/ppermute | solution.py:24
  13.9 26.1 %collective-permute-start.2 = (bf16[128,1024]{1,0:T(8,128)(2,1)S(1)}, bf16[128,1024]{1,0:T(8,128)(2,1)}, u32[]{:S(2)}, u32[]{:S(2)}) collective-permute-start(bf16[128,1024]{1,0:T(8,128)(2,1)S(1)} %get-tuple-element.23), channel_id=1, source_target_pairs={{0,8},{1,9},{2,10},{3,11},{4,12},{5,13},{6,14},{7,15},{16,24},{17,... | collective-permute-start | bytes 786440 | tf_op jit(solution)/shard_map/ppermute | solution.py:38
  35.7 41.7 %all-to-all-start = ((bf16[4,8,64,768]{3,2,1,0:T(8,128)(2,1)}), bf16[4,8,64,768]{3,2,1,0:T(8,128)(2,1)S(1)}, u32[]{:S(2)}, u32[]{:S(2)}) async-start(bf16[4,8,64,768]{3,2,1,0:T(8,128)(2,1)} %get-tuple-element.21), calls=%async_computation | async-start | bytes 6291456 | tf_op jit(solution)/shard_map/all_to_all | solution.py:361
  40.0 74.8 %all-gather.3.cloned.1.call-start = ((), (), s32[]{:S(2)}) async-start(), calls=%async_computation.3 | async-start | bytes 4718592 | tf_op jit(solution)/shard_map/all_gather | solution.py:365
  40.1 22.1 %collective-permute-start.3 = (bf16[128,1024]{1,0:T(8,128)(2,1)}, bf16[128,1024]{1,0:T(8,128)(2,1)S(1)}, u32[]{:S(2)}, u32[]{:S(2)}) collective-permute-start(bf16[128,1024]{1,0:T(8,128)(2,1)} %collective-permute-done.2), channel_id=1, source_target_pairs={{0,16},{1,17},{2,18},{3,19},{4,20},{5,21},{6,22},{7,23},{16,0},{17... | collective-permute-start | bytes 786440 | tf_op jit(solution)/shard_map/ppermute | solution.py:38
  64.1 19.7 %collective-permute-start.4 = (bf16[8,64,256]{2,1,0:T(8,128)(2,1)}, bf16[8,64,256]{2,1,0:T(8,128)(2,1)S(1)}, u32[]{:S(2)}, u32[]{:S(2)}) collective-permute-start(bf16[8,64,256]{2,1,0:T(8,128)(2,1)} %get-tuple-element.27), channel_id=1, source_target_pairs={{0,2},{2,4},{4,6},{6,0},{1,3},{3,5},{5,7},{7,1},{8,10},{10,12},{12... | collective-permute-start | bytes 786440 | tf_op jit(solution)/shard_map/ppermute | solution.py:24
  66.2 17.6 %collective-permute-start.5 = (bf16[8,64,256]{2,1,0:T(8,128)(2,1)}, bf16[8,64,256]{2,1,0:T(8,128)(2,1)}, u32[]{:S(2)}, u32[]{:S(2)}) collective-permute-start(bf16[8,64,256]{2,1,0:T(8,128)(2,1)} %get-tuple-element.28), channel_id=1, source_target_pairs={{0,6},{2,0},{4,2},{6,4},{1,7},{3,1},{5,3},{7,5},{8,14},{10,8},{12,... | collective-permute-start | bytes 786440 | tf_op jit(solution)/shard_map/ppermute | solution.py:24
  69.9 13.8 %collective-permute-start.6 = (bf16[8,64,256]{2,1,0:T(8,128)(2,1)}, bf16[8,64,256]{2,1,0:T(8,128)(2,1)}, u32[]{:S(2)}, u32[]{:S(2)}) collective-permute-start(bf16[8,64,256]{2,1,0:T(8,128)(2,1)} %get-tuple-element.29), channel_id=1, source_target_pairs={{0,4},{2,6},{4,0},{6,2},{1,5},{3,7},{5,1},{7,3},{8,12},{10,14},{12... | collective-permute-start | bytes 786440 | tf_op jit(solution)/shard_map/ppermute | solution.py:24
  78.1 1.0 copy-start.1
  79.1 23.1 %all-to-all-start.1 = ((bf16[4,128,768]{2,1,0:T(8,128)(2,1)}), bf16[4,128,768]{2,1,0:T(8,128)(2,1)S(1)}, u32[]{:S(2)}, u32[]{:S(2)}) async-start(bf16[4,128,768]{2,1,0:T(8,128)(2,1)} %bitcast.17), calls=%async_computation.1 | async-start | bytes 1572864 | tf_op jit(solution)/shard_map/all_to_all | solution.py:372
  83.8 1.0 copy-start.2
  84.7 10.3 %copy-start = (bf16[224,1024]{1,0:T(8,128)(2,1)S(1)}, bf16[224,1024]{1,0:T(8,128)(2,1)}, u32[]{:S(2)}) copy-start(bf16[224,1024]{1,0:T(8,128)(2,1)} %grads.3) | copy-start | bytes 1376260
  85.9 16.3 %collective-permute-start.7 = (bf16[128,256]{1,0:T(8,128)(2,1)S(1)}, bf16[128,256]{1,0:T(8,128)(2,1)S(1)}, u32[]{:S(2)}, u32[]{:S(2)}) collective-permute-start(bf16[128,256]{1,0:T(8,128)(2,1)S(1)} %get-tuple-element.31), channel_id=1, source_target_pairs={{0,128},{128,256},{256,384},{384,0},{1,129},{129,257},{257,385},{3... | collective-permute-start | bytes 196616 | tf_op jit(solution)/shard_map/ppermute | solution.py:24
  88.5 13.7 %collective-permute-start.8 = (bf16[128,256]{1,0:T(8,128)(2,1)S(1)}, bf16[128,256]{1,0:T(8,128)(2,1)S(1)}, u32[]{:S(2)}, u32[]{:S(2)}) collective-permute-start(bf16[128,256]{1,0:T(8,128)(2,1)S(1)} %get-tuple-element.32), channel_id=1, source_target_pairs={{0,384},{128,0},{256,128},{384,256},{1,385},{129,1},{257,129},{385... | collective-permute-start | bytes 196616 | tf_op jit(solution)/shard_map/ppermute | solution.py:24
  93.0 9.2 %collective-permute-start.9 = (bf16[128,256]{1,0:T(8,128)(2,1)S(1)}, bf16[128,256]{1,0:T(8,128)(2,1)S(1)}, u32[]{:S(2)}, u32[]{:S(2)}) collective-permute-start(bf16[128,256]{1,0:T(8,128)(2,1)S(1)} %get-tuple-element.33), channel_id=1, source_target_pairs={{0,256},{128,384},{256,0},{384,128},{1,257},{129,385},{257,1},{385... | collective-permute-start | bytes 196616 | tf_op jit(solution)/shard_map/ppermute | solution.py:24
  103.1 28.2 %all-to-all-start.2 = ((bf16[16,8,1024]{2,1,0:T(8,128)(2,1)}), bf16[16,8,1024]{2,1,0:T(8,128)(2,1)S(1)}, u32[]{:S(2)}, u32[]{:S(2)}) async-start(bf16[16,8,1024]{2,1,0:T(8,128)(2,1)} %bitcast.15), calls=%async_computation.2 | async-start | bytes 524288 | tf_op jit(solution)/shard_map/all_to_all | solution.py:378
Sparse Core Ops, SparseCore 0:
  10.7 42.0 all-gather.4
  64.1 46.3 all-gather.2

commit v8 on v7

--- a/solution.py
+++ b/solution.py
@@ -177,8 +177,9 @@
     )(where, acts, acts_in, grads, grads_in)
 
 
-def left_kernel(parts, out, held, sems):
+def left_kernel(parts, out, held, result, sems, out_sems):
     pieces, terms, rows, columns = held.shape
+    stores = []
     copies = [
         pltpu.make_async_copy(parts.at[:, pl.ds(q * rows, rows)], held.at[q], sems.at[q])
         for q in range(pieces)
@@ -189,7 +190,13 @@
         if q + AHEAD < pieces:
             copies[q + AHEAD].start()
         copy.wait()
-        out[q * rows : (q + 1) * rows] = total_of([held[q, k] for k in range(terms)], out.dtype)
+        result[q] = total_of([held[q, k] for k in range(terms)], out.dtype)
+        stores.append(
+            pltpu.make_async_copy(result.at[q], out.at[pl.ds(q * rows, rows)], out_sems.at[q])
+        )
+        stores[-1].start()
+    for copy in stores:
+        copy.wait()
 
 
 def left_sums(parts):
@@ -197,11 +204,13 @@
     pieces = 4
     return pl.pallas_call(
         left_kernel,
-        out_shape=jax.ShapeDtypeStruct((rows, columns), parts.dtype),
+        out_shape=pltpu.HBM((rows, columns), parts.dtype),
         in_specs=[pl.BlockSpec(memory_space=pl.ANY)],
-        out_specs=pl.BlockSpec(memory_space=pltpu.VMEM),
+        out_specs=pl.BlockSpec(memory_space=pl.ANY),
         scratch_shapes=[
             pltpu.VMEM((pieces, terms, rows // pieces, columns), parts.dtype),
+            pltpu.VMEM((pieces, rows // pieces, columns), parts.dtype),
+            pltpu.SemaphoreType.DMA((pieces,)),
             pltpu.SemaphoreType.DMA((pieces,)),
         ],
         compiler_params=pltpu.CompilerParams(vmem_limit_bytes=16 * MIB),
@@ -213,23 +222,34 @@
 
 
 def right_kernel(*refs):
-    count = len(refs) // 2
-    parts, outs = refs[:count], refs[count:]
+    held, sems = refs[-2:]
+    count = held.shape[0]
+    parts, outs = refs[:count], refs[count:-2]
     rows = outs[0].shape[0]
+    copies = [
+        pltpu.make_async_copy(part, held.at[k], sems.at[k]) for k, part in enumerate(parts)
+    ]
+    for copy in copies:
+        copy.start()
+    for copy in copies:
+        copy.wait()
     for k, out in enumerate(outs):
         run = slice(k * rows, (k + 1) * rows)
-        out[...] = total_of([part[run] for part in parts], out.dtype)
+        out[...] = total_of([held[i, run] for i in range(count)], out.dtype)
 
 
 def right_sums(parts):
     rows, columns = parts[0].shape
-    vmem = pl.BlockSpec(memory_space=pltpu.VMEM)
     count = len(parts)
     return pl.pallas_call(
         right_kernel,
         out_shape=[jax.ShapeDtypeStruct((rows // count, columns), parts[0].dtype)] * count,
-        in_specs=[vmem] * count,
-        out_specs=[vmem] * count,
+        in_specs=[pl.BlockSpec(memory_space=pl.ANY)] * count,
+        out_specs=[pl.BlockSpec(memory_space=pltpu.VMEM)] * count,
+        scratch_shapes=[
+            pltpu.VMEM((count, rows, columns), parts[0].dtype),
+            pltpu.SemaphoreType.DMA((count,)),
+        ],
         compiler_params=pltpu.CompilerParams(vmem_limit_bytes=16 * MIB),
         cost_estimate=pl.CostEstimate(
             flops=CHAIN, bytes_accessed=2 * count * rows * columns, transcendentals=0
@@ -362,20 +382,19 @@
     right = [right[0]] + [shift(right[k], "y", k) for k in (1, 3, 2)]
 
     swapped = chip_shift(fetched, lambda i, z: (i, z ^ 1))
-    other_half = lax.all_gather(
-        jnp.concatenate([fetched, swapped], axis=0), ("y", "c"), axis=0, tiled=True
-    )
-
+    both = jnp.concatenate([fetched, swapped], axis=0)
+    both, *_ = lax.optimization_barrier((both, right[1], right[2]))
+    other_half = lax.all_gather(both, ("y", "c"), axis=0, tiled=True)
+
+    right = right_sums([part.reshape(NX * chunk, columns - LEFT) for part in right])
     left = left_sums(left.reshape(NX, NY * chunk, LEFT)).reshape(NY, chunk, LEFT)
-    right = right_sums([part.reshape(NX * chunk, columns - LEFT) for part in right])
-    grads_later, _ = lax.optimization_barrier((grads_out, left))
     left = lax.all_to_all(left, "y", split_axis=0, concat_axis=0, tiled=True)
     right = [right[0]] + [shift(right[k], "x", k) for k in (1, 3, 2)]
+    rows = joined_sums(left, right).reshape(NZ, 8, columns)
+    grads_later, _ = lax.optimization_barrier((grads_out, rows))
+    rows = lax.all_to_all(rows, ("zh", "zl"), split_axis=0, concat_axis=0, tiled=True)
     own_half = own_half.reshape(groups, shard_rows, columns)
     grad_input = input_part(zh * groups, 0 * odd, grads_later, own_half, width)
-    grad_input, left = lax.optimization_barrier((grad_input, left))
-    rows = joined_sums(left, right).reshape(NZ, 8, columns)
-    rows = lax.all_to_all(rows, ("zh", "zl"), split_axis=0, concat_axis=0, tiled=True)
     other_half = other_half.reshape(groups, shard_rows, columns)
     grad_input = input_part(
         (1 - zh) * groups, odd, grads_later, other_half, width, grad_input

time: 139 us -> 136 us (0.978)
  the two profiles are of different devices: /device:TPU:24 before, /device:TPU:32 now
where the time goes in v8:
time: 136 us; the launch traced here: 135 us
  starting transfers between devices  59.8 us (44%)
  waiting for transfers between devices  32.9 us (24%)
  Pallas kernels  24.3 us (18%)
  between operations  14.2 us (10%)
  other arithmetic  2.67 us (2%)
    ppermute x8, starting transfers between devices, shift(): lax.ppermute(value, axis, [(i, (i + step) % size) for i in range(size)])  22.1 us
    ppermute x2, starting transfers between devices, chip_shift(): return lax.ppermute(value, AXES, pairs)  16.7 us
    ppermute x2, waiting for transfers between devices, chip_shift(): return lax.ppermute(value, AXES, pairs)  14.1 us
    pallas_call x2, Pallas kernels, input_part(): pl.pallas_call(input_kernel, out_shape=jax.ShapeDtypeStruct((tokens, widt...  12.6 us
    all_to_all x1, starting transfers between devices, shards(): lax.all_to_all(rows, ('zh', 'zl'), split_axis=0, concat_axis=0, tiled=True)  12.1 us
    ppermute x8, waiting for transfers between devices, shift(): lax.ppermute(value, axis, [(i, (i + step) % size) for i in range(size)])  11.8 us
    pallas_call x1, Pallas kernels, partials(): pl.pallas_call(functools.partial(partial_kernel, factor), out_shape=[pltp...  5.94 us
    all_to_all x1, waiting for transfers between devices, shards(): left = lax.all_to_all(left, 'x', split_axis=0, concat_axis=0, tiled=True)  4.69 us
  transfers between devices with their start and end apart: 15, of which 8 were waited for; matrix products, arithmetic and copies ran while one was open for 1% of the time, Pallas kernels for 16%

profile of v8, /device:TPU:32, one launch (start us, length us, event | category | flops | bytes accessed | tf_op | source)
XLA Modules:
  0.0 134.8 jit_solution(5653082192338396705)
XLA Ops:
  7.2 2.4 %weights.1 = (bf16[256,1024]{1,0:T(8,128)(2,1)}, bf16[128,1024]{1,0:T(8,128)(2,1)S(1)}) custom-call(s32[1]{0:T(128)} %bitcast.1.odd, bf16[256,1024]{1,0:T(8,128)(2,1)} %quant.1, f32[8,256]{1,0:T(8,128)} %bitcast.22), custom_call_target="tpu_custom_call" | custom-call | flops 262144 | bytes 1048576 | tf_op jit(solution)/shard_map/weights/pallas_call | solution.py:65
  9.6 1.9 %collective-permute-start = (bf16[224,4096]{1,0:T(8,128)(2,1)}, bf16[224,4096]{1,0:T(8,128)(2,1)S(1)}, u32[]{:S(2)}, u32[]{:S(2)}) collective-permute-start(bf16[224,4096]{1,0:T(8,128)(2,1)} %acts.1), channel_id=1, source_target_pairs={{0,1},{1,0},{2,3},{3,2},{4,5},{5,4},{6,7},{7,6},{8,9},{9,8},{10,11... | collective-permute-start | bytes 5505032 | tf_op jit(solution)/shard_map/ppermute | solution.py:24
  11.5 2.4 %collective-permute-start.1 = (bf16[224,1024]{1,0:T(8,128)(2,1)}, bf16[224,1024]{1,0:T(8,128)(2,1)S(1)}, u32[]{:S(2)}, u32[]{:S(2)}) collective-permute-start(bf16[224,1024]{1,0:T(8,128)(2,1)} %grads.3), channel_id=1, source_target_pairs={{0,1},{1,0},{2,3},{3,2},{4,5},{5,4},{6,7},{7,6},{8,9},{9,8},{10,11... | collective-permute-start | bytes 1376264 | tf_op jit(solution)/shard_map/ppermute | solution.py:24
  13.9 14.8 %collective-permute-start.8 = (bf16[128,1024]{1,0:T(8,128)(2,1)S(1)}, bf16[128,1024]{1,0:T(8,128)(2,1)}, u32[]{:S(2)}, u32[]{:S(2)}) collective-permute-start(bf16[128,1024]{1,0:T(8,128)(2,1)S(1)} %get-tuple-element.30), channel_id=1, source_target_pairs={{0,8},{1,9},{2,10},{3,11},{4,12},{5,13},{6,14},{7,15},{16,24},{17,... | collective-permute-start | bytes 786440 | tf_op jit(solution)/shard_map/ppermute | solution.py:38
  28.9 5.9 %partials.1 = (bf16[4,8,64,768]{3,2,1,0:T(8,128)(2,1)}, bf16[8,64,256]{2,1,0:T(8,128)(2,1)}, bf16[8,64,256]{2,1,0:T(8,128)(2,1)}, bf16[8,64,256]{2,1,0:T(8,128)(2,1)}, bf16[8,64,256]{2,1,0:T(8,128)(2,1)}) custom-call(s32[3]{0:T(128)S(1)} %pad_add_fusion.1.where, bf16[224,4096]{1,0:T(8,128)(2,1)} %acts.1, bf16[224,4096]{1,0:T(8,128)(2,1)S(1)} %collective-permute-done.acts_in, ...), custom_call_target="tpu_custom_call" | custom-call | flops 1879048192 | bytes 7864320 | tf_op jit(solution)/shard_map/partials/pallas_call | solution.py:156
  34.8 4.3 %all-to-all-start = ((bf16[4,8,64,768]{3,2,1,0:T(8,128)(2,1)}), bf16[4,8,64,768]{3,2,1,0:T(8,128)(2,1)S(1)}, u32[]{:S(2)}, u32[]{:S(2)}) async-start(bf16[4,8,64,768]{3,2,1,0:T(8,128)(2,1)} %get-tuple-element.20), calls=%async_computation | async-start | bytes 6291456 | tf_op jit(solution)/shard_map/all_to_all | solution.py:381
  39.1 13.3 %collective-permute-done.8 = bf16[128,1024]{1,0:T(8,128)(2,1)} collective-permute-done((bf16[128,1024]{1,0:T(8,128)(2,1)S(1)}, bf16[128,1024]{1,0:T(8,128)(2,1)}, u32[]{:S(2)}, u32[]{:S(2)}) %collective-permute-start.8) | collective-permute-done | bytes 262176 | tf_op jit(solution)/shard_map/ppermute | solution.py:38
  52.4 1.9 %collective-permute-start.9 = (bf16[128,1024]{1,0:T(8,128)(2,1)}, bf16[128,1024]{1,0:T(8,128)(2,1)S(1)}, u32[]{:S(2)}, u32[]{:S(2)}) collective-permute-start(bf16[128,1024]{1,0:T(8,128)(2,1)} %collective-permute-done.8), channel_id=1, source_target_pairs={{0,16},{1,17},{2,18},{3,19},{4,20},{5,21},{6,22},{7,23},{16,0},{17... | collective-permute-start | bytes 786440 | tf_op jit(solution)/shard_map/ppermute | solution.py:38
  54.4 4.9 %collective-permute-start.3 = (bf16[8,64,256]{2,1,0:T(8,128)(2,1)}, bf16[8,64,256]{2,1,0:T(8,128)(2,1)S(1)}, u32[]{:S(2)}, u32[]{:S(2)}) collective-permute-start(bf16[8,64,256]{2,1,0:T(8,128)(2,1)} %get-tuple-element.23), channel_id=1, source_target_pairs={{0,6},{2,0},{4,2},{6,4},{1,7},{3,1},{5,3},{7,5},{8,14},{10,8},{12,... | collective-permute-start | bytes 786440 | tf_op jit(solution)/shard_map/ppermute | solution.py:24
  59.3 1.9 %collective-permute-start.2 = (bf16[8,64,256]{2,1,0:T(8,128)(2,1)}, bf16[8,64,256]{2,1,0:T(8,128)(2,1)}, u32[]{:S(2)}, u32[]{:S(2)}) collective-permute-start(bf16[8,64,256]{2,1,0:T(8,128)(2,1)} %get-tuple-element.22), channel_id=1, source_target_pairs={{0,2},{2,4},{4,6},{6,0},{1,3},{3,5},{5,7},{7,1},{8,10},{10,12},{12... | collective-permute-start | bytes 786440 | tf_op jit(solution)/shard_map/ppermute | solution.py:24
  62.0 1.8 %pad_maximum_fusion = bf16[256,1024]{1,0:T(8,128)(2,1)} fusion(bf16[128,1024]{1,0:T(8,128)(2,1)S(1)} %collective-permute-done.9, bf16[128,1024]{1,0:T(8,128)(2,1)} %collective-permute-done.8), kind=kLoop, calls=%fused_computation | loop fusion | flops 1048576 | bytes 1048576 | tf_op jit(solution)/shard_map/concatenate | solution.py:385
  64.6 5.3 %collective-permute-done.2 = bf16[8,64,256]{2,1,0:T(8,128)(2,1)} collective-permute-done((bf16[8,64,256]{2,1,0:T(8,128)(2,1)}, bf16[8,64,256]{2,1,0:T(8,128)(2,1)}, u32[]{:S(2)}, u32[]{:S(2)}) %collective-permute-start.2) | collective-permute-done | bytes 262176 | tf_op jit(solution)/shard_map/ppermute | solution.py:24
  69.9 1.9 %collective-permute-start.4 = (bf16[8,64,256]{2,1,0:T(8,128)(2,1)}, bf16[8,64,256]{2,1,0:T(8,128)(2,1)}, u32[]{:S(2)}, u32[]{:S(2)}) collective-permute-start(bf16[8,64,256]{2,1,0:T(8,128)(2,1)} %get-tuple-element.24), channel_id=1, source_target_pairs={{0,4},{2,6},{4,0},{6,2},{1,5},{3,7},{5,1},{7,3},{8,12},{10,14},{12... | collective-permute-start | bytes 786440 | tf_op jit(solution)/shard_map/ppermute | solution.py:24
  71.9 4.7 %all-to-all-done = bf16[4,8,64,768]{3,2,1,0:T(8,128)(2,1)S(1)} async-done(((bf16[4,8,64,768]{3,2,1,0:T(8,128)(2,1)}), bf16[4,8,64,768]{3,2,1,0:T(8,128)(2,1)S(1)}, u32[]{:S(2)}, u32[]{:S(2)}) %all-to-all-start) | async-done | bytes 3145760 | tf_op jit(solution)/shard_map/all_to_all | solution.py:381
  76.6 1.4 %left_sums.1 = bf16[512,768]{1,0:T(8,128)(2,1)} custom-call(bf16[4,512,768]{2,1,0:T(8,128)(2,1)S(1)} %bitcast.16), custom_call_target="tpu_custom_call" | custom-call | flops 16000000000 | bytes 3145728 | tf_op jit(solution)/shard_map/left_sums/pallas_call | solution.py:205
  77.9 4.5 %all-to-all-start.1 = ((bf16[4,128,768]{2,1,0:T(8,128)(2,1)}), bf16[4,128,768]{2,1,0:T(8,128)(2,1)S(1)}, u32[]{:S(2)}, u32[]{:S(2)}) async-start(bf16[4,128,768]{2,1,0:T(8,128)(2,1)} %bitcast.21), calls=%async_computation.1 | async-start | bytes 1572864 | tf_op jit(solution)/shard_map/all_to_all | solution.py:391
  84.6 2.5 %collective-permute-start.5 = (bf16[128,256]{1,0:T(8,128)(2,1)S(1)}, bf16[128,256]{1,0:T(8,128)(2,1)S(1)}, u32[]{:S(2)}, u32[]{:S(2)}) collective-permute-start(bf16[128,256]{1,0:T(8,128)(2,1)S(1)} %get-tuple-element.26), channel_id=1, source_target_pairs={{0,128},{128,256},{256,384},{384,0},{1,129},{129,257},{257,385},{3... | collective-permute-start | bytes 196616 | tf_op jit(solution)/shard_map/ppermute | solution.py:24
  87.1 4.6 %collective-permute-start.6 = (bf16[128,256]{1,0:T(8,128)(2,1)S(1)}, bf16[128,256]{1,0:T(8,128)(2,1)S(1)}, u32[]{:S(2)}, u32[]{:S(2)}) collective-permute-start(bf16[128,256]{1,0:T(8,128)(2,1)S(1)} %get-tuple-element.27), channel_id=1, source_target_pairs={{0,384},{128,0},{256,128},{384,256},{1,385},{129,1},{257,129},{385... | collective-permute-start | bytes 196616 | tf_op jit(solution)/shard_map/ppermute | solution.py:24
  91.7 1.9 %collective-permute-start.7 = (bf16[128,256]{1,0:T(8,128)(2,1)S(1)}, bf16[128,256]{1,0:T(8,128)(2,1)S(1)}, u32[]{:S(2)}, u32[]{:S(2)}) collective-permute-start(bf16[128,256]{1,0:T(8,128)(2,1)S(1)} %get-tuple-element.28), channel_id=1, source_target_pairs={{0,256},{128,384},{256,0},{384,128},{1,257},{129,385},{257,1},{385... | collective-permute-start | bytes 196616 | tf_op jit(solution)/shard_map/ppermute | solution.py:24
  93.7 5.7 %collective-permute-done.7.refs_3_ = bf16[128,256]{1,0:T(8,128)(2,1)S(1)} collective-permute-done((bf16[128,256]{1,0:T(8,128)(2,1)S(1)}, bf16[128,256]{1,0:T(8,128)(2,1)S(1)}, u32[]{:S(2)}, u32[]{:S(2)}) %collective-permute-start.7) | collective-permute-done | bytes 65568 | tf_op jit(solution)/shard_map/ppermute | solution.py:24
  100.2 12.1 %all-to-all-start.2 = ((bf16[16,8,1024]{2,1,0:T(8,128)(2,1)}), bf16[16,8,1024]{2,1,0:T(8,128)(2,1)S(1)}, u32[]{:S(2)}, u32[]{:S(2)}) async-start(bf16[16,8,1024]{2,1,0:T(8,128)(2,1)} %bitcast.12), calls=%async_computation.2 | async-start | bytes 524288 | tf_op jit(solution)/shard_map/all_to_all | solution.py:395
  112.5 6.3 %input_part.2.rest_0_ = bf16[224,4096]{1,0:T(8,128)(2,1)} custom-call(s32[2]{0:T(128)S(1)} %pad_add_fusion.2.where, bf16[224,1024]{1,0:T(8,128)(2,1)S(1)} %copy-done, bf16[8,256,1024]{2,1,0:T(8,128)(2,1)} %bitcast.19), custom_call_target="tpu_custom_call" | custom-call | flops 939524096 | bytes 5111808 | tf_op jit(solution)/shard_map/input_part/pallas_call | solution.py:338
  118.8 6.3 %input_part.3 = bf16[224,4096]{1,0:T(8,128)(2,1)} custom-call(s32[2]{0:T(128)S(1)} %pad_add_fusion.where, bf16[224,1024]{1,0:T(8,128)(2,1)S(1)} %copy-done, bf16[8,256,1024]{2,1,0:T(8,128)(2,1)} %bitcast.20, bf16[224,4096]{1,0:T(8,128)(2,1)} %input_part.2.rest_0_), custom_call_target="tpu_custom_call", output_to_operand_aliasing={{}: (3, {})} | custom-call | flops 939524096 | bytes 5111808 | tf_op jit(solution)/shard_map/input_part/pallas_call | solution.py:338
  125.1 2.2 %all-to-all-done.2 = bf16[16,8,1024]{2,1,0:T(8,128)(2,1)S(1)} async-done(((bf16[16,8,1024]{2,1,0:T(8,128)(2,1)}), bf16[16,8,1024]{2,1,0:T(8,128)(2,1)S(1)}, u32[]{:S(2)}, u32[]{:S(2)}) %all-to-all-start.2) | async-done | bytes 262176 | tf_op jit(solution)/shard_map/all_to_all | solution.py:395
  (24 shorter events, 5.6 us)
Async XLA Ops:
  7.2 105.3 %all-gather.5.cloned.1.call-start = ((), (), s32[]{:S(2)}) async-start(), calls=%async_computation.4 | async-start | bytes 4718592 | tf_op jit(solution)/shard_map/all_gather | solution.py:374
  9.6 19.3 %collective-permute-start = (bf16[224,4096]{1,0:T(8,128)(2,1)}, bf16[224,4096]{1,0:T(8,128)(2,1)S(1)}, u32[]{:S(2)}, u32[]{:S(2)}) collective-permute-start(bf16[224,4096]{1,0:T(8,128)(2,1)} %acts.1), channel_id=1, source_target_pairs={{0,1},{1,0},{2,3},{3,2},{4,5},{5,4},{6,7},{7,6},{8,9},{9,8},{10,11... | collective-permute-start | bytes 5505032 | tf_op jit(solution)/shard_map/ppermute | solution.py:24
  11.5 17.3 %collective-permute-start.1 = (bf16[224,1024]{1,0:T(8,128)(2,1)}, bf16[224,1024]{1,0:T(8,128)(2,1)S(1)}, u32[]{:S(2)}, u32[]{:S(2)}) collective-permute-start(bf16[224,1024]{1,0:T(8,128)(2,1)} %grads.3), channel_id=1, source_target_pairs={{0,1},{1,0},{2,3},{3,2},{4,5},{5,4},{6,7},{7,6},{8,9},{9,8},{10,11... | collective-permute-start | bytes 1376264 | tf_op jit(solution)/shard_map/ppermute | solution.py:24
  13.9 38.5 %collective-permute-start.8 = (bf16[128,1024]{1,0:T(8,128)(2,1)S(1)}, bf16[128,1024]{1,0:T(8,128)(2,1)}, u32[]{:S(2)}, u32[]{:S(2)}) collective-permute-start(bf16[128,1024]{1,0:T(8,128)(2,1)S(1)} %get-tuple-element.30), channel_id=1, source_target_pairs={{0,8},{1,9},{2,10},{3,11},{4,12},{5,13},{6,14},{7,15},{16,24},{17,... | collective-permute-start | bytes 786440 | tf_op jit(solution)/shard_map/ppermute | solution.py:38
  34.8 41.7 %all-to-all-start = ((bf16[4,8,64,768]{3,2,1,0:T(8,128)(2,1)}), bf16[4,8,64,768]{3,2,1,0:T(8,128)(2,1)S(1)}, u32[]{:S(2)}, u32[]{:S(2)}) async-start(bf16[4,8,64,768]{3,2,1,0:T(8,128)(2,1)} %get-tuple-element.20), calls=%async_computation | async-start | bytes 6291456 | tf_op jit(solution)/shard_map/all_to_all | solution.py:381
  39.1 79.7 %all-gather.3.cloned.1.call-start = ((), (), s32[]{:S(2)}) async-start(), calls=%async_computation.3 | async-start | bytes 4718592 | tf_op jit(solution)/shard_map/all_gather | solution.py:387
  52.4 9.6 %collective-permute-start.9 = (bf16[128,1024]{1,0:T(8,128)(2,1)}, bf16[128,1024]{1,0:T(8,128)(2,1)S(1)}, u32[]{:S(2)}, u32[]{:S(2)}) collective-permute-start(bf16[128,1024]{1,0:T(8,128)(2,1)} %collective-permute-done.8), channel_id=1, source_target_pairs={{0,16},{1,17},{2,18},{3,19},{4,20},{5,21},{6,22},{7,23},{16,0},{17... | collective-permute-start | bytes 786440 | tf_op jit(solution)/shard_map/ppermute | solution.py:38
  54.4 10.2 %collective-permute-start.3 = (bf16[8,64,256]{2,1,0:T(8,128)(2,1)}, bf16[8,64,256]{2,1,0:T(8,128)(2,1)S(1)}, u32[]{:S(2)}, u32[]{:S(2)}) collective-permute-start(bf16[8,64,256]{2,1,0:T(8,128)(2,1)} %get-tuple-element.23), channel_id=1, source_target_pairs={{0,6},{2,0},{4,2},{6,4},{1,7},{3,1},{5,3},{7,5},{8,14},{10,8},{12,... | collective-permute-start | bytes 786440 | tf_op jit(solution)/shard_map/ppermute | solution.py:24
  59.3 10.6 %collective-permute-start.2 = (bf16[8,64,256]{2,1,0:T(8,128)(2,1)}, bf16[8,64,256]{2,1,0:T(8,128)(2,1)}, u32[]{:S(2)}, u32[]{:S(2)}) collective-permute-start(bf16[8,64,256]{2,1,0:T(8,128)(2,1)} %get-tuple-element.22), channel_id=1, source_target_pairs={{0,2},{2,4},{4,6},{6,0},{1,3},{3,5},{5,7},{7,1},{8,10},{10,12},{12... | collective-permute-start | bytes 786440 | tf_op jit(solution)/shard_map/ppermute | solution.py:24
  69.9 12.5 %collective-permute-start.4 = (bf16[8,64,256]{2,1,0:T(8,128)(2,1)}, bf16[8,64,256]{2,1,0:T(8,128)(2,1)}, u32[]{:S(2)}, u32[]{:S(2)}) collective-permute-start(bf16[8,64,256]{2,1,0:T(8,128)(2,1)} %get-tuple-element.24), channel_id=1, source_target_pairs={{0,4},{2,6},{4,0},{6,2},{1,5},{3,7},{5,1},{7,3},{8,12},{10,14},{12... | collective-permute-start | bytes 786440 | tf_op jit(solution)/shard_map/ppermute | solution.py:24
  77.9 21.4 %all-to-all-start.1 = ((bf16[4,128,768]{2,1,0:T(8,128)(2,1)}), bf16[4,128,768]{2,1,0:T(8,128)(2,1)S(1)}, u32[]{:S(2)}, u32[]{:S(2)}) async-start(bf16[4,128,768]{2,1,0:T(8,128)(2,1)} %bitcast.21), calls=%async_computation.1 | async-start | bytes 1572864 | tf_op jit(solution)/shard_map/all_to_all | solution.py:391
  82.5 1.0 copy-start.1
  84.6 9.0 %collective-permute-start.5 = (bf16[128,256]{1,0:T(8,128)(2,1)S(1)}, bf16[128,256]{1,0:T(8,128)(2,1)S(1)}, u32[]{:S(2)}, u32[]{:S(2)}) collective-permute-start(bf16[128,256]{1,0:T(8,128)(2,1)S(1)} %get-tuple-element.26), channel_id=1, source_target_pairs={{0,128},{128,256},{256,384},{384,0},{1,129},{129,257},{257,385},{3... | collective-permute-start | bytes 196616 | tf_op jit(solution)/shard_map/ppermute | solution.py:24
  87.1 6.6 %collective-permute-start.6 = (bf16[128,256]{1,0:T(8,128)(2,1)S(1)}, bf16[128,256]{1,0:T(8,128)(2,1)S(1)}, u32[]{:S(2)}, u32[]{:S(2)}) collective-permute-start(bf16[128,256]{1,0:T(8,128)(2,1)S(1)} %get-tuple-element.27), channel_id=1, source_target_pairs={{0,384},{128,0},{256,128},{384,256},{1,385},{129,1},{257,129},{385... | collective-permute-start | bytes 196616 | tf_op jit(solution)/shard_map/ppermute | solution.py:24
  91.7 7.7 %collective-permute-start.7 = (bf16[128,256]{1,0:T(8,128)(2,1)S(1)}, bf16[128,256]{1,0:T(8,128)(2,1)S(1)}, u32[]{:S(2)}, u32[]{:S(2)}) collective-permute-start(bf16[128,256]{1,0:T(8,128)(2,1)S(1)} %get-tuple-element.28), channel_id=1, source_target_pairs={{0,256},{128,384},{256,0},{384,128},{1,257},{129,385},{257,1},{385... | collective-permute-start | bytes 196616 | tf_op jit(solution)/shard_map/ppermute | solution.py:24
  99.4 13.1 %copy-start = (bf16[224,1024]{1,0:T(8,128)(2,1)S(1)}, bf16[224,1024]{1,0:T(8,128)(2,1)}, u32[]{:S(2)}) copy-start(bf16[224,1024]{1,0:T(8,128)(2,1)} %grads.3) | copy-start | bytes 1376260
  100.2 27.1 %all-to-all-start.2 = ((bf16[16,8,1024]{2,1,0:T(8,128)(2,1)}), bf16[16,8,1024]{2,1,0:T(8,128)(2,1)S(1)}, u32[]{:S(2)}, u32[]{:S(2)}) async-start(bf16[16,8,1024]{2,1,0:T(8,128)(2,1)} %bitcast.12), calls=%async_computation.2 | async-start | bytes 524288 | tf_op jit(solution)/shard_map/all_to_all | solution.py:395
Sparse Core Ops, SparseCore 0:
  10.2 43.9 all-gather.4
  70.1 41.8 all-gather.2

commit v9 on v5

--- a/solution.py
+++ b/solution.py
@@ -14,6 +14,8 @@
 NZ = NZL * NZH
 AXES = ("x", "zl", "zh", "y", "c")
 MIB = 1024 * 1024
+AHEAD = 3
+CHAIN = 320 * 10**8
 
 
 def shift(value, axis, step):
@@ -33,6 +35,13 @@
                 for c in range(NC):
                     pairs.append((index(x, z, y, c), index(to_x, to_z, y, c)))
     return lax.ppermute(value, AXES, pairs)
+
+
+def total_of(parts, dtype):
+    total = parts[0].astype(jnp.float32)
+    for part in parts[1:]:
+        total = total + part.astype(jnp.float32)
+    return total.astype(dtype)
 
 
 def weight_kernel(odd, quant, scales, weight, half):
@@ -152,39 +161,45 @@
     )(core, acts, acts_in, grads, grads_in)
 
 
-def sum_kernel(parts, out, held, sems):
-    count = parts.shape[0]
-    pieces, _, rows, _ = held.shape
+def sum_kernel(parts, out, held, result, sems, out_sems):
+    pieces, terms, rows, columns = held.shape
+    stores = []
     copies = [
         pltpu.make_async_copy(parts.at[:, pl.ds(q * rows, rows)], held.at[q], sems.at[q])
         for q in range(pieces)
     ]
-    for copy in copies:
+    for copy in copies[:AHEAD]:
         copy.start()
     for q, copy in enumerate(copies):
+        if q + AHEAD < pieces:
+            copies[q + AHEAD].start()
         copy.wait()
-        total = held[q, 0].astype(jnp.float32)
-        for k in range(1, count):
-            total = total + held[q, k].astype(jnp.float32)
-        out[q * rows : (q + 1) * rows] = total.astype(out.dtype)
+        result[q] = total_of([held[q, k] for k in range(terms)], out.dtype)
+        stores.append(
+            pltpu.make_async_copy(result.at[q], out.at[pl.ds(q * rows, rows)], out_sems.at[q])
+        )
+        stores[-1].start()
+    for copy in stores:
+        copy.wait()
 
 
 def sums(parts):
-    count, rows, columns = parts.shape
-    each = min(rows, 64)
-    pieces = rows // each
+    terms, rows, columns = parts.shape
+    pieces = 4
     return pl.pallas_call(
         sum_kernel,
-        out_shape=jax.ShapeDtypeStruct((rows, columns), parts.dtype),
+        out_shape=pltpu.HBM((rows, columns), parts.dtype),
         in_specs=[pl.BlockSpec(memory_space=pl.ANY)],
-        out_specs=pl.BlockSpec(memory_space=pltpu.VMEM),
+        out_specs=pl.BlockSpec(memory_space=pl.ANY),
         scratch_shapes=[
-            pltpu.VMEM((pieces, count, each, columns), parts.dtype),
+            pltpu.VMEM((pieces, terms, rows // pieces, columns), parts.dtype),
+            pltpu.VMEM((pieces, rows // pieces, columns), parts.dtype),
+            pltpu.SemaphoreType.DMA((pieces,)),
             pltpu.SemaphoreType.DMA((pieces,)),
         ],
         compiler_params=pltpu.CompilerParams(vmem_limit_bytes=16 * MIB),
         cost_estimate=pl.CostEstimate(
-            flops=2 * 10**10, bytes_accessed=2 * count * rows * columns, transcendentals=0
+            flops=CHAIN, bytes_accessed=2 * terms * rows * columns, transcendentals=0
         ),
         name="sums",
     )(parts)
@@ -192,33 +207,41 @@
 
 def input_kernel(where, grads, weight, *rest):
     out, held, lhs, result, in_sems, out_sems = rest[-6:]
-    groups, pieces, rows, _ = weight.shape
-    span = pieces * rows
-    width = groups * span
-    first = pltpu.make_async_copy(grads, lhs, in_sems.at[groups])
+    groups, rows, _ = held.shape
+    first = pltpu.make_async_copy(grads, lhs, in_sems.at[2 * groups])
     first.start()
-    copies = [
-        pltpu.make_async_copy(weight.at[group], held.at[group], in_sems.at[group])
-        for group in range(groups)
-    ]
-    for copy in copies:
-        copy.start()
+    half = rows // 2
+    copies = []
+    for group in range(groups):
+        copies.append(
+            [
+                pltpu.make_async_copy(
+                    weight.at[group, pl.ds(i * half, half)],
+                    held.at[group, pl.ds(pl.multiple_of((where[1] ^ i) * half, half), half)],
+                    in_sems.at[2 * group + i],
+                )
+                for i in range(2)
+            ]
+        )
+    for pair in copies[:AHEAD]:
+        for copy in pair:
+            copy.start()
     first.wait()
     done = []
-    for group, copy in enumerate(copies):
-        copy.wait()
-        for piece in range(pieces):
-            start = group * span + piece * rows
-            block = held[group, lax.rem(piece + where[1], pieces)]
-            result[:, start : start + rows] = lax.dot_general(
-                lhs[...], block, (((1,), (1,)), ((), ())), preferred_element_type=jnp.float32
-            ).astype(result.dtype)
-        start = pl.multiple_of(where[0] * width + group * span, span)
+    for group, pair in enumerate(copies):
+        if group + AHEAD < groups:
+            for copy in copies[group + AHEAD]:
+                copy.start()
+        for copy in pair:
+            copy.wait()
+        run = pl.ds(group * rows, rows)
+        result[:, run] = lax.dot_general(
+            lhs[...], held[group], (((1,), (1,)), ((), ())), preferred_element_type=jnp.float32
+        ).astype(result.dtype)
+        start = pl.multiple_of((where[0] + group) * rows, rows)
         done.append(
             pltpu.make_async_copy(
-                result.at[:, pl.ds(group * span, span)],
-                out.at[:, pl.ds(start, span)],
-                out_sems.at[group],
+                result.at[:, run], out.at[:, pl.ds(start, rows)], out_sems.at[group]
             )
         )
         done[-1].start()
@@ -226,11 +249,11 @@
         copy.wait()
 
 
-def input_half(where, grads, weight, width, before=None):
+def input_part(place, turn, grads, weight, width, before=None):
     tokens, columns = grads.shape
-    groups, pieces, rows, _ = weight.shape
+    groups, rows, _ = weight.shape
     weight = pltpu.with_memory_space_constraint(weight, pltpu.HBM)
-    args = [where, grads, weight]
+    args = [jnp.stack([place, turn]).astype(jnp.int32), grads, weight]
     aliases = {}
     if before is not None:
         args.append(before)
@@ -242,20 +265,20 @@
         in_specs=[pl.BlockSpec(memory_space=pltpu.SMEM)] + [anywhere] * (len(args) - 1),
         out_specs=anywhere,
         scratch_shapes=[
-            pltpu.VMEM((groups, pieces, rows, columns), jnp.bfloat16),
+            pltpu.VMEM((groups, rows, columns), jnp.bfloat16),
             pltpu.VMEM((tokens, columns), jnp.bfloat16),
-            pltpu.VMEM((tokens, groups * pieces * rows), jnp.bfloat16),
-            pltpu.SemaphoreType.DMA((groups + 1,)),
+            pltpu.VMEM((tokens, groups * rows), jnp.bfloat16),
+            pltpu.SemaphoreType.DMA((2 * groups + 1,)),
             pltpu.SemaphoreType.DMA((groups,)),
         ],
         input_output_aliases=aliases,
         compiler_params=pltpu.CompilerParams(vmem_limit_bytes=16 * MIB),
         cost_estimate=pl.CostEstimate(
-            flops=2 * tokens * columns * pieces * groups * rows,
-            bytes_accessed=2 * pieces * groups * rows * columns + 4 * tokens * columns,
+            flops=2 * tokens * columns * groups * rows,
+            bytes_accessed=2 * groups * rows * columns + 4 * tokens * columns,
             transcendentals=0,
         ),
-        name="input_half",
+        name="input_part",
     )(*args)
 
 
@@ -267,32 +290,35 @@
     zl, zh, c = (lax.axis_index(name) for name in ("zl", "zh", "c"))
     odd = zl % 2
     groups = NY * NC
+    chunk = NZH * NZL * 8
 
     acts_in = shift(acts, "c", 1)
     grads_in = shift(grads_out, "c", 1)
     weight, piece = weights(odd[None].astype(jnp.int32), quant, scales)
     own_half = lax.all_gather(weight, ("y", "c"), axis=0, tiled=True)
+    fetched = chip_shift(piece, lambda i, z: (i, (z + NZL) % NZ))
+
     factor = 1.0 / math.sqrt(total_tokens)
-    parts = partials(c[None].astype(jnp.int32), acts, acts_in, grads_out, grads_in, factor)
-    received = lax.all_to_all(parts, "x", split_axis=0, concat_axis=0, tiled=True)
-    first = chip_shift(piece, lambda i, z: (i, (z + NZL) % NZ))
-    second = chip_shift(first, lambda i, z: (i, z ^ 1))
-    other_half = lax.all_gather(
-        jnp.concatenate([first, second], axis=0), ("y", "c"), axis=0, tiled=True
-    )
-    chunk = NZH * NZL * 8
-    summed = sums(received.reshape(NX, NY * chunk, columns)).reshape(NY, chunk, columns)
-    grads_later, summed = lax.optimization_barrier((grads_out, summed))
-    received = lax.all_to_all(summed, "y", split_axis=0, concat_axis=0, tiled=True)
-    own_half = own_half.reshape(groups, 1, shard_rows, columns)
-    place = jnp.stack([zh, 0 * odd]).astype(jnp.int32)
-    grad_input = input_half(place, grads_later, own_half, width)
+    core = c[None].astype(jnp.int32)
+    core, _ = lax.optimization_barrier((core, weight))
+    parts = partials(core, acts, acts_in, grads_out, grads_in, factor)
+    parts = parts.reshape(NX * NY, chunk, columns)
+    received = lax.all_to_all(parts, ("x", "y"), split_axis=0, concat_axis=0, tiled=True)
+
+    fetched, _ = lax.optimization_barrier((fetched, parts))
+    swapped = chip_shift(fetched, lambda i, z: (i, z ^ 1))
+    both = jnp.concatenate([fetched, swapped], axis=0)
+    other_half = lax.all_gather(both, ("y", "c"), axis=0, tiled=True)
+    own_half = own_half.reshape(groups, shard_rows, columns)
+    grad_input = input_part(zh * groups, 0 * odd, grads_out, own_half, width)
     grad_input, received = lax.optimization_barrier((grad_input, received))
     rows = sums(received).reshape(NZ, 8, columns)
+    grads_later, _ = lax.optimization_barrier((grads_out, rows))
     rows = lax.all_to_all(rows, ("zh", "zl"), split_axis=0, concat_axis=0, tiled=True)
-    other_half = other_half.reshape(groups, 2, shard_rows // 2, columns)
-    place = jnp.stack([1 - zh, odd]).astype(jnp.int32)
-    grad_input = input_half(place, grads_later, other_half, width, grad_input)
+    other_half = other_half.reshape(groups, shard_rows, columns)
+    grad_input = input_part(
+        (1 - zh) * groups, odd, grads_later, other_half, width, grad_input
+    )
     grad_input, rows = lax.optimization_barrier((grad_input, rows))
     weight_grad = jnp.sum(rows, axis=0, dtype=jnp.float32)
     return (grad_input, weight_grad)

time: 142 us -> 165 us (1.16)
  the two profiles are of different devices: /device:TPU:32 before, /device:TPU:1 now
where the time goes in v9:
time: 165 us
  waiting for transfers between devices  74.5 us (45%)
  starting transfers between devices  50.8 us (31%)
  Pallas kernels  23.4 us (14%)
  between operations  14.2 us (9%)
    all_gather x1, waiting for transfers between devices, shards(): own_half = lax.all_gather(weight, ('y', 'c'), axis=0, tiled=True)  38.7 us
    all_gather x1, waiting for transfers between devices, shards(): other_half = lax.all_gather(both, ('y', 'c'), axis=0, tiled=True)  28.8 us
    ppermute x2, starting transfers between devices, chip_shift(): return lax.ppermute(value, AXES, pairs)  21.7 us
    pallas_call x2, Pallas kernels, input_part(): pl.pallas_call(input_kernel, out_shape=jax.ShapeDtypeStruct((tokens, widt...  12.6 us
    all_to_all x1, starting transfers between devices, shards(): lax.all_to_all(rows, ('zh', 'zl'), split_axis=0, concat_axis=0, tiled=True)  11.3 us
    ppermute x2, starting transfers between devices, shift(): lax.ppermute(value, axis, [(i, (i + step) % size) for i in range(size)])  10.7 us
    ppermute x2, waiting for transfers between devices, chip_shift(): return lax.ppermute(value, AXES, pairs)  7 us
    all_to_all x1, starting transfers between devices, shards(): lax.all_to_all(parts, ('x', 'y'), split_axis=0, concat_axis=0, tiled=True)  6.95 us
  transfers between devices with their start and end apart: 8, of which 4 were waited for; matrix products, arithmetic and copies ran while one was open for 1% of the time, Pallas kernels for 13%

profile of v9, /device:TPU:1, one launch (start us, length us, event | category | flops | bytes accessed | tf_op | source)
XLA Modules:
  0.0 164.5 jit_solution(11300529819415161163)
XLA Ops:
  7.2 0.0 all-gather.3.cloned.1.call-start
  7.2 2.4 %weights.1 = (bf16[256,1024]{1,0:T(8,128)(2,1)}, bf16[128,1024]{1,0:T(8,128)(2,1)S(1)}) custom-call(s32[1]{0:T(128)} %bitcast.1.odd, bf16[256,1024]{1,0:T(8,128)(2,1)} %quant.1, f32[8,256]{1,0:T(8,128)} %bitcast.13), custom_call_target="tpu_custom_call" | custom-call | flops 262144 | bytes 1048576 | tf_op jit(solution)/shard_map/weights/pallas_call | solution.py:64
  9.6 0.0 all-gather.3.cloned.1.call-update
  9.6 8.8 %collective-permute-start = (bf16[224,4096]{1,0:T(8,128)(2,1)}, bf16[224,4096]{1,0:T(8,128)(2,1)S(1)}, u32[]{:S(2)}, u32[]{:S(2)}) collective-permute-start(bf16[224,4096]{1,0:T(8,128)(2,1)} %acts.1), channel_id=1, source_target_pairs={{0,1},{1,0},{2,3},{3,2},{4,5},{5,4},{6,7},{7,6},{8,9},{9,8},{10,11... | collective-permute-start | bytes 5505032 | tf_op jit(solution)/shard_map/ppermute | solution.py:23
  18.4 1.9 %collective-permute-start.1 = (bf16[224,1024]{1,0:T(8,128)(2,1)}, bf16[224,1024]{1,0:T(8,128)(2,1)S(1)}, u32[]{:S(2)}, u32[]{:S(2)}) collective-permute-start(bf16[224,1024]{1,0:T(8,128)(2,1)} %grads.4), channel_id=1, source_target_pairs={{0,1},{1,0},{2,3},{3,2},{4,5},{5,4},{6,7},{7,6},{8,9},{9,8},{10,11... | collective-permute-start | bytes 1376264 | tf_op jit(solution)/shard_map/ppermute | solution.py:23
  20.3 10.1 %collective-permute-start.2 = (bf16[128,1024]{1,0:T(8,128)(2,1)S(1)}, bf16[128,1024]{1,0:T(8,128)(2,1)S(1)}, u32[]{:S(2)}, u32[]{:S(2)}) collective-permute-start(bf16[128,1024]{1,0:T(8,128)(2,1)S(1)} %get-tuple-element.15), channel_id=1, source_target_pairs={{0,8},{1,9},{2,10},{3,11},{4,12},{5,13},{6,14},{7,15},{16,24},{17,... | collective-permute-start | bytes 786440 | tf_op jit(solution)/shard_map/ppermute | solution.py:37
  30.4 5.5 %partials.1 = bf16[4,8,64,1024]{3,2,1,0:T(8,128)(2,1)} custom-call(s32[1]{0:T(128)} %bitcast.5.core, bf16[224,4096]{1,0:T(8,128)(2,1)} %acts.1, bf16[224,4096]{1,0:T(8,128)(2,1)S(1)} %collective-permute-done.acts_in, bf16[224,1024]{1,0:T(8,128)(2,1)} %grads.4, bf16[224,1024]{1,0:T(8,128)(2,1)S(1)} %collective-permute-done.1.grads_in), custom_call_target="tpu_custom_call" | custom-call | flops 1879048192 | bytes 7864320 | tf_op jit(solution)/shard_map/partials/pallas_call | solution.py:140
  35.9 0.0 copy-start
  36.0 7.0 %all-to-all-start = ((bf16[16,128,1024]{2,1,0:T(8,128)(2,1)}), bf16[16,128,1024]{2,1,0:T(8,128)(2,1)}, u32[]{:S(2)}, u32[]{:S(2)}) async-start(bf16[16,128,1024]{2,1,0:T(8,128)(2,1)} %bitcast.9), calls=%async_computation | async-start | bytes 8388608 | tf_op jit(solution)/shard_map/all_to_all | solution.py:306
  42.9 0.0 all-gather.5.cloned.1.call-start
  43.0 1.5 collective-permute-done.2
  44.5 11.7 %collective-permute-start.3 = (bf16[128,1024]{1,0:T(8,128)(2,1)S(1)}, bf16[128,1024]{1,0:T(8,128)(2,1)S(1)}, u32[]{:S(2)}, u32[]{:S(2)}) collective-permute-start(bf16[128,1024]{1,0:T(8,128)(2,1)S(1)} %collective-permute-done.2), channel_id=1, source_target_pairs={{0,16},{1,17},{2,18},{3,19},{4,20},{5,21},{6,22},{7,23},{16,0},{17... | collective-permute-start | bytes 786440 | tf_op jit(solution)/shard_map/ppermute | solution.py:37
  56.1 5.5 %collective-permute-done.3 = bf16[128,1024]{1,0:T(8,128)(2,1)S(1)} collective-permute-done((bf16[128,1024]{1,0:T(8,128)(2,1)S(1)}, bf16[128,1024]{1,0:T(8,128)(2,1)S(1)}, u32[]{:S(2)}, u32[]{:S(2)}) %collective-permute-start.3) | collective-permute-done | bytes 262176 | tf_op jit(solution)/shard_map/ppermute | solution.py:37
  61.6 0.8 pad_maximum_fusion
  62.5 0.0 all-gather.5.cloned.1.call-update
  62.5 0.1 pad_add_fusion.1.where
  62.6 38.7 %all-gather.3.cloned.1.call-done = bf16[2048,1024]{1,0:T(8,128)(2,1)} async-done(((bf16[256,1024]{1,0:T(8,128)(2,1)}), bf16[2048,1024]{1,0:T(8,128)(2,1)}) %all-gather.3.cloned.1.call-update) | async-done | bytes 4194320 | tf_op jit(solution)/shard_map/all_gather | solution.py:298
  101.2 6.3 %input_part.2.rest_0_ = bf16[224,4096]{1,0:T(8,128)(2,1)} custom-call(s32[2]{0:T(128)S(1)} %pad_add_fusion.1.where, bf16[224,1024]{1,0:T(8,128)(2,1)S(1)} %copy-done, bf16[8,256,1024]{2,1,0:T(8,128)(2,1)} %bitcast.10), custom_call_target="tpu_custom_call" | custom-call | flops 939524096 | bytes 5111808 | tf_op jit(solution)/shard_map/input_part/pallas_call | solution.py:262
  107.5 3.0 %sums.1 = bf16[128,1024]{1,0:T(8,128)(2,1)} custom-call(bf16[16,128,1024]{2,1,0:T(8,128)(2,1)} %all-to-all-done.parts), custom_call_target="tpu_custom_call" | custom-call | flops 32000000000 | bytes 4194304 | tf_op jit(solution)/shard_map/sums/pallas_call | solution.py:189
  110.6 11.3 %all-to-all-start.1 = ((bf16[16,8,1024]{2,1,0:T(8,128)(2,1)}), bf16[16,8,1024]{2,1,0:T(8,128)(2,1)S(1)}, u32[]{:S(2)}, u32[]{:S(2)}) async-start(bf16[16,8,1024]{2,1,0:T(8,128)(2,1)} %bitcast.12), calls=%async_computation.1 | async-start | bytes 524288 | tf_op jit(solution)/shard_map/all_to_all | solution.py:317
  121.9 0.1 pad_add_fusion.where
  121.9 28.8 %all-gather.5.cloned.1.call-done = bf16[2048,1024]{1,0:T(8,128)(2,1)} async-done(((bf16[256,1024]{1,0:T(8,128)(2,1)}), bf16[2048,1024]{1,0:T(8,128)(2,1)}) %all-gather.5.cloned.1.call-update) | async-done | bytes 4194320 | tf_op jit(solution)/shard_map/all_gather | solution.py:311
  150.7 6.3 %input_part.3 = bf16[224,4096]{1,0:T(8,128)(2,1)} custom-call(s32[2]{0:T(128)S(1)} %pad_add_fusion.where, bf16[224,1024]{1,0:T(8,128)(2,1)S(1)} %copy-done, bf16[8,256,1024]{2,1,0:T(8,128)(2,1)} %bitcast.11, bf16[224,4096]{1,0:T(8,128)(2,1)} %input_part.2.rest_0_), custom_call_target="tpu_custom_call", output_to_operand_aliasing={{}: (3, {})} | custom-call | flops 939524096 | bytes 5111808 | tf_op jit(solution)/shard_map/input_part/pallas_call | solution.py:262
  157.0 0.7 convert_reduce_fusion
  (5 shorter events, 0.0 us)
Async XLA Ops:
  7.2 94.1 %all-gather.3.cloned.1.call-start = ((), (), s32[]{:S(2)}) async-start(), calls=%async_computation.2 | async-start | bytes 4718592 | tf_op jit(solution)/shard_map/all_gather | solution.py:298
  9.6 20.8 %collective-permute-start = (bf16[224,4096]{1,0:T(8,128)(2,1)}, bf16[224,4096]{1,0:T(8,128)(2,1)S(1)}, u32[]{:S(2)}, u32[]{:S(2)}) collective-permute-start(bf16[224,4096]{1,0:T(8,128)(2,1)} %acts.1), channel_id=1, source_target_pairs={{0,1},{1,0},{2,3},{3,2},{4,5},{5,4},{6,7},{7,6},{8,9},{9,8},{10,11... | collective-permute-start | bytes 5505032 | tf_op jit(solution)/shard_map/ppermute | solution.py:23
  18.4 12.0 %collective-permute-start.1 = (bf16[224,1024]{1,0:T(8,128)(2,1)}, bf16[224,1024]{1,0:T(8,128)(2,1)S(1)}, u32[]{:S(2)}, u32[]{:S(2)}) collective-permute-start(bf16[224,1024]{1,0:T(8,128)(2,1)} %grads.4), channel_id=1, source_target_pairs={{0,1},{1,0},{2,3},{3,2},{4,5},{5,4},{6,7},{7,6},{8,9},{9,8},{10,11... | collective-permute-start | bytes 1376264 | tf_op jit(solution)/shard_map/ppermute | solution.py:23
  20.3 24.1 %collective-permute-start.2 = (bf16[128,1024]{1,0:T(8,128)(2,1)S(1)}, bf16[128,1024]{1,0:T(8,128)(2,1)S(1)}, u32[]{:S(2)}, u32[]{:S(2)}) collective-permute-start(bf16[128,1024]{1,0:T(8,128)(2,1)S(1)} %get-tuple-element.15), channel_id=1, source_target_pairs={{0,8},{1,9},{2,10},{3,11},{4,12},{5,13},{6,14},{7,15},{16,24},{17,... | collective-permute-start | bytes 786440 | tf_op jit(solution)/shard_map/ppermute | solution.py:37
  35.9 65.3 %copy-start = (bf16[224,1024]{1,0:T(8,128)(2,1)S(1)}, bf16[224,1024]{1,0:T(8,128)(2,1)}, u32[]{:S(2)}) copy-start(bf16[224,1024]{1,0:T(8,128)(2,1)} %grads.4) | copy-start | bytes 1376260
  36.0 71.6 %all-to-all-start = ((bf16[16,128,1024]{2,1,0:T(8,128)(2,1)}), bf16[16,128,1024]{2,1,0:T(8,128)(2,1)}, u32[]{:S(2)}, u32[]{:S(2)}) async-start(bf16[16,128,1024]{2,1,0:T(8,128)(2,1)} %bitcast.9), calls=%async_computation | async-start | bytes 8388608 | tf_op jit(solution)/shard_map/all_to_all | solution.py:306
  42.9 107.8 %all-gather.5.cloned.1.call-start = ((), (), s32[]{:S(2)}) async-start(), calls=%async_computation.3 | async-start | bytes 4718592 | tf_op jit(solution)/shard_map/all_gather | solution.py:311
  44.5 17.2 %collective-permute-start.3 = (bf16[128,1024]{1,0:T(8,128)(2,1)S(1)}, bf16[128,1024]{1,0:T(8,128)(2,1)S(1)}, u32[]{:S(2)}, u32[]{:S(2)}) collective-permute-start(bf16[128,1024]{1,0:T(8,128)(2,1)S(1)} %collective-permute-done.2), channel_id=1, source_target_pairs={{0,16},{1,17},{2,18},{3,19},{4,20},{5,21},{6,22},{7,23},{16,0},{17... | collective-permute-start | bytes 786440 | tf_op jit(solution)/shard_map/ppermute | solution.py:37
  110.6 46.5 %all-to-all-start.1 = ((bf16[16,8,1024]{2,1,0:T(8,128)(2,1)}), bf16[16,8,1024]{2,1,0:T(8,128)(2,1)S(1)}, u32[]{:S(2)}, u32[]{:S(2)}) async-start(bf16[16,8,1024]{2,1,0:T(8,128)(2,1)} %bitcast.12), calls=%async_computation.1 | async-start | bytes 524288 | tf_op jit(solution)/shard_map/all_to_all | solution.py:317
Sparse Core Ops, SparseCore 0:
  10.7 90.4 all-gather.2
  103.4 47.2 all-gather.4

commit v10 on v8

--- a/solution.py
+++ b/solution.py
@@ -241,6 +241,7 @@
 def right_sums(parts):
     rows, columns = parts[0].shape
     count = len(parts)
+    parts = [pltpu.with_memory_space_constraint(parts[0], pltpu.HBM), *parts[1:]]
     return pl.pallas_call(
         right_kernel,
         out_shape=[jax.ShapeDtypeStruct((rows // count, columns), parts[0].dtype)] * count,
@@ -379,17 +380,17 @@
     where, _ = lax.optimization_barrier((where, weight))
     left, *right = partials(where, acts, acts_in, grads_out, grads_in, factor)
     left = lax.all_to_all(left, "x", split_axis=0, concat_axis=0, tiled=True)
-    right = [right[0]] + [shift(right[k], "y", k) for k in (1, 3, 2)]
+    right = [right[0]] + [shift(right[k], "y", k) for k in (2, 1, 3)]
 
     swapped = chip_shift(fetched, lambda i, z: (i, z ^ 1))
     both = jnp.concatenate([fetched, swapped], axis=0)
-    both, *_ = lax.optimization_barrier((both, right[1], right[2]))
+    both, *_ = lax.optimization_barrier((both, *right))
     other_half = lax.all_gather(both, ("y", "c"), axis=0, tiled=True)
 
     right = right_sums([part.reshape(NX * chunk, columns - LEFT) for part in right])
     left = left_sums(left.reshape(NX, NY * chunk, LEFT)).reshape(NY, chunk, LEFT)
     left = lax.all_to_all(left, "y", split_axis=0, concat_axis=0, tiled=True)
-    right = [right[0]] + [shift(right[k], "x", k) for k in (1, 3, 2)]
+    right = [right[0]] + [shift(right[k], "x", k) for k in (2, 1, 3)]
     rows = joined_sums(left, right).reshape(NZ, 8, columns)
     grads_later, _ = lax.optimization_barrier((grads_out, rows))
     rows = lax.all_to_all(rows, ("zh", "zl"), split_axis=0, concat_axis=0, tiled=True)

time: 136 us -> 134 us (0.985)
  the two profiles are of different devices: /device:TPU:32 before, /device:TPU:14 now
where the time goes in v10:
time: 134 us; the launch traced here: 133 us
  starting transfers between devices  76.1 us (57%)
  Pallas kernels  24.4 us (18%)
  waiting for transfers between devices  15.6 us (12%)
  between operations  14.2 us (11%)
  other arithmetic  2.68 us (2%)
    ppermute x2, starting transfers between devices, chip_shift(): return lax.ppermute(value, AXES, pairs)  31.4 us
    ppermute x8, starting transfers between devices, shift(): lax.ppermute(value, axis, [(i, (i + step) % size) for i in range(size)])  24.2 us
    pallas_call x2, Pallas kernels, input_part(): pl.pallas_call(input_kernel, out_shape=jax.ShapeDtypeStruct((tokens, widt...  12.6 us
    ppermute x8, waiting for transfers between devices, shift(): lax.ppermute(value, axis, [(i, (i + step) % size) for i in range(size)])  11.1 us
    all_to_all x1, starting transfers between devices, shards(): lax.all_to_all(rows, ('zh', 'zl'), split_axis=0, concat_axis=0, tiled=True)  10.7 us
    pallas_call x1, Pallas kernels, partials(): pl.pallas_call(functools.partial(partial_kernel, factor), out_shape=[pltp...  5.98 us
    all_to_all x1, starting transfers between devices, shards(): left = lax.all_to_all(left, 'y', split_axis=0, concat_axis=0, tiled=True)  4.94 us
    all_to_all x1, starting transfers between devices, shards(): left = lax.all_to_all(left, 'x', split_axis=0, concat_axis=0, tiled=True)  4.78 us
  transfers between devices with their start and end apart: 15, of which 6 were waited for; matrix products, arithmetic and copies ran while one was open for 2% of the time, Pallas kernels for 17%

profile of v10, /device:TPU:14, one launch (start us, length us, event | category | flops | bytes accessed | tf_op | source)
XLA Modules:
  0.0 132.9 jit_solution(15998518467142930638)
XLA Ops:
  7.2 2.3 %weights.1 = (bf16[256,1024]{1,0:T(8,128)(2,1)}, bf16[128,1024]{1,0:T(8,128)(2,1)S(1)}) custom-call(s32[1]{0:T(128)} %bitcast.1.odd, bf16[256,1024]{1,0:T(8,128)(2,1)} %quant.1, f32[8,256]{1,0:T(8,128)} %bitcast.21), custom_call_target="tpu_custom_call" | custom-call | flops 262144 | bytes 1048576 | tf_op jit(solution)/shard_map/weights/pallas_call | solution.py:65
  9.6 1.9 %collective-permute-start = (bf16[224,4096]{1,0:T(8,128)(2,1)}, bf16[224,4096]{1,0:T(8,128)(2,1)S(1)}, u32[]{:S(2)}, u32[]{:S(2)}) collective-permute-start(bf16[224,4096]{1,0:T(8,128)(2,1)} %acts.1), channel_id=1, source_target_pairs={{0,1},{1,0},{2,3},{3,2},{4,5},{5,4},{6,7},{7,6},{8,9},{9,8},{10,11... | collective-permute-start | bytes 5505032 | tf_op jit(solution)/shard_map/ppermute | solution.py:24
  11.5 2.4 %collective-permute-start.1 = (bf16[224,1024]{1,0:T(8,128)(2,1)}, bf16[224,1024]{1,0:T(8,128)(2,1)S(1)}, u32[]{:S(2)}, u32[]{:S(2)}) collective-permute-start(bf16[224,1024]{1,0:T(8,128)(2,1)} %grads.3), channel_id=1, source_target_pairs={{0,1},{1,0},{2,3},{3,2},{4,5},{5,4},{6,7},{7,6},{8,9},{9,8},{10,11... | collective-permute-start | bytes 1376264 | tf_op jit(solution)/shard_map/ppermute | solution.py:24
  13.9 15.7 %collective-permute-start.8 = (bf16[128,1024]{1,0:T(8,128)(2,1)S(1)}, bf16[128,1024]{1,0:T(8,128)(2,1)}, u32[]{:S(2)}, u32[]{:S(2)}) collective-permute-start(bf16[128,1024]{1,0:T(8,128)(2,1)S(1)} %get-tuple-element.30), channel_id=1, source_target_pairs={{0,8},{1,9},{2,10},{3,11},{4,12},{5,13},{6,14},{7,15},{16,24},{17,... | collective-permute-start | bytes 786440 | tf_op jit(solution)/shard_map/ppermute | solution.py:38
  29.8 6.0 %partials.1 = (bf16[4,8,64,768]{3,2,1,0:T(8,128)(2,1)}, bf16[8,64,256]{2,1,0:T(8,128)(2,1)}, bf16[8,64,256]{2,1,0:T(8,128)(2,1)}, bf16[8,64,256]{2,1,0:T(8,128)(2,1)}, bf16[8,64,256]{2,1,0:T(8,128)(2,1)}) custom-call(s32[3]{0:T(128)S(1)} %pad_add_fusion.1.where, bf16[224,4096]{1,0:T(8,128)(2,1)} %acts.1, bf16[224,4096]{1,0:T(8,128)(2,1)S(1)} %collective-permute-done.acts_in, ...), custom_call_target="tpu_custom_call" | custom-call | flops 1879048192 | bytes 7864320 | tf_op jit(solution)/shard_map/partials/pallas_call | solution.py:156
  35.7 4.8 %all-to-all-start = ((bf16[4,8,64,768]{3,2,1,0:T(8,128)(2,1)}), bf16[4,8,64,768]{3,2,1,0:T(8,128)(2,1)S(1)}, u32[]{:S(2)}, u32[]{:S(2)}) async-start(bf16[4,8,64,768]{3,2,1,0:T(8,128)(2,1)} %get-tuple-element.20), calls=%async_computation | async-start | bytes 6291456 | tf_op jit(solution)/shard_map/all_to_all | solution.py:382
  40.5 15.7 %collective-permute-start.9 = (bf16[128,1024]{1,0:T(8,128)(2,1)}, bf16[128,1024]{1,0:T(8,128)(2,1)S(1)}, u32[]{:S(2)}, u32[]{:S(2)}) collective-permute-start(bf16[128,1024]{1,0:T(8,128)(2,1)} %collective-permute-done.8), channel_id=1, source_target_pairs={{0,16},{1,17},{2,18},{3,19},{4,20},{5,21},{6,22},{7,23},{16,0},{17... | collective-permute-start | bytes 786440 | tf_op jit(solution)/shard_map/ppermute | solution.py:38
  56.2 3.5 %collective-permute-start.3 = (bf16[8,64,256]{2,1,0:T(8,128)(2,1)}, bf16[8,64,256]{2,1,0:T(8,128)(2,1)S(1)}, u32[]{:S(2)}, u32[]{:S(2)}) collective-permute-start(bf16[8,64,256]{2,1,0:T(8,128)(2,1)} %get-tuple-element.23), channel_id=1, source_target_pairs={{0,2},{2,4},{4,6},{6,0},{1,3},{3,5},{5,7},{7,1},{8,10},{10,12},{12... | collective-permute-start | bytes 786440 | tf_op jit(solution)/shard_map/ppermute | solution.py:24
  59.7 2.4 %collective-permute-start.4 = (bf16[8,64,256]{2,1,0:T(8,128)(2,1)}, bf16[8,64,256]{2,1,0:T(8,128)(2,1)}, u32[]{:S(2)}, u32[]{:S(2)}) collective-permute-start(bf16[8,64,256]{2,1,0:T(8,128)(2,1)} %get-tuple-element.24), channel_id=1, source_target_pairs={{0,6},{2,0},{4,2},{6,4},{1,7},{3,1},{5,3},{7,5},{8,14},{10,8},{12,... | collective-permute-start | bytes 786440 | tf_op jit(solution)/shard_map/ppermute | solution.py:24
  62.1 4.2 %collective-permute-start.2 = (bf16[8,64,256]{2,1,0:T(8,128)(2,1)}, bf16[8,64,256]{2,1,0:T(8,128)(2,1)}, u32[]{:S(2)}, u32[]{:S(2)}) collective-permute-start(bf16[8,64,256]{2,1,0:T(8,128)(2,1)} %get-tuple-element.22), channel_id=1, source_target_pairs={{0,4},{2,6},{4,0},{6,2},{1,5},{3,7},{5,1},{7,3},{8,12},{10,14},{12... | collective-permute-start | bytes 786440 | tf_op jit(solution)/shard_map/ppermute | solution.py:24
  66.3 1.8 %pad_maximum_fusion = bf16[256,1024]{1,0:T(8,128)(2,1)} fusion(bf16[128,1024]{1,0:T(8,128)(2,1)S(1)} %collective-permute-done.9, bf16[128,1024]{1,0:T(8,128)(2,1)} %collective-permute-done.8), kind=kLoop, calls=%fused_computation | loop fusion | flops 1048576 | bytes 1048576 | tf_op jit(solution)/shard_map/concatenate | solution.py:386
  68.1 2.3 %collective-permute-done.4 = bf16[8,64,256]{2,1,0:T(8,128)(2,1)} collective-permute-done((bf16[8,64,256]{2,1,0:T(8,128)(2,1)}, bf16[8,64,256]{2,1,0:T(8,128)(2,1)}, u32[]{:S(2)}, u32[]{:S(2)}) %collective-permute-start.4) | collective-permute-done | bytes 262176 | tf_op jit(solution)/shard_map/ppermute | solution.py:24
  70.5 4.8 %collective-permute-done.2 = bf16[8,64,256]{2,1,0:T(8,128)(2,1)} collective-permute-done((bf16[8,64,256]{2,1,0:T(8,128)(2,1)}, bf16[8,64,256]{2,1,0:T(8,128)(2,1)}, u32[]{:S(2)}, u32[]{:S(2)}) %collective-permute-start.2) | collective-permute-done | bytes 262176 | tf_op jit(solution)/shard_map/ppermute | solution.py:24
  75.9 1.4 %left_sums.1 = bf16[512,768]{1,0:T(8,128)(2,1)} custom-call(bf16[4,512,768]{2,1,0:T(8,128)(2,1)S(1)} %bitcast.16), custom_call_target="tpu_custom_call" | custom-call | flops 16000000000 | bytes 3145728 | tf_op jit(solution)/shard_map/left_sums/pallas_call | solution.py:205
  77.3 4.9 %all-to-all-start.1 = ((bf16[4,128,768]{2,1,0:T(8,128)(2,1)}), bf16[4,128,768]{2,1,0:T(8,128)(2,1)S(1)}, u32[]{:S(2)}, u32[]{:S(2)}) async-start(bf16[4,128,768]{2,1,0:T(8,128)(2,1)} %bitcast.20), calls=%async_computation.1 | async-start | bytes 1572864 | tf_op jit(solution)/shard_map/all_to_all | solution.py:392
  82.2 1.3 right_sums.1
  83.5 4.0 %collective-permute-start.5 = (bf16[128,256]{1,0:T(8,128)(2,1)S(1)}, bf16[128,256]{1,0:T(8,128)(2,1)S(1)}, u32[]{:S(2)}, u32[]{:S(2)}) collective-permute-start(bf16[128,256]{1,0:T(8,128)(2,1)S(1)} %get-tuple-element.26), channel_id=1, source_target_pairs={{0,256},{128,384},{256,0},{384,128},{1,257},{129,385},{257,1},{385... | collective-permute-start | bytes 196616 | tf_op jit(solution)/shard_map/ppermute | solution.py:24
  87.5 2.5 %collective-permute-start.6 = (bf16[128,256]{1,0:T(8,128)(2,1)S(1)}, bf16[128,256]{1,0:T(8,128)(2,1)S(1)}, u32[]{:S(2)}, u32[]{:S(2)}) collective-permute-start(bf16[128,256]{1,0:T(8,128)(2,1)S(1)} %get-tuple-element.27), channel_id=1, source_target_pairs={{0,128},{128,256},{256,384},{384,0},{1,129},{129,257},{257,385},{3... | collective-permute-start | bytes 196616 | tf_op jit(solution)/shard_map/ppermute | solution.py:24
  90.0 3.4 %collective-permute-start.7 = (bf16[128,256]{1,0:T(8,128)(2,1)S(1)}, bf16[128,256]{1,0:T(8,128)(2,1)S(1)}, u32[]{:S(2)}, u32[]{:S(2)}) collective-permute-start(bf16[128,256]{1,0:T(8,128)(2,1)S(1)} %get-tuple-element.28), channel_id=1, source_target_pairs={{0,384},{128,0},{256,128},{384,256},{1,385},{129,1},{257,129},{385... | collective-permute-start | bytes 196616 | tf_op jit(solution)/shard_map/ppermute | solution.py:24
  93.6 3.7 %collective-permute-done.7.refs_3_ = bf16[128,256]{1,0:T(8,128)(2,1)S(1)} collective-permute-done((bf16[128,256]{1,0:T(8,128)(2,1)S(1)}, bf16[128,256]{1,0:T(8,128)(2,1)S(1)}, u32[]{:S(2)}, u32[]{:S(2)}) %collective-permute-start.7) | collective-permute-done | bytes 65568 | tf_op jit(solution)/shard_map/ppermute | solution.py:24
  98.2 10.7 %all-to-all-start.2 = ((bf16[16,8,1024]{2,1,0:T(8,128)(2,1)}), bf16[16,8,1024]{2,1,0:T(8,128)(2,1)S(1)}, u32[]{:S(2)}, u32[]{:S(2)}) async-start(bf16[16,8,1024]{2,1,0:T(8,128)(2,1)} %bitcast.12), calls=%async_computation.2 | async-start | bytes 524288 | tf_op jit(solution)/shard_map/all_to_all | solution.py:396
  109.0 6.3 %input_part.2.rest_0_ = bf16[224,4096]{1,0:T(8,128)(2,1)} custom-call(s32[2]{0:T(128)S(1)} %pad_add_fusion.2.where, bf16[224,1024]{1,0:T(8,128)(2,1)S(1)} %copy-done, bf16[8,256,1024]{2,1,0:T(8,128)(2,1)} %bitcast.18), custom_call_target="tpu_custom_call" | custom-call | flops 939524096 | bytes 5111808 | tf_op jit(solution)/shard_map/input_part/pallas_call | solution.py:339
  115.3 6.3 %input_part.3 = bf16[224,4096]{1,0:T(8,128)(2,1)} custom-call(s32[2]{0:T(128)S(1)} %pad_add_fusion.where, bf16[224,1024]{1,0:T(8,128)(2,1)S(1)} %copy-done, bf16[8,256,1024]{2,1,0:T(8,128)(2,1)} %bitcast.19, bf16[224,4096]{1,0:T(8,128)(2,1)} %input_part.2.rest_0_), custom_call_target="tpu_custom_call", output_to_operand_aliasing={{}: (3, {})} | custom-call | flops 939524096 | bytes 5111808 | tf_op jit(solution)/shard_map/input_part/pallas_call | solution.py:339
  121.6 3.8 %all-to-all-done.2 = bf16[16,8,1024]{2,1,0:T(8,128)(2,1)S(1)} async-done(((bf16[16,8,1024]{2,1,0:T(8,128)(2,1)}), bf16[16,8,1024]{2,1,0:T(8,128)(2,1)S(1)}, u32[]{:S(2)}, u32[]{:S(2)}) %all-to-all-start.2) | async-done | bytes 262176 | tf_op jit(solution)/shard_map/all_to_all | solution.py:396
  (22 shorter events, 2.8 us)
Async XLA Ops:
  7.2 101.8 %all-gather.5.cloned.1.call-start = ((), (), s32[]{:S(2)}) async-start(), calls=%async_computation.4 | async-start | bytes 4718592 | tf_op jit(solution)/shard_map/all_gather | solution.py:375
  9.6 20.2 %collective-permute-start = (bf16[224,4096]{1,0:T(8,128)(2,1)}, bf16[224,4096]{1,0:T(8,128)(2,1)S(1)}, u32[]{:S(2)}, u32[]{:S(2)}) collective-permute-start(bf16[224,4096]{1,0:T(8,128)(2,1)} %acts.1), channel_id=1, source_target_pairs={{0,1},{1,0},{2,3},{3,2},{4,5},{5,4},{6,7},{7,6},{8,9},{9,8},{10,11... | collective-permute-start | bytes 5505032 | tf_op jit(solution)/shard_map/ppermute | solution.py:24
  11.5 18.2 %collective-permute-start.1 = (bf16[224,1024]{1,0:T(8,128)(2,1)}, bf16[224,1024]{1,0:T(8,128)(2,1)S(1)}, u32[]{:S(2)}, u32[]{:S(2)}) collective-permute-start(bf16[224,1024]{1,0:T(8,128)(2,1)} %grads.3), channel_id=1, source_target_pairs={{0,1},{1,0},{2,3},{3,2},{4,5},{5,4},{6,7},{7,6},{8,9},{9,8},{10,11... | collective-permute-start | bytes 1376264 | tf_op jit(solution)/shard_map/ppermute | solution.py:24
  13.9 26.6 %collective-permute-start.8 = (bf16[128,1024]{1,0:T(8,128)(2,1)S(1)}, bf16[128,1024]{1,0:T(8,128)(2,1)}, u32[]{:S(2)}, u32[]{:S(2)}) collective-permute-start(bf16[128,1024]{1,0:T(8,128)(2,1)S(1)} %get-tuple-element.30), channel_id=1, source_target_pairs={{0,8},{1,9},{2,10},{3,11},{4,12},{5,13},{6,14},{7,15},{16,24},{17,... | collective-permute-start | bytes 786440 | tf_op jit(solution)/shard_map/ppermute | solution.py:38
  35.7 40.2 %all-to-all-start = ((bf16[4,8,64,768]{3,2,1,0:T(8,128)(2,1)}), bf16[4,8,64,768]{3,2,1,0:T(8,128)(2,1)S(1)}, u32[]{:S(2)}, u32[]{:S(2)}) async-start(bf16[4,8,64,768]{3,2,1,0:T(8,128)(2,1)} %get-tuple-element.20), calls=%async_computation | async-start | bytes 6291456 | tf_op jit(solution)/shard_map/all_to_all | solution.py:382
  40.5 74.8 %all-gather.3.cloned.1.call-start = ((), (), s32[]{:S(2)}) async-start(), calls=%async_computation.3 | async-start | bytes 4718592 | tf_op jit(solution)/shard_map/all_gather | solution.py:388
  40.5 25.8 %collective-permute-start.9 = (bf16[128,1024]{1,0:T(8,128)(2,1)}, bf16[128,1024]{1,0:T(8,128)(2,1)S(1)}, u32[]{:S(2)}, u32[]{:S(2)}) collective-permute-start(bf16[128,1024]{1,0:T(8,128)(2,1)} %collective-permute-done.8), channel_id=1, source_target_pairs={{0,16},{1,17},{2,18},{3,19},{4,20},{5,21},{6,22},{7,23},{16,0},{17... | collective-permute-start | bytes 786440 | tf_op jit(solution)/shard_map/ppermute | solution.py:38
  56.2 11.9 %collective-permute-start.3 = (bf16[8,64,256]{2,1,0:T(8,128)(2,1)}, bf16[8,64,256]{2,1,0:T(8,128)(2,1)S(1)}, u32[]{:S(2)}, u32[]{:S(2)}) collective-permute-start(bf16[8,64,256]{2,1,0:T(8,128)(2,1)} %get-tuple-element.23), channel_id=1, source_target_pairs={{0,2},{2,4},{4,6},{6,0},{1,3},{3,5},{5,7},{7,1},{8,10},{10,12},{12... | collective-permute-start | bytes 786440 | tf_op jit(solution)/shard_map/ppermute | solution.py:24
  59.7 10.7 %collective-permute-start.4 = (bf16[8,64,256]{2,1,0:T(8,128)(2,1)}, bf16[8,64,256]{2,1,0:T(8,128)(2,1)}, u32[]{:S(2)}, u32[]{:S(2)}) collective-permute-start(bf16[8,64,256]{2,1,0:T(8,128)(2,1)} %get-tuple-element.24), channel_id=1, source_target_pairs={{0,6},{2,0},{4,2},{6,4},{1,7},{3,1},{5,3},{7,5},{8,14},{10,8},{12,... | collective-permute-start | bytes 786440 | tf_op jit(solution)/shard_map/ppermute | solution.py:24
  62.1 13.1 %collective-permute-start.2 = (bf16[8,64,256]{2,1,0:T(8,128)(2,1)}, bf16[8,64,256]{2,1,0:T(8,128)(2,1)}, u32[]{:S(2)}, u32[]{:S(2)}) collective-permute-start(bf16[8,64,256]{2,1,0:T(8,128)(2,1)} %get-tuple-element.22), channel_id=1, source_target_pairs={{0,4},{2,6},{4,0},{6,2},{1,5},{3,7},{5,1},{7,3},{8,12},{10,14},{12... | collective-permute-start | bytes 786440 | tf_op jit(solution)/shard_map/ppermute | solution.py:24
  77.3 20.1 %all-to-all-start.1 = ((bf16[4,128,768]{2,1,0:T(8,128)(2,1)}), bf16[4,128,768]{2,1,0:T(8,128)(2,1)S(1)}, u32[]{:S(2)}, u32[]{:S(2)}) async-start(bf16[4,128,768]{2,1,0:T(8,128)(2,1)} %bitcast.20), calls=%async_computation.1 | async-start | bytes 1572864 | tf_op jit(solution)/shard_map/all_to_all | solution.py:392
  83.5 9.8 %collective-permute-start.5 = (bf16[128,256]{1,0:T(8,128)(2,1)S(1)}, bf16[128,256]{1,0:T(8,128)(2,1)S(1)}, u32[]{:S(2)}, u32[]{:S(2)}) collective-permute-start(bf16[128,256]{1,0:T(8,128)(2,1)S(1)} %get-tuple-element.26), channel_id=1, source_target_pairs={{0,256},{128,384},{256,0},{384,128},{1,257},{129,385},{257,1},{385... | collective-permute-start | bytes 196616 | tf_op jit(solution)/shard_map/ppermute | solution.py:24
  87.5 6.2 %collective-permute-start.6 = (bf16[128,256]{1,0:T(8,128)(2,1)S(1)}, bf16[128,256]{1,0:T(8,128)(2,1)S(1)}, u32[]{:S(2)}, u32[]{:S(2)}) collective-permute-start(bf16[128,256]{1,0:T(8,128)(2,1)S(1)} %get-tuple-element.27), channel_id=1, source_target_pairs={{0,128},{128,256},{256,384},{384,0},{1,129},{129,257},{257,385},{3... | collective-permute-start | bytes 196616 | tf_op jit(solution)/shard_map/ppermute | solution.py:24
  90.0 7.4 %collective-permute-start.7 = (bf16[128,256]{1,0:T(8,128)(2,1)S(1)}, bf16[128,256]{1,0:T(8,128)(2,1)S(1)}, u32[]{:S(2)}, u32[]{:S(2)}) collective-permute-start(bf16[128,256]{1,0:T(8,128)(2,1)S(1)} %get-tuple-element.28), channel_id=1, source_target_pairs={{0,384},{128,0},{256,128},{384,256},{1,385},{129,1},{257,129},{385... | collective-permute-start | bytes 196616 | tf_op jit(solution)/shard_map/ppermute | solution.py:24
  97.3 11.7 %copy-start = (bf16[224,1024]{1,0:T(8,128)(2,1)S(1)}, bf16[224,1024]{1,0:T(8,128)(2,1)}, u32[]{:S(2)}) copy-start(bf16[224,1024]{1,0:T(8,128)(2,1)} %grads.3) | copy-start | bytes 1376260
  98.2 27.3 %all-to-all-start.2 = ((bf16[16,8,1024]{2,1,0:T(8,128)(2,1)}), bf16[16,8,1024]{2,1,0:T(8,128)(2,1)S(1)}, u32[]{:S(2)}, u32[]{:S(2)}) async-start(bf16[16,8,1024]{2,1,0:T(8,128)(2,1)} %bitcast.12), calls=%async_computation.2 | async-start | bytes 524288 | tf_op jit(solution)/shard_map/all_to_all | solution.py:396
Sparse Core Ops, SparseCore 0:
  10.2 43.0 all-gather.4
  75.4 38.3 all-gather.2

commit v11 on v10

--- a/solution.py
+++ b/solution.py
@@ -15,8 +15,8 @@
 AXES = ("x", "zl", "zh", "y", "c")
 MIB = 1024 * 1024
 AHEAD = 3
-LEFT = 768
-CHAIN = 16 * 10**9
+LEFT = 640
+CHAIN = 14 * 10**9
 
 
 def shift(value, axis, step):
@@ -215,7 +215,7 @@
         ],
         compiler_params=pltpu.CompilerParams(vmem_limit_bytes=16 * MIB),
         cost_estimate=pl.CostEstimate(
-            flops=CHAIN, bytes_accessed=2 * terms * rows * columns, transcendentals=0
+            flops=2 * CHAIN, bytes_accessed=2 * terms * rows * columns, transcendentals=0
         ),
         name="left_sums",
     )(parts)
@@ -382,6 +382,7 @@
     left = lax.all_to_all(left, "x", split_axis=0, concat_axis=0, tiled=True)
     right = [right[0]] + [shift(right[k], "y", k) for k in (2, 1, 3)]
 
+    fetched, _ = lax.optimization_barrier((fetched, right[2]))
     swapped = chip_shift(fetched, lambda i, z: (i, z ^ 1))
     both = jnp.concatenate([fetched, swapped], axis=0)
     both, *_ = lax.optimization_barrier((both, *right))

time: 134 us -> 138 us (1.030)
  the two profiles are of different devices: /device:TPU:14 before, /device:TPU:24 now
where the time goes in v11:
time: 138 us; the launch traced here: 137 us
  starting transfers between devices  75.3 us (55%)
  Pallas kernels  24.5 us (18%)
  waiting for transfers between devices  20.8 us (15%)
  between operations  14.2 us (10%)
  other arithmetic  1.7 us (1%)
    ppermute x8, starting transfers between devices, shift(): lax.ppermute(value, axis, [(i, (i + step) % size) for i in range(size)])  30.3 us
    ppermute x2, starting transfers between devices, chip_shift(): return lax.ppermute(value, AXES, pairs)  23 us
    ppermute x2, waiting for transfers between devices, chip_shift(): return lax.ppermute(value, AXES, pairs)  12.7 us
    pallas_call x2, Pallas kernels, input_part(): pl.pallas_call(input_kernel, out_shape=jax.ShapeDtypeStruct((tokens, widt...  12.6 us
    all_to_all x1, starting transfers between devices, shards(): lax.all_to_all(rows, ('zh', 'zl'), split_axis=0, concat_axis=0, tiled=True)  12 us
    pallas_call x1, Pallas kernels, partials(): pl.pallas_call(functools.partial(partial_kernel, factor), out_shape=[pltp...  5.95 us
    all_to_all x1, starting transfers between devices, shards(): left = lax.all_to_all(left, 'y', split_axis=0, concat_axis=0, tiled=True)  5.68 us
    ppermute x8, waiting for transfers between devices, shift(): lax.ppermute(value, axis, [(i, (i + step) % size) for i in range(size)])  4.31 us
  transfers between devices with their start and end apart: 15, of which 6 were waited for; matrix products, arithmetic and copies ran while one was open for 1% of the time, Pallas kernels for 16%

profile of v11, /device:TPU:24, one launch (start us, length us, event | category | flops | bytes accessed | tf_op | source)
XLA Modules:
  0.0 136.6 jit_solution(12663023123858029999)
XLA Ops:
  7.2 2.4 %weights.1 = (bf16[256,1024]{1,0:T(8,128)(2,1)}, bf16[128,1024]{1,0:T(8,128)(2,1)}) custom-call(s32[1]{0:T(128)} %bitcast.1.odd, bf16[256,1024]{1,0:T(8,128)(2,1)} %quant.1, f32[8,256]{1,0:T(8,128)} %bitcast.22), custom_call_target="tpu_custom_call" | custom-call | flops 262144 | bytes 1048576 | tf_op jit(solution)/shard_map/weights/pallas_call | solution.py:65
  9.7 1.9 %collective-permute-start = (bf16[224,4096]{1,0:T(8,128)(2,1)}, bf16[224,4096]{1,0:T(8,128)(2,1)S(1)}, u32[]{:S(2)}, u32[]{:S(2)}) collective-permute-start(bf16[224,4096]{1,0:T(8,128)(2,1)} %acts.1), channel_id=1, source_target_pairs={{0,1},{1,0},{2,3},{3,2},{4,5},{5,4},{6,7},{7,6},{8,9},{9,8},{10,11... | collective-permute-start | bytes 5505032 | tf_op jit(solution)/shard_map/ppermute | solution.py:24
  11.6 2.4 %collective-permute-start.1 = (bf16[224,1024]{1,0:T(8,128)(2,1)}, bf16[224,1024]{1,0:T(8,128)(2,1)S(1)}, u32[]{:S(2)}, u32[]{:S(2)}) collective-permute-start(bf16[224,1024]{1,0:T(8,128)(2,1)} %grads.3), channel_id=1, source_target_pairs={{0,1},{1,0},{2,3},{3,2},{4,5},{5,4},{6,7},{7,6},{8,9},{9,8},{10,11... | collective-permute-start | bytes 1376264 | tf_op jit(solution)/shard_map/ppermute | solution.py:24
  14.1 2.1 %collective-permute-done.1.grads_in = bf16[224,1024]{1,0:T(8,128)(2,1)S(1)} collective-permute-done((bf16[224,1024]{1,0:T(8,128)(2,1)}, bf16[224,1024]{1,0:T(8,128)(2,1)S(1)}, u32[]{:S(2)}, u32[]{:S(2)}) %collective-permute-start.1) | collective-permute-done | bytes 458784 | tf_op jit(solution)/shard_map/ppermute | solution.py:24
  16.2 5.9 %partials.1 = (bf16[4,8,64,640]{3,2,1,0:T(8,128)(2,1)}, bf16[8,64,384]{2,1,0:T(8,128)(2,1)}, bf16[8,64,384]{2,1,0:T(8,128)(2,1)}, bf16[8,64,384]{2,1,0:T(8,128)(2,1)}, bf16[8,64,384]{2,1,0:T(8,128)(2,1)}) custom-call(s32[3]{0:T(128)S(1)} %pad_add_fusion.1.where, bf16[224,4096]{1,0:T(8,128)(2,1)} %acts.1, bf16[224,4096]{1,0:T(8,128)(2,1)S(1)} %collective-permute-done.acts_in, ...), custom_call_target="tpu_custom_call" | custom-call | flops 1879048192 | bytes 7864320 | tf_op jit(solution)/shard_map/partials/pallas_call | solution.py:156
  22.2 4.3 %all-to-all-start = ((bf16[4,8,64,640]{3,2,1,0:T(8,128)(2,1)}), bf16[4,8,64,640]{3,2,1,0:T(8,128)(2,1)S(1)}, u32[]{:S(2)}, u32[]{:S(2)}) async-start(bf16[4,8,64,640]{3,2,1,0:T(8,128)(2,1)} %get-tuple-element.21), calls=%async_computation | async-start | bytes 5242880 | tf_op jit(solution)/shard_map/all_to_all | solution.py:382
  26.5 7.0 %collective-permute-start.3 = (bf16[8,64,384]{2,1,0:T(8,128)(2,1)}, bf16[8,64,384]{2,1,0:T(8,128)(2,1)S(1)}, u32[]{:S(2)}, u32[]{:S(2)}) collective-permute-start(bf16[8,64,384]{2,1,0:T(8,128)(2,1)} %get-tuple-element.24), channel_id=1, source_target_pairs={{0,2},{2,4},{4,6},{6,0},{1,3},{3,5},{5,7},{7,1},{8,10},{10,12},{12... | collective-permute-start | bytes 1179656 | tf_op jit(solution)/shard_map/ppermute | solution.py:24
  33.5 10.9 %collective-permute-start.8 = (bf16[128,1024]{1,0:T(8,128)(2,1)}, bf16[128,1024]{1,0:T(8,128)(2,1)S(1)}, u32[]{:S(2)}, u32[]{:S(2)}) collective-permute-start(bf16[128,1024]{1,0:T(8,128)(2,1)} %get-tuple-element.31), channel_id=1, source_target_pairs={{0,8},{1,9},{2,10},{3,11},{4,12},{5,13},{6,14},{7,15},{16,24},{17,... | collective-permute-start | bytes 786440 | tf_op jit(solution)/shard_map/ppermute | solution.py:38
  44.4 3.7 %collective-permute-start.4 = (bf16[8,64,384]{2,1,0:T(8,128)(2,1)}, bf16[8,64,384]{2,1,0:T(8,128)(2,1)S(1)}, u32[]{:S(2)}, u32[]{:S(2)}) collective-permute-start(bf16[8,64,384]{2,1,0:T(8,128)(2,1)} %get-tuple-element.25), channel_id=1, source_target_pairs={{0,6},{2,0},{4,2},{6,4},{1,7},{3,1},{5,3},{7,5},{8,14},{10,8},{12,... | collective-permute-start | bytes 1179656 | tf_op jit(solution)/shard_map/ppermute | solution.py:24
  48.1 3.2 %collective-permute-start.2 = (bf16[8,64,384]{2,1,0:T(8,128)(2,1)}, bf16[8,64,384]{2,1,0:T(8,128)(2,1)}, u32[]{:S(2)}, u32[]{:S(2)}) collective-permute-start(bf16[8,64,384]{2,1,0:T(8,128)(2,1)} %get-tuple-element.23), channel_id=1, source_target_pairs={{0,4},{2,6},{4,0},{6,2},{1,5},{3,7},{5,1},{7,3},{8,12},{10,14},{12... | collective-permute-start | bytes 1179656 | tf_op jit(solution)/shard_map/ppermute | solution.py:24
  51.2 7.3 %collective-permute-done.8 = bf16[128,1024]{1,0:T(8,128)(2,1)S(1)} collective-permute-done((bf16[128,1024]{1,0:T(8,128)(2,1)}, bf16[128,1024]{1,0:T(8,128)(2,1)S(1)}, u32[]{:S(2)}, u32[]{:S(2)}) %collective-permute-start.8) | collective-permute-done | bytes 262176 | tf_op jit(solution)/shard_map/ppermute | solution.py:38
  58.6 12.1 %collective-permute-start.9 = (bf16[128,1024]{1,0:T(8,128)(2,1)S(1)}, bf16[128,1024]{1,0:T(8,128)(2,1)S(1)}, u32[]{:S(2)}, u32[]{:S(2)}) collective-permute-start(bf16[128,1024]{1,0:T(8,128)(2,1)S(1)} %collective-permute-done.8), channel_id=1, source_target_pairs={{0,16},{1,17},{2,18},{3,19},{4,20},{5,21},{6,22},{7,23},{16,0},{17... | collective-permute-start | bytes 786440 | tf_op jit(solution)/shard_map/ppermute | solution.py:38
  70.7 5.3 %collective-permute-done.9 = bf16[128,1024]{1,0:T(8,128)(2,1)S(1)} collective-permute-done((bf16[128,1024]{1,0:T(8,128)(2,1)S(1)}, bf16[128,1024]{1,0:T(8,128)(2,1)S(1)}, u32[]{:S(2)}, u32[]{:S(2)}) %collective-permute-start.9) | collective-permute-done | bytes 262176 | tf_op jit(solution)/shard_map/ppermute | solution.py:38
  76.9 1.4 %left_sums.1 = bf16[512,640]{1,0:T(8,128)(2,1)} custom-call(bf16[4,512,640]{2,1,0:T(8,128)(2,1)S(1)} %bitcast.16), custom_call_target="tpu_custom_call" | custom-call | flops 28000000000 | bytes 2621440 | tf_op jit(solution)/shard_map/left_sums/pallas_call | solution.py:205
  78.3 5.7 %all-to-all-start.1 = ((bf16[4,128,640]{2,1,0:T(8,128)(2,1)}), bf16[4,128,640]{2,1,0:T(8,128)(2,1)S(1)}, u32[]{:S(2)}, u32[]{:S(2)}) async-start(bf16[4,128,640]{2,1,0:T(8,128)(2,1)} %bitcast.21), calls=%async_computation.1 | async-start | bytes 1310720 | tf_op jit(solution)/shard_map/all_to_all | solution.py:393
  83.9 1.3 right_sums.1
  85.3 5.1 %collective-permute-start.5 = (bf16[128,384]{1,0:T(8,128)(2,1)S(1)}, bf16[128,384]{1,0:T(8,128)(2,1)S(1)}, u32[]{:S(2)}, u32[]{:S(2)}) collective-permute-start(bf16[128,384]{1,0:T(8,128)(2,1)S(1)} %get-tuple-element.27), channel_id=1, source_target_pairs={{0,256},{128,384},{256,0},{384,128},{1,257},{129,385},{257,1},{385... | collective-permute-start | bytes 294920 | tf_op jit(solution)/shard_map/ppermute | solution.py:24
  90.4 2.5 %collective-permute-start.6 = (bf16[128,384]{1,0:T(8,128)(2,1)S(1)}, bf16[128,384]{1,0:T(8,128)(2,1)S(1)}, u32[]{:S(2)}, u32[]{:S(2)}) collective-permute-start(bf16[128,384]{1,0:T(8,128)(2,1)S(1)} %get-tuple-element.28), channel_id=1, source_target_pairs={{0,128},{128,256},{256,384},{384,0},{1,129},{129,257},{257,385},{3... | collective-permute-start | bytes 294920 | tf_op jit(solution)/shard_map/ppermute | solution.py:24
  92.9 4.6 %collective-permute-start.7 = (bf16[128,384]{1,0:T(8,128)(2,1)S(1)}, bf16[128,384]{1,0:T(8,128)(2,1)S(1)}, u32[]{:S(2)}, u32[]{:S(2)}) collective-permute-start(bf16[128,384]{1,0:T(8,128)(2,1)S(1)} %get-tuple-element.29), channel_id=1, source_target_pairs={{0,384},{128,0},{256,128},{384,256},{1,385},{129,1},{257,129},{385... | collective-permute-start | bytes 294920 | tf_op jit(solution)/shard_map/ppermute | solution.py:24
  98.2 1.5 %collective-permute-done.7.refs_3_ = bf16[128,384]{1,0:T(8,128)(2,1)S(1)} collective-permute-done((bf16[128,384]{1,0:T(8,128)(2,1)S(1)}, bf16[128,384]{1,0:T(8,128)(2,1)S(1)}, u32[]{:S(2)}, u32[]{:S(2)}) %collective-permute-start.7) | collective-permute-done | bytes 98336 | tf_op jit(solution)/shard_map/ppermute | solution.py:24
  100.5 12.0 %all-to-all-start.2 = ((bf16[16,8,1024]{2,1,0:T(8,128)(2,1)}), bf16[16,8,1024]{2,1,0:T(8,128)(2,1)S(1)}, u32[]{:S(2)}, u32[]{:S(2)}) async-start(bf16[16,8,1024]{2,1,0:T(8,128)(2,1)} %bitcast.12), calls=%async_computation.2 | async-start | bytes 524288 | tf_op jit(solution)/shard_map/all_to_all | solution.py:397
  112.7 6.3 %input_part.2.rest_0_ = bf16[224,4096]{1,0:T(8,128)(2,1)} custom-call(s32[2]{0:T(128)S(1)} %pad_add_fusion.2.where, bf16[224,1024]{1,0:T(8,128)(2,1)S(1)} %copy-done, bf16[8,256,1024]{2,1,0:T(8,128)(2,1)} %bitcast.19), custom_call_target="tpu_custom_call" | custom-call | flops 939524096 | bytes 5111808 | tf_op jit(solution)/shard_map/input_part/pallas_call | solution.py:339
  119.1 6.3 %input_part.3 = bf16[224,4096]{1,0:T(8,128)(2,1)} custom-call(s32[2]{0:T(128)S(1)} %pad_add_fusion.where, bf16[224,1024]{1,0:T(8,128)(2,1)S(1)} %copy-done, bf16[8,256,1024]{2,1,0:T(8,128)(2,1)} %bitcast.20, bf16[224,4096]{1,0:T(8,128)(2,1)} %input_part.2.rest_0_), custom_call_target="tpu_custom_call", output_to_operand_aliasing={{}: (3, {})} | custom-call | flops 939524096 | bytes 5111808 | tf_op jit(solution)/shard_map/input_part/pallas_call | solution.py:339
  125.4 3.7 %all-to-all-done.2 = bf16[16,8,1024]{2,1,0:T(8,128)(2,1)S(1)} async-done(((bf16[16,8,1024]{2,1,0:T(8,128)(2,1)}), bf16[16,8,1024]{2,1,0:T(8,128)(2,1)S(1)}, u32[]{:S(2)}, u32[]{:S(2)}) %all-to-all-start.2) | async-done | bytes 262176 | tf_op jit(solution)/shard_map/all_to_all | solution.py:397
  (22 shorter events, 3.3 us)
Async XLA Ops:
  7.2 105.6 %all-gather.5.cloned.1.call-start = ((), (), s32[]{:S(2)}) async-start(), calls=%async_computation.4 | async-start | bytes 4718592 | tf_op jit(solution)/shard_map/all_gather | solution.py:375
  9.7 6.6 %collective-permute-start = (bf16[224,4096]{1,0:T(8,128)(2,1)}, bf16[224,4096]{1,0:T(8,128)(2,1)S(1)}, u32[]{:S(2)}, u32[]{:S(2)}) collective-permute-start(bf16[224,4096]{1,0:T(8,128)(2,1)} %acts.1), channel_id=1, source_target_pairs={{0,1},{1,0},{2,3},{3,2},{4,5},{5,4},{6,7},{7,6},{8,9},{9,8},{10,11... | collective-permute-start | bytes 5505032 | tf_op jit(solution)/shard_map/ppermute | solution.py:24
  11.6 4.6 %collective-permute-start.1 = (bf16[224,1024]{1,0:T(8,128)(2,1)}, bf16[224,1024]{1,0:T(8,128)(2,1)S(1)}, u32[]{:S(2)}, u32[]{:S(2)}) collective-permute-start(bf16[224,1024]{1,0:T(8,128)(2,1)} %grads.3), channel_id=1, source_target_pairs={{0,1},{1,0},{2,3},{3,2},{4,5},{5,4},{6,7},{7,6},{8,9},{9,8},{10,11... | collective-permute-start | bytes 1376264 | tf_op jit(solution)/shard_map/ppermute | solution.py:24
  22.2 54.7 %all-to-all-start = ((bf16[4,8,64,640]{3,2,1,0:T(8,128)(2,1)}), bf16[4,8,64,640]{3,2,1,0:T(8,128)(2,1)S(1)}, u32[]{:S(2)}, u32[]{:S(2)}) async-start(bf16[4,8,64,640]{3,2,1,0:T(8,128)(2,1)} %get-tuple-element.21), calls=%async_computation | async-start | bytes 5242880 | tf_op jit(solution)/shard_map/all_to_all | solution.py:382
  26.5 92.6 %all-gather.3.cloned.1.call-start = ((), (), s32[]{:S(2)}) async-start(), calls=%async_computation.3 | async-start | bytes 4718592 | tf_op jit(solution)/shard_map/all_gather | solution.py:389
  26.5 32.1 %collective-permute-start.3 = (bf16[8,64,384]{2,1,0:T(8,128)(2,1)}, bf16[8,64,384]{2,1,0:T(8,128)(2,1)S(1)}, u32[]{:S(2)}, u32[]{:S(2)}) collective-permute-start(bf16[8,64,384]{2,1,0:T(8,128)(2,1)} %get-tuple-element.24), channel_id=1, source_target_pairs={{0,2},{2,4},{4,6},{6,0},{1,3},{3,5},{5,7},{7,1},{8,10},{10,12},{12... | collective-permute-start | bytes 1179656 | tf_op jit(solution)/shard_map/ppermute | solution.py:24
  33.5 25.1 %collective-permute-start.8 = (bf16[128,1024]{1,0:T(8,128)(2,1)}, bf16[128,1024]{1,0:T(8,128)(2,1)S(1)}, u32[]{:S(2)}, u32[]{:S(2)}) collective-permute-start(bf16[128,1024]{1,0:T(8,128)(2,1)} %get-tuple-element.31), channel_id=1, source_target_pairs={{0,8},{1,9},{2,10},{3,11},{4,12},{5,13},{6,14},{7,15},{16,24},{17,... | collective-permute-start | bytes 786440 | tf_op jit(solution)/shard_map/ppermute | solution.py:38
  44.4 32.4 %collective-permute-start.4 = (bf16[8,64,384]{2,1,0:T(8,128)(2,1)}, bf16[8,64,384]{2,1,0:T(8,128)(2,1)S(1)}, u32[]{:S(2)}, u32[]{:S(2)}) collective-permute-start(bf16[8,64,384]{2,1,0:T(8,128)(2,1)} %get-tuple-element.25), channel_id=1, source_target_pairs={{0,6},{2,0},{4,2},{6,4},{1,7},{3,1},{5,3},{7,5},{8,14},{10,8},{12,... | collective-permute-start | bytes 1179656 | tf_op jit(solution)/shard_map/ppermute | solution.py:24
  48.1 28.8 %collective-permute-start.2 = (bf16[8,64,384]{2,1,0:T(8,128)(2,1)}, bf16[8,64,384]{2,1,0:T(8,128)(2,1)}, u32[]{:S(2)}, u32[]{:S(2)}) collective-permute-start(bf16[8,64,384]{2,1,0:T(8,128)(2,1)} %get-tuple-element.23), channel_id=1, source_target_pairs={{0,4},{2,6},{4,0},{6,2},{1,5},{3,7},{5,1},{7,3},{8,12},{10,14},{12... | collective-permute-start | bytes 1179656 | tf_op jit(solution)/shard_map/ppermute | solution.py:24
  58.6 17.4 %collective-permute-start.9 = (bf16[128,1024]{1,0:T(8,128)(2,1)S(1)}, bf16[128,1024]{1,0:T(8,128)(2,1)S(1)}, u32[]{:S(2)}, u32[]{:S(2)}) collective-permute-start(bf16[128,1024]{1,0:T(8,128)(2,1)S(1)} %collective-permute-done.8), channel_id=1, source_target_pairs={{0,16},{1,17},{2,18},{3,19},{4,20},{5,21},{6,22},{7,23},{16,0},{17... | collective-permute-start | bytes 786440 | tf_op jit(solution)/shard_map/ppermute | solution.py:38
  78.3 21.4 %all-to-all-start.1 = ((bf16[4,128,640]{2,1,0:T(8,128)(2,1)}), bf16[4,128,640]{2,1,0:T(8,128)(2,1)S(1)}, u32[]{:S(2)}, u32[]{:S(2)}) async-start(bf16[4,128,640]{2,1,0:T(8,128)(2,1)} %bitcast.21), calls=%async_computation.1 | async-start | bytes 1310720 | tf_op jit(solution)/shard_map/all_to_all | solution.py:393
  85.3 12.2 %collective-permute-start.5 = (bf16[128,384]{1,0:T(8,128)(2,1)S(1)}, bf16[128,384]{1,0:T(8,128)(2,1)S(1)}, u32[]{:S(2)}, u32[]{:S(2)}) collective-permute-start(bf16[128,384]{1,0:T(8,128)(2,1)S(1)} %get-tuple-element.27), channel_id=1, source_target_pairs={{0,256},{128,384},{256,0},{384,128},{1,257},{129,385},{257,1},{385... | collective-permute-start | bytes 294920 | tf_op jit(solution)/shard_map/ppermute | solution.py:24
  90.4 7.7 %collective-permute-start.6 = (bf16[128,384]{1,0:T(8,128)(2,1)S(1)}, bf16[128,384]{1,0:T(8,128)(2,1)S(1)}, u32[]{:S(2)}, u32[]{:S(2)}) collective-permute-start(bf16[128,384]{1,0:T(8,128)(2,1)S(1)} %get-tuple-element.28), channel_id=1, source_target_pairs={{0,128},{128,256},{256,384},{384,0},{1,129},{129,257},{257,385},{3... | collective-permute-start | bytes 294920 | tf_op jit(solution)/shard_map/ppermute | solution.py:24
  92.9 6.8 %collective-permute-start.7 = (bf16[128,384]{1,0:T(8,128)(2,1)S(1)}, bf16[128,384]{1,0:T(8,128)(2,1)S(1)}, u32[]{:S(2)}, u32[]{:S(2)}) collective-permute-start(bf16[128,384]{1,0:T(8,128)(2,1)S(1)} %get-tuple-element.29), channel_id=1, source_target_pairs={{0,384},{128,0},{256,128},{384,256},{1,385},{129,1},{257,129},{385... | collective-permute-start | bytes 294920 | tf_op jit(solution)/shard_map/ppermute | solution.py:24
  99.7 13.0 %copy-start = (bf16[224,1024]{1,0:T(8,128)(2,1)S(1)}, bf16[224,1024]{1,0:T(8,128)(2,1)}, u32[]{:S(2)}) copy-start(bf16[224,1024]{1,0:T(8,128)(2,1)} %grads.3) | copy-start | bytes 1376260
  100.5 28.5 %all-to-all-start.2 = ((bf16[16,8,1024]{2,1,0:T(8,128)(2,1)}), bf16[16,8,1024]{2,1,0:T(8,128)(2,1)S(1)}, u32[]{:S(2)}, u32[]{:S(2)}) async-start(bf16[16,8,1024]{2,1,0:T(8,128)(2,1)} %bitcast.12), calls=%async_computation.2 | async-start | bytes 524288 | tf_op jit(solution)/shard_map/all_to_all | solution.py:397
Sparse Core Ops, SparseCore 0:
  10.2 56.1 all-gather.4
  77.0 40.0 all-gather.2

commit v12 on v10

--- a/solution.py
+++ b/solution.py
@@ -384,7 +384,7 @@
 
     swapped = chip_shift(fetched, lambda i, z: (i, z ^ 1))
     both = jnp.concatenate([fetched, swapped], axis=0)
-    both, *_ = lax.optimization_barrier((both, *right))
+    both, *_ = lax.optimization_barrier((both, right[1], right[3]))
     other_half = lax.all_gather(both, ("y", "c"), axis=0, tiled=True)
 
     right = right_sums([part.reshape(NX * chunk, columns - LEFT) for part in right])

time: 134 us -> 133 us (level)
  the two profiles are of different devices: /device:TPU:14 before, /device:TPU:24 now
where the time goes in v12:
time: 133 us; the launch traced here: 131 us
  starting transfers between devices  74.3 us (56%)
  Pallas kernels  24.4 us (18%)
  waiting for transfers between devices  15.6 us (12%)
  between operations  14.2 us (11%)
  other arithmetic  2.68 us (2%)
    ppermute x2, starting transfers between devices, chip_shift(): return lax.ppermute(value, AXES, pairs)  31.9 us
    ppermute x8, starting transfers between devices, shift(): lax.ppermute(value, axis, [(i, (i + step) % size) for i in range(size)])  21.9 us
    pallas_call x2, Pallas kernels, input_part(): pl.pallas_call(input_kernel, out_shape=jax.ShapeDtypeStruct((tokens, widt...  12.6 us
    all_to_all x1, starting transfers between devices, shards(): lax.all_to_all(rows, ('zh', 'zl'), split_axis=0, concat_axis=0, tiled=True)  11.4 us
    ppermute x8, waiting for transfers between devices, shift(): lax.ppermute(value, axis, [(i, (i + step) % size) for i in range(size)])  10.3 us
    pallas_call x1, Pallas kernels, partials(): pl.pallas_call(functools.partial(partial_kernel, factor), out_shape=[pltp...  5.96 us
    all_to_all x1, starting transfers between devices, shards(): left = lax.all_to_all(left, 'y', split_axis=0, concat_axis=0, tiled=True)  4.69 us
    all_to_all x1, starting transfers between devices, shards(): left = lax.all_to_all(left, 'x', split_axis=0, concat_axis=0, tiled=True)  4.3 us
  transfers between devices with their start and end apart: 15, of which 6 were waited for; matrix products, arithmetic and copies ran while one was open for 2% of the time, Pallas kernels for 17%

profile of v12, /device:TPU:24, one launch (start us, length us, event | category | flops | bytes accessed | tf_op | source)
XLA Modules:
  0.0 131.2 jit_solution(5866476414032072884)
XLA Ops:
  7.2 2.3 %weights.1 = (bf16[256,1024]{1,0:T(8,128)(2,1)}, bf16[128,1024]{1,0:T(8,128)(2,1)S(1)}) custom-call(s32[1]{0:T(128)} %bitcast.1.odd, bf16[256,1024]{1,0:T(8,128)(2,1)} %quant.1, f32[8,256]{1,0:T(8,128)} %bitcast.21), custom_call_target="tpu_custom_call" | custom-call | flops 262144 | bytes 1048576 | tf_op jit(solution)/shard_map/weights/pallas_call | solution.py:65
  9.6 1.9 %collective-permute-start = (bf16[224,4096]{1,0:T(8,128)(2,1)}, bf16[224,4096]{1,0:T(8,128)(2,1)S(1)}, u32[]{:S(2)}, u32[]{:S(2)}) collective-permute-start(bf16[224,4096]{1,0:T(8,128)(2,1)} %acts.1), channel_id=1, source_target_pairs={{0,1},{1,0},{2,3},{3,2},{4,5},{5,4},{6,7},{7,6},{8,9},{9,8},{10,11... | collective-permute-start | bytes 5505032 | tf_op jit(solution)/shard_map/ppermute | solution.py:24
  11.5 2.4 %collective-permute-start.1 = (bf16[224,1024]{1,0:T(8,128)(2,1)}, bf16[224,1024]{1,0:T(8,128)(2,1)S(1)}, u32[]{:S(2)}, u32[]{:S(2)}) collective-permute-start(bf16[224,1024]{1,0:T(8,128)(2,1)} %grads.3), channel_id=1, source_target_pairs={{0,1},{1,0},{2,3},{3,2},{4,5},{5,4},{6,7},{7,6},{8,9},{9,8},{10,11... | collective-permute-start | bytes 1376264 | tf_op jit(solution)/shard_map/ppermute | solution.py:24
  13.9 15.7 %collective-permute-start.8 = (bf16[128,1024]{1,0:T(8,128)(2,1)S(1)}, bf16[128,1024]{1,0:T(8,128)(2,1)}, u32[]{:S(2)}, u32[]{:S(2)}) collective-permute-start(bf16[128,1024]{1,0:T(8,128)(2,1)S(1)} %get-tuple-element.30), channel_id=1, source_target_pairs={{0,8},{1,9},{2,10},{3,11},{4,12},{5,13},{6,14},{7,15},{16,24},{17,... | collective-permute-start | bytes 786440 | tf_op jit(solution)/shard_map/ppermute | solution.py:38
  29.8 6.0 %partials.1 = (bf16[4,8,64,768]{3,2,1,0:T(8,128)(2,1)}, bf16[8,64,256]{2,1,0:T(8,128)(2,1)}, bf16[8,64,256]{2,1,0:T(8,128)(2,1)}, bf16[8,64,256]{2,1,0:T(8,128)(2,1)}, bf16[8,64,256]{2,1,0:T(8,128)(2,1)}) custom-call(s32[3]{0:T(128)S(1)} %pad_add_fusion.1.where, bf16[224,4096]{1,0:T(8,128)(2,1)} %acts.1, bf16[224,4096]{1,0:T(8,128)(2,1)S(1)} %collective-permute-done.acts_in, ...), custom_call_target="tpu_custom_call" | custom-call | flops 1879048192 | bytes 7864320 | tf_op jit(solution)/shard_map/partials/pallas_call | solution.py:156
  35.7 4.3 %all-to-all-start = ((bf16[4,8,64,768]{3,2,1,0:T(8,128)(2,1)}), bf16[4,8,64,768]{3,2,1,0:T(8,128)(2,1)S(1)}, u32[]{:S(2)}, u32[]{:S(2)}) async-start(bf16[4,8,64,768]{3,2,1,0:T(8,128)(2,1)} %get-tuple-element.20), calls=%async_computation | async-start | bytes 6291456 | tf_op jit(solution)/shard_map/all_to_all | solution.py:382
  40.0 16.2 %collective-permute-start.9 = (bf16[128,1024]{1,0:T(8,128)(2,1)}, bf16[128,1024]{1,0:T(8,128)(2,1)S(1)}, u32[]{:S(2)}, u32[]{:S(2)}) collective-permute-start(bf16[128,1024]{1,0:T(8,128)(2,1)} %collective-permute-done.8), channel_id=1, source_target_pairs={{0,16},{1,17},{2,18},{3,19},{4,20},{5,21},{6,22},{7,23},{16,0},{17... | collective-permute-start | bytes 786440 | tf_op jit(solution)/shard_map/ppermute | solution.py:38
  56.2 2.7 %collective-permute-start.4 = (bf16[8,64,256]{2,1,0:T(8,128)(2,1)}, bf16[8,64,256]{2,1,0:T(8,128)(2,1)S(1)}, u32[]{:S(2)}, u32[]{:S(2)}) collective-permute-start(bf16[8,64,256]{2,1,0:T(8,128)(2,1)} %get-tuple-element.24), channel_id=1, source_target_pairs={{0,6},{2,0},{4,2},{6,4},{1,7},{3,1},{5,3},{7,5},{8,14},{10,8},{12,... | collective-permute-start | bytes 786440 | tf_op jit(solution)/shard_map/ppermute | solution.py:24
  58.9 2.9 %collective-permute-start.2 = (bf16[8,64,256]{2,1,0:T(8,128)(2,1)}, bf16[8,64,256]{2,1,0:T(8,128)(2,1)}, u32[]{:S(2)}, u32[]{:S(2)}) collective-permute-start(bf16[8,64,256]{2,1,0:T(8,128)(2,1)} %get-tuple-element.22), channel_id=1, source_target_pairs={{0,4},{2,6},{4,0},{6,2},{1,5},{3,7},{5,1},{7,3},{8,12},{10,14},{12... | collective-permute-start | bytes 786440 | tf_op jit(solution)/shard_map/ppermute | solution.py:24
  62.2 1.8 %pad_maximum_fusion = bf16[256,1024]{1,0:T(8,128)(2,1)} fusion(bf16[128,1024]{1,0:T(8,128)(2,1)S(1)} %collective-permute-done.9, bf16[128,1024]{1,0:T(8,128)(2,1)} %collective-permute-done.8), kind=kLoop, calls=%fused_computation | loop fusion | flops 1048576 | bytes 1048576 | tf_op jit(solution)/shard_map/concatenate | solution.py:386
  64.0 8.4 %collective-permute-done.4 = bf16[8,64,256]{2,1,0:T(8,128)(2,1)S(1)} collective-permute-done((bf16[8,64,256]{2,1,0:T(8,128)(2,1)}, bf16[8,64,256]{2,1,0:T(8,128)(2,1)S(1)}, u32[]{:S(2)}, u32[]{:S(2)}) %collective-permute-start.4) | collective-permute-done | bytes 262176 | tf_op jit(solution)/shard_map/ppermute | solution.py:24
  72.4 1.9 %collective-permute-start.3 = (bf16[8,64,256]{2,1,0:T(8,128)(2,1)}, bf16[8,64,256]{2,1,0:T(8,128)(2,1)}, u32[]{:S(2)}, u32[]{:S(2)}) collective-permute-start(bf16[8,64,256]{2,1,0:T(8,128)(2,1)} %get-tuple-element.23), channel_id=1, source_target_pairs={{0,2},{2,4},{4,6},{6,0},{1,3},{3,5},{5,7},{7,1},{8,10},{10,12},{12... | collective-permute-start | bytes 786440 | tf_op jit(solution)/shard_map/ppermute | solution.py:24
  74.3 3.1 %all-to-all-done = bf16[4,8,64,768]{3,2,1,0:T(8,128)(2,1)S(1)} async-done(((bf16[4,8,64,768]{3,2,1,0:T(8,128)(2,1)}), bf16[4,8,64,768]{3,2,1,0:T(8,128)(2,1)S(1)}, u32[]{:S(2)}, u32[]{:S(2)}) %all-to-all-start) | async-done | bytes 3145760 | tf_op jit(solution)/shard_map/all_to_all | solution.py:382
  77.5 1.4 %left_sums.1 = bf16[512,768]{1,0:T(8,128)(2,1)} custom-call(bf16[4,512,768]{2,1,0:T(8,128)(2,1)S(1)} %bitcast.16), custom_call_target="tpu_custom_call" | custom-call | flops 16000000000 | bytes 3145728 | tf_op jit(solution)/shard_map/left_sums/pallas_call | solution.py:205
  78.9 4.7 %all-to-all-start.1 = ((bf16[4,128,768]{2,1,0:T(8,128)(2,1)}), bf16[4,128,768]{2,1,0:T(8,128)(2,1)S(1)}, u32[]{:S(2)}, u32[]{:S(2)}) async-start(bf16[4,128,768]{2,1,0:T(8,128)(2,1)} %bitcast.20), calls=%async_computation.1 | async-start | bytes 1572864 | tf_op jit(solution)/shard_map/all_to_all | solution.py:392
  83.5 1.3 right_sums.1
  84.8 3.1 %collective-permute-start.5 = (bf16[128,256]{1,0:T(8,128)(2,1)S(1)}, bf16[128,256]{1,0:T(8,128)(2,1)S(1)}, u32[]{:S(2)}, u32[]{:S(2)}) collective-permute-start(bf16[128,256]{1,0:T(8,128)(2,1)S(1)} %get-tuple-element.26), channel_id=1, source_target_pairs={{0,256},{128,384},{256,0},{384,128},{1,257},{129,385},{257,1},{385... | collective-permute-start | bytes 196616 | tf_op jit(solution)/shard_map/ppermute | solution.py:24
  87.9 2.8 %collective-permute-start.6 = (bf16[128,256]{1,0:T(8,128)(2,1)S(1)}, bf16[128,256]{1,0:T(8,128)(2,1)S(1)}, u32[]{:S(2)}, u32[]{:S(2)}) collective-permute-start(bf16[128,256]{1,0:T(8,128)(2,1)S(1)} %get-tuple-element.27), channel_id=1, source_target_pairs={{0,128},{128,256},{256,384},{384,0},{1,129},{129,257},{257,385},{3... | collective-permute-start | bytes 196616 | tf_op jit(solution)/shard_map/ppermute | solution.py:24
  90.7 4.3 %collective-permute-start.7 = (bf16[128,256]{1,0:T(8,128)(2,1)S(1)}, bf16[128,256]{1,0:T(8,128)(2,1)S(1)}, u32[]{:S(2)}, u32[]{:S(2)}) collective-permute-start(bf16[128,256]{1,0:T(8,128)(2,1)S(1)} %get-tuple-element.28), channel_id=1, source_target_pairs={{0,384},{128,0},{256,128},{384,256},{1,385},{129,1},{257,129},{385... | collective-permute-start | bytes 196616 | tf_op jit(solution)/shard_map/ppermute | solution.py:24
  95.3 1.6 %collective-permute-done.7.refs_3_ = bf16[128,256]{1,0:T(8,128)(2,1)S(1)} collective-permute-done((bf16[128,256]{1,0:T(8,128)(2,1)S(1)}, bf16[128,256]{1,0:T(8,128)(2,1)S(1)}, u32[]{:S(2)}, u32[]{:S(2)}) %collective-permute-start.7) | collective-permute-done | bytes 65568 | tf_op jit(solution)/shard_map/ppermute | solution.py:24
  97.7 11.4 %all-to-all-start.2 = ((bf16[16,8,1024]{2,1,0:T(8,128)(2,1)}), bf16[16,8,1024]{2,1,0:T(8,128)(2,1)S(1)}, u32[]{:S(2)}, u32[]{:S(2)}) async-start(bf16[16,8,1024]{2,1,0:T(8,128)(2,1)} %bitcast.12), calls=%async_computation.2 | async-start | bytes 524288 | tf_op jit(solution)/shard_map/all_to_all | solution.py:396
  109.3 6.3 %input_part.2.rest_0_ = bf16[224,4096]{1,0:T(8,128)(2,1)} custom-call(s32[2]{0:T(128)S(1)} %pad_add_fusion.2.where, bf16[224,1024]{1,0:T(8,128)(2,1)S(1)} %copy-done, bf16[8,256,1024]{2,1,0:T(8,128)(2,1)} %bitcast.18), custom_call_target="tpu_custom_call" | custom-call | flops 939524096 | bytes 5111808 | tf_op jit(solution)/shard_map/input_part/pallas_call | solution.py:339
  115.7 6.3 %input_part.3 = bf16[224,4096]{1,0:T(8,128)(2,1)} custom-call(s32[2]{0:T(128)S(1)} %pad_add_fusion.where, bf16[224,1024]{1,0:T(8,128)(2,1)S(1)} %copy-done, bf16[8,256,1024]{2,1,0:T(8,128)(2,1)} %bitcast.19, bf16[224,4096]{1,0:T(8,128)(2,1)} %input_part.2.rest_0_), custom_call_target="tpu_custom_call", output_to_operand_aliasing={{}: (3, {})} | custom-call | flops 939524096 | bytes 5111808 | tf_op jit(solution)/shard_map/input_part/pallas_call | solution.py:339
  122.0 1.7 %all-to-all-done.2 = bf16[16,8,1024]{2,1,0:T(8,128)(2,1)S(1)} async-done(((bf16[16,8,1024]{2,1,0:T(8,128)(2,1)}), bf16[16,8,1024]{2,1,0:T(8,128)(2,1)S(1)}, u32[]{:S(2)}, u32[]{:S(2)}) %all-to-all-start.2) | async-done | bytes 262176 | tf_op jit(solution)/shard_map/all_to_all | solution.py:396
  (22 shorter events, 2.6 us)
Async XLA Ops:
  7.2 102.2 %all-gather.5.cloned.1.call-start = ((), (), s32[]{:S(2)}) async-start(), calls=%async_computation.4 | async-start | bytes 4718592 | tf_op jit(solution)/shard_map/all_gather | solution.py:375
  9.6 20.2 %collective-permute-start = (bf16[224,4096]{1,0:T(8,128)(2,1)}, bf16[224,4096]{1,0:T(8,128)(2,1)S(1)}, u32[]{:S(2)}, u32[]{:S(2)}) collective-permute-start(bf16[224,4096]{1,0:T(8,128)(2,1)} %acts.1), channel_id=1, source_target_pairs={{0,1},{1,0},{2,3},{3,2},{4,5},{5,4},{6,7},{7,6},{8,9},{9,8},{10,11... | collective-permute-start | bytes 5505032 | tf_op jit(solution)/shard_map/ppermute | solution.py:24
  11.5 18.2 %collective-permute-start.1 = (bf16[224,1024]{1,0:T(8,128)(2,1)}, bf16[224,1024]{1,0:T(8,128)(2,1)S(1)}, u32[]{:S(2)}, u32[]{:S(2)}) collective-permute-start(bf16[224,1024]{1,0:T(8,128)(2,1)} %grads.3), channel_id=1, source_target_pairs={{0,1},{1,0},{2,3},{3,2},{4,5},{5,4},{6,7},{7,6},{8,9},{9,8},{10,11... | collective-permute-start | bytes 1376264 | tf_op jit(solution)/shard_map/ppermute | solution.py:24
  13.9 26.1 %collective-permute-start.8 = (bf16[128,1024]{1,0:T(8,128)(2,1)S(1)}, bf16[128,1024]{1,0:T(8,128)(2,1)}, u32[]{:S(2)}, u32[]{:S(2)}) collective-permute-start(bf16[128,1024]{1,0:T(8,128)(2,1)S(1)} %get-tuple-element.30), channel_id=1, source_target_pairs={{0,8},{1,9},{2,10},{3,11},{4,12},{5,13},{6,14},{7,15},{16,24},{17,... | collective-permute-start | bytes 786440 | tf_op jit(solution)/shard_map/ppermute | solution.py:38
  35.7 41.8 %all-to-all-start = ((bf16[4,8,64,768]{3,2,1,0:T(8,128)(2,1)}), bf16[4,8,64,768]{3,2,1,0:T(8,128)(2,1)S(1)}, u32[]{:S(2)}, u32[]{:S(2)}) async-start(bf16[4,8,64,768]{3,2,1,0:T(8,128)(2,1)} %get-tuple-element.20), calls=%async_computation | async-start | bytes 6291456 | tf_op jit(solution)/shard_map/all_to_all | solution.py:382
  40.0 75.6 %all-gather.3.cloned.1.call-start = ((), (), s32[]{:S(2)}) async-start(), calls=%async_computation.3 | async-start | bytes 4718592 | tf_op jit(solution)/shard_map/all_gather | solution.py:388
  40.0 22.2 %collective-permute-start.9 = (bf16[128,1024]{1,0:T(8,128)(2,1)}, bf16[128,1024]{1,0:T(8,128)(2,1)S(1)}, u32[]{:S(2)}, u32[]{:S(2)}) collective-permute-start(bf16[128,1024]{1,0:T(8,128)(2,1)} %collective-permute-done.8), channel_id=1, source_target_pairs={{0,16},{1,17},{2,18},{3,19},{4,20},{5,21},{6,22},{7,23},{16,0},{17... | collective-permute-start | bytes 786440 | tf_op jit(solution)/shard_map/ppermute | solution.py:38
  56.2 16.1 %collective-permute-start.4 = (bf16[8,64,256]{2,1,0:T(8,128)(2,1)}, bf16[8,64,256]{2,1,0:T(8,128)(2,1)S(1)}, u32[]{:S(2)}, u32[]{:S(2)}) collective-permute-start(bf16[8,64,256]{2,1,0:T(8,128)(2,1)} %get-tuple-element.24), channel_id=1, source_target_pairs={{0,6},{2,0},{4,2},{6,4},{1,7},{3,1},{5,3},{7,5},{8,14},{10,8},{12,... | collective-permute-start | bytes 786440 | tf_op jit(solution)/shard_map/ppermute | solution.py:24
  58.9 13.5 %collective-permute-start.2 = (bf16[8,64,256]{2,1,0:T(8,128)(2,1)}, bf16[8,64,256]{2,1,0:T(8,128)(2,1)}, u32[]{:S(2)}, u32[]{:S(2)}) collective-permute-start(bf16[8,64,256]{2,1,0:T(8,128)(2,1)} %get-tuple-element.22), channel_id=1, source_target_pairs={{0,4},{2,6},{4,0},{6,2},{1,5},{3,7},{5,1},{7,3},{8,12},{10,14},{12... | collective-permute-start | bytes 786440 | tf_op jit(solution)/shard_map/ppermute | solution.py:24
  72.4 11.1 %collective-permute-start.3 = (bf16[8,64,256]{2,1,0:T(8,128)(2,1)}, bf16[8,64,256]{2,1,0:T(8,128)(2,1)}, u32[]{:S(2)}, u32[]{:S(2)}) collective-permute-start(bf16[8,64,256]{2,1,0:T(8,128)(2,1)} %get-tuple-element.23), channel_id=1, source_target_pairs={{0,2},{2,4},{4,6},{6,0},{1,3},{3,5},{5,7},{7,1},{8,10},{10,12},{12... | collective-permute-start | bytes 786440 | tf_op jit(solution)/shard_map/ppermute | solution.py:24
  78.9 18.0 %all-to-all-start.1 = ((bf16[4,128,768]{2,1,0:T(8,128)(2,1)}), bf16[4,128,768]{2,1,0:T(8,128)(2,1)S(1)}, u32[]{:S(2)}, u32[]{:S(2)}) async-start(bf16[4,128,768]{2,1,0:T(8,128)(2,1)} %bitcast.20), calls=%async_computation.1 | async-start | bytes 1572864 | tf_op jit(solution)/shard_map/all_to_all | solution.py:392
  84.8 10.2 %collective-permute-start.5 = (bf16[128,256]{1,0:T(8,128)(2,1)S(1)}, bf16[128,256]{1,0:T(8,128)(2,1)S(1)}, u32[]{:S(2)}, u32[]{:S(2)}) collective-permute-start(bf16[128,256]{1,0:T(8,128)(2,1)S(1)} %get-tuple-element.26), channel_id=1, source_target_pairs={{0,256},{128,384},{256,0},{384,128},{1,257},{129,385},{257,1},{385... | collective-permute-start | bytes 196616 | tf_op jit(solution)/shard_map/ppermute | solution.py:24
  87.9 7.4 %collective-permute-start.6 = (bf16[128,256]{1,0:T(8,128)(2,1)S(1)}, bf16[128,256]{1,0:T(8,128)(2,1)S(1)}, u32[]{:S(2)}, u32[]{:S(2)}) collective-permute-start(bf16[128,256]{1,0:T(8,128)(2,1)S(1)} %get-tuple-element.27), channel_id=1, source_target_pairs={{0,128},{128,256},{256,384},{384,0},{1,129},{129,257},{257,385},{3... | collective-permute-start | bytes 196616 | tf_op jit(solution)/shard_map/ppermute | solution.py:24
  90.7 6.2 %collective-permute-start.7 = (bf16[128,256]{1,0:T(8,128)(2,1)S(1)}, bf16[128,256]{1,0:T(8,128)(2,1)S(1)}, u32[]{:S(2)}, u32[]{:S(2)}) collective-permute-start(bf16[128,256]{1,0:T(8,128)(2,1)S(1)} %get-tuple-element.28), channel_id=1, source_target_pairs={{0,384},{128,0},{256,128},{384,256},{1,385},{129,1},{257,129},{385... | collective-permute-start | bytes 196616 | tf_op jit(solution)/shard_map/ppermute | solution.py:24
  96.9 12.4 %copy-start = (bf16[224,1024]{1,0:T(8,128)(2,1)S(1)}, bf16[224,1024]{1,0:T(8,128)(2,1)}, u32[]{:S(2)}) copy-start(bf16[224,1024]{1,0:T(8,128)(2,1)} %grads.3) | copy-start | bytes 1376260
  97.7 26.0 %all-to-all-start.2 = ((bf16[16,8,1024]{2,1,0:T(8,128)(2,1)}), bf16[16,8,1024]{2,1,0:T(8,128)(2,1)S(1)}, u32[]{:S(2)}, u32[]{:S(2)}) async-start(bf16[16,8,1024]{2,1,0:T(8,128)(2,1)} %bitcast.12), calls=%async_computation.2 | async-start | bytes 524288 | tf_op jit(solution)/shard_map/all_to_all | solution.py:396
Sparse Core Ops, SparseCore 0:
  10.2 42.1 all-gather.4
  72.5 38.3 all-gather.2
